TPU v7x, 512 devices: a whole 4x4x16 slice. The times are simulated.
512 devices in a mesh: ctx: 16 (over y, x), exp: 32 (over z, core).
Axes of the slice: x: 4, y: 4, z: 16, core: 2. Of those that a mesh axis runs over, the one named last changes fastest.
Arguments:
- features: bfloat16 [2048, 65536], P('exp', 'ctx'), may hold values from -36 to 36
- write_vectors: bfloat16 [128, 65536], P(None, 'ctx'), may hold values from -0.5 to 0.5
- read_vectors: bfloat16 [128, 65536], P(None, 'ctx'), may hold values from -6 to 6
- log_decay: float32 [64, 65536], P('exp', 'ctx'), may hold values from -0.8 to 0, as said below
- doc_lengths: int32 [8], replicated, may hold values from 1 to 16384, 65536 in all
- expert_ids: int32 [65536, 2], P(('ctx', 'exp')), may hold values from 0 to 31, all different within a row; in each aligned block of 128 rows (0 to 127, 128 to 255, ...) at most 10 rows name the same one
- route_weights: float32 [65536, 2], P(('ctx', 'exp')), may hold values from 0.2 to 1
- norm_gain: float32 [2048], replicated, may hold values from 0.1 to 1.9
- expert_in: bfloat16 [32, 2048, 1536], P('exp', 'ctx'), may hold values from -0.125 to 0.125
- expert_out: bfloat16 [32, 2048, 768], P('exp', 'ctx'), may hold values from -0.21875 to 0.21875
- out_grad: bfloat16 [2048, 65536], P(None, ('ctx', 'exp')), may hold values from -6 to 6
Outputs:
- block_out: bfloat16 [2048, 65536], P(None, ('ctx', 'exp'))
- input_grad: bfloat16 [2048, 65536], P('exp', 'ctx')
Inputs may be any that keep to these rules, and one draw needn't show every extreme that they name: `expert_ids`: over the 128 rows of one device no expert is named more than 10 times; the ids of a row differ. `log_decay`: strictly negative.
All inputs are finite; a program needn't handle non-finite values.
Results may differ from a plain program's by a relative error of at most 0.017.
Values may be sent and summed in bfloat16 or wider, within the bound.
No kernel may reach another device: no remote copies, remote signals or barrier semaphores. Data moves between devices by JAX's collectives and lax.ppermute only.
A program may use at most 128 MiB of HBM per device.

v0:
```python
import jax
import jax.numpy as jnp
from jax import lax
from jax.sharding import PartitionSpec as P

precise = lax.Precision.HIGHEST


def passed_along(value, axis, by):
    size = lax.axis_size(axis)
    pairs = [(i, i + by) for i in range(size) if 0 <= i + by < size]
    return lax.ppermute(value, axis, pairs)


def block_weights(decay_block, flag_block):
    cumulative = jnp.cumsum(decay_block, axis=1)
    starts_upto = jnp.cumsum(flag_block)
    position = jnp.arange(flag_block.shape[0], dtype=jnp.int32)
    lower_mask = position[:, None] >= position[None, :]
    same_doc = lower_mask & (starts_upto[:, None] == starts_upto[None, :])
    log_gap = cumulative[:, :, None] - cumulative[:, None, :]
    pair_weight = jnp.where(same_doc[None], jnp.exp(jnp.where(same_doc[None], log_gap, 0.0)), 0.0)
    entering = jnp.where(starts_upto[None, :] == 0, jnp.exp(cumulative), 0.0)
    leaving = jnp.where(
        starts_upto[None, :] == starts_upto[-1], jnp.exp(cumulative[:, -1:] - cumulative), 0.0
    )
    through_all = jnp.where(starts_upto[-1] == 0, jnp.exp(cumulative[:, -1]), 0.0)
    return (pair_weight, entering, leaving, through_all)


def doc_flags(doc_lengths, offset, span_count):
    doc_ends = jnp.cumsum(doc_lengths)
    starts = doc_ends - doc_lengths
    position = offset + jnp.arange(span_count, dtype=jnp.int32)
    return jnp.sum((position[:, None] == starts[None, :]).astype(jnp.float32), axis=1)


def local_step(carry, parts):
    product_now, state_now = carry
    through_one, summary_one = parts
    return (
        (product_now * through_one, through_one[:, None, None] * state_now + summary_one),
        (product_now, state_now),
    )


def chain_forward(dev_through, dev_summary):
    n_ctx = lax.axis_size("ctx")
    empty_state = jnp.zeros_like(dev_summary)

    def relay_step(position, incoming):
        return passed_along(
            (dev_through[:, None, None] * incoming + dev_summary).astype(jnp.bfloat16), "ctx", 1
        ).astype(jnp.float32)

    return lax.fori_loop(0, n_ctx - 1, relay_step, empty_state)


def chain_backward(dev_through, dev_summary):
    n_ctx = lax.axis_size("ctx")
    empty_state = jnp.zeros_like(dev_summary)

    def relay_step(position, incoming):
        return passed_along(
            (dev_through[:, None, None] * incoming + dev_summary).astype(jnp.bfloat16), "ctx", -1
        ).astype(jnp.float32)

    return lax.fori_loop(0, n_ctx - 1, relay_step, empty_state)


def slot_tables(expert_ids, route_weights, experts, capacity):
    tok_count, top_count = expert_ids.shape
    flat_ids = expert_ids.reshape(-1)
    columns = jnp.arange(experts, dtype=jnp.int32)
    picked = (flat_ids[:, None] == columns[None, :]).astype(jnp.int32)
    earlier = jnp.cumsum(picked, axis=0) - picked
    slot_rank = jnp.sum(earlier * picked, axis=1)
    target = (flat_ids * capacity + slot_rank).reshape(tok_count, top_count)
    places = jnp.arange(experts * capacity, dtype=jnp.int32)
    matches = places[:, None, None] == target[None, :, :]
    select = jnp.any(matches, axis=2).astype(jnp.bfloat16)
    weighted = jnp.sum(jnp.where(matches, route_weights[None, :, :], 0.0), axis=2)
    return (select, weighted)


def per_device(
    features,
    write_vectors,
    read_vectors,
    log_decay,
    doc_lengths,
    expert_ids,
    route_weights,
    norm_gain,
    expert_in,
    expert_out,
    out_grad,
):
    n_exp = lax.axis_size("exp")
    width_dev, seq_local = features.shape
    heads_dev = log_decay.shape[0]
    head_size = width_dev // heads_dev
    state_size = write_vectors.shape[0]
    block_size = min(512, seq_local)
    num_blocks = seq_local // block_size
    contract_last = (((1,), (1,)), ((), ()))
    contract_first = (((0,), (0,)), ((), ()))
    flags = doc_flags(doc_lengths, lax.axis_index("ctx") * seq_local, seq_local)
    x_blocks = features.reshape(heads_dev, head_size, num_blocks, block_size).transpose(2, 0, 1, 3)
    write_blocks = write_vectors.reshape(state_size, num_blocks, block_size).transpose(1, 0, 2)
    read_blocks = read_vectors.reshape(state_size, num_blocks, block_size).transpose(1, 0, 2)
    decay_blocks = log_decay.reshape(heads_dev, num_blocks, block_size).transpose(1, 0, 2)
    flag_blocks = flags.reshape(num_blocks, block_size)

    def forward_block(parts):
        x_block, write_block, read_block, decay_block, flag_block = parts
        pair_weight, entering_now, leaving_now, through_now = block_weights(decay_block, flag_block)
        x_float = x_block.astype(jnp.float32)
        write_float = write_block.astype(jnp.float32)
        scores = jnp.dot(read_block.T, write_block, preferred_element_type=jnp.float32)
        inside_now = jnp.einsum(
            "hts,hps->hpt", pair_weight * scores[None], x_float, precision=precise
        )
        summary_now = jnp.einsum(
            "ns,hs,hps->hnp", write_float, leaving_now, x_float, precision=precise
        )
        return (inside_now, entering_now, leaving_now, through_now, summary_now)

    inside, entering, leaving, through, summary = lax.map(
        forward_block, (x_blocks, write_blocks, read_blocks, decay_blocks, flag_blocks)
    )
    initial = (
        jnp.ones((heads_dev,), jnp.float32),
        jnp.zeros((heads_dev, state_size, head_size), jnp.float32),
    )
    (dev_through, dev_summary), (product_before, state_before) = lax.scan(
        local_step, initial, (through, summary)
    )
    incoming = chain_forward(dev_through, dev_summary)
    start_states = state_before + product_before[:, :, None, None] * incoming[None]
    read_float_all = read_blocks.astype(jnp.float32)
    write_float_all = write_blocks.astype(jnp.float32)
    carried = (
        jnp.einsum("bnt,bhnp->bhpt", read_float_all, start_states, precision=precise)
        * entering[:, :, None, :]
    )
    y_heads = (
        (inside + carried).transpose(1, 2, 0, 3).reshape(width_dev, seq_local).astype(jnp.bfloat16)
    )
    y_tokens = lax.all_to_all(y_heads, "exp", split_axis=1, concat_axis=0, tiled=True)
    y_float = y_tokens.astype(jnp.float32)
    rscale = lax.rsqrt(jnp.mean(y_float * y_float, axis=0) + 1e-06)
    normed = (y_float * rscale[None, :] * norm_gain[:, None]).astype(jnp.bfloat16)
    tok_dev, top_count = expert_ids.shape
    capacity = max(2, (tok_dev * top_count * 5 + 4 * n_exp - 1) // (4 * n_exp))
    select, weighted = slot_tables(expert_ids, route_weights, n_exp, capacity)
    outgoing = lax.dot_general(
        select, normed, contract_last, preferred_element_type=jnp.float32
    ).astype(jnp.bfloat16)
    outgoing = outgoing.reshape(n_exp, capacity, -1)
    gathered_in, gathered_out = (
        lax.all_gather(expert_in, "ctx", axis=1, tiled=True),
        lax.all_gather(expert_out, "ctx", axis=1, tiled=True),
    )
    weight_in = gathered_in[0]
    weight_out = gathered_out[0]
    received = lax.all_to_all(outgoing, "exp", split_axis=0, concat_axis=0, tiled=True)
    sources, per_source, feature_count = received.shape
    rows_flat = received.reshape(sources * per_source, feature_count)
    projected = jnp.dot(rows_flat, weight_in, preferred_element_type=jnp.float32)
    hidden_count = projected.shape[1] // 2
    gate_part = projected[:, :hidden_count]
    up_part = projected[:, hidden_count:]
    hidden = (jax.nn.silu(gate_part) * up_part).astype(jnp.bfloat16)
    results = lax.dot_general(
        hidden, weight_out, contract_last, preferred_element_type=jnp.float32
    ).astype(jnp.bfloat16)
    sent_back = lax.all_to_all(
        results.reshape(sources, per_source, feature_count),
        "exp",
        split_axis=0,
        concat_axis=0,
        tiled=True,
    )
    gate_saved = gate_part.reshape(sources, per_source, hidden_count)
    up_saved = up_part.reshape(sources, per_source, hidden_count)
    slot_total = n_exp * capacity
    combined_float = sent_back.reshape(slot_total, -1).astype(jnp.float32)
    moe = lax.dot_general(combined_float, weighted, contract_first, precision=precise)
    block_out = (normed.astype(jnp.float32) + moe).astype(jnp.bfloat16)
    grad_float = out_grad.astype(jnp.float32)
    back_in = lax.dot_general(weighted, grad_float, contract_last, precision=precise).astype(
        jnp.bfloat16
    )
    arrived = lax.all_to_all(
        back_in.reshape(n_exp, capacity, -1), "exp", split_axis=0, concat_axis=0, tiled=True
    ).reshape(slot_total, -1)
    gate_flat = gate_saved.reshape(slot_total, -1)
    up_flat = up_saved.reshape(slot_total, -1)
    d_hidden = jnp.dot(arrived, weight_out, preferred_element_type=jnp.float32)
    sigmoid_gate = jax.nn.sigmoid(gate_flat)
    d_gate = (d_hidden * up_flat * sigmoid_gate * (1.0 + gate_flat * (1.0 - sigmoid_gate))).astype(
        jnp.bfloat16
    )
    d_up = (d_hidden * gate_flat * sigmoid_gate).astype(jnp.bfloat16)
    back_out = lax.dot_general(
        jnp.concatenate([d_gate, d_up], axis=1),
        weight_in,
        contract_last,
        preferred_element_type=jnp.float32,
    ).astype(jnp.bfloat16)
    returned = lax.all_to_all(
        back_out.reshape(n_exp, capacity, -1), "exp", split_axis=0, concat_axis=0, tiled=True
    ).reshape(slot_total, -1)
    d_normed = grad_float + lax.dot_general(
        returned, select, contract_first, preferred_element_type=jnp.float32
    )
    scaled_grad = norm_gain[:, None] * d_normed
    mean_term = jnp.mean(y_float * scaled_grad, axis=0)
    y_grad = (
        rscale[None, :] * scaled_grad - y_float * (rscale**3)[None, :] * mean_term[None, :]
    ).astype(jnp.bfloat16)
    grad_heads = lax.all_to_all(y_grad, "exp", split_axis=0, concat_axis=1, tiled=True)
    grad_blocks = grad_heads.reshape(heads_dev, head_size, num_blocks, block_size).transpose(
        2, 0, 1, 3
    )

    def backward_block(parts):
        grad_block, write_block, read_block, decay_block, flag_block = parts
        pair_weight, entering_now, leaving_now, through_now = block_weights(decay_block, flag_block)
        grad_block_float = grad_block.astype(jnp.float32)
        read_float = read_block.astype(jnp.float32)
        scores = jnp.dot(read_block.T, write_block, preferred_element_type=jnp.float32)
        inside_now = jnp.einsum(
            "hts,hpt->hps", pair_weight * scores[None], grad_block_float, precision=precise
        )
        summary_now = jnp.einsum(
            "nt,ht,hpt->hnp", read_float, entering_now, grad_block_float, precision=precise
        )
        return (inside_now, summary_now)

    inside_back, back_summary = lax.map(
        backward_block, (grad_blocks, write_blocks, read_blocks, decay_blocks, flag_blocks)
    )
    (through_again, dev_back), (product_after, adjoint_after) = lax.scan(
        local_step, initial, (through, back_summary), reverse=True
    )
    incoming_back = chain_backward(dev_through, dev_back)
    after_states = adjoint_after + product_after[:, :, None, None] * incoming_back[None]
    carried_back = (
        jnp.einsum("bns,bhnp->bhps", write_float_all, after_states, precision=precise)
        * leaving[:, :, None, :]
    )
    input_grad = (
        (inside_back + carried_back)
        .transpose(1, 2, 0, 3)
        .reshape(width_dev, seq_local)
        .astype(jnp.bfloat16)
    )
    return (block_out, input_grad)


def solution(mesh):
    placed = (
        P("exp", "ctx"),
        P(None, "ctx"),
        P(None, "ctx"),
        P("exp", "ctx"),
        P(),
        P(("ctx", "exp"), None),
        P(("ctx", "exp"), None),
        P(),
        P("exp", "ctx", None),
        P("exp", "ctx", None),
        P(None, ("ctx", "exp")),
    )
    return jax.shard_map(
        per_device,
        mesh=mesh,
        in_specs=placed,
        out_specs=(P(None, ("ctx", "exp")), P("exp", "ctx")),
        check_vma=False,
    )
```

profile of v0, /device:TPU:6, one launch (start us, length us, event | category | flops | bytes accessed | tf_op | source)
XLA Modules:
  0.0 1024.5 jit_solution(6979590649531132796)
XLA Ops:
  17.5 93.8 %while.90 = (s32[]{:T(128)}, f32[8,2,32,512]{3,2,1,0:T(8,128)}, f32[8,2,512]{2,1,0:T(2,128)}, f32[8,2,512]{2,1,0:T(2,128)}, f32[8,2]{1,0:T(8,128)S(1)}, /*index=...) while((s32[]{:T(128)}, f32[8,2,32,512]{3,2,1,0:T(8,128)}, ...), condition=%wide.region_7.8_spmd, body=%wide.region_2.7_spmd.sunk | while | flops 321920064 | bytes 3423299 | solution.py:129
  21.3 3.3 fusion.183
  33.0 3.4 fusion.183
  44.7 3.3 fusion.183
  56.4 3.4 fusion.183
  79.9 3.4 fusion.183
  91.6 3.3 fusion.183
  103.3 3.4 fusion.183
  112.4 13.5 %while.92 = (s32[]{:T(128)}, f32[2]{0:T(128)S(1)}, f32[2,128,32]{2,1,0:T(8,128)S(1)}, f32[8,2]{1,0:T(8,128)S(1)}, f32[8,2,128,32]{3,2,1,0:T(8,128)}, /*index=5*/...) while((s32[]{:T(128)}, f32[2]{0:T(128)S(1)}, f32[2,128,32]{2,1,0:T(8,128)S(1)}, ...), condition=%wide.region_9.10_spmd.clone, body=%wide.region_8.9_spmd.clone.sunk | while | flops 32775 | bytes 393909 | solution.py:136
  126.4 123.6 %while.93 = (s32[]{:T(128)}, f32[2,128,32]{2,1,0:T(8,128)S(1)}, f32[2]{0:T(128)S(1)}, f32[2,128,32]{2,1,0:T(8,128)S(1)}, s32[]{:T(128)}, /*index=5*/s32[]{:T(128)}) while((s32[]{:T(128)}, f32[2,128,32]{2,1,0:T(8,128)S(1)}, f32[2]{0:T(128)S(1)}, f32[2,128,32]{2,1,0:T(8,128)S(1)}, s32[]{:T(128)}, /*index=5*/s32[]{:T(128)}) %tuple.165), condition=%wide.region_11.12_spmd.clone, body=%wide.region_10.11_spmd.clone.sunk | while | flops 40963 | bytes 196735 | solution.py:56
  126.5 3.4 collective-permute-start
  132.8 5.5 collective-permute-start
  140.3 6.4 collective-permute-start
  148.7 6.4 collective-permute-start
  157.1 6.4 collective-permute-start
  165.5 6.4 collective-permute-start
  174.2 6.5 collective-permute-start
  182.7 6.4 collective-permute-start
  191.1 6.4 collective-permute-start
  199.5 6.4 collective-permute-start
  207.9 6.4 collective-permute-start
  216.3 6.4 collective-permute-start
  224.6 6.5 collective-permute-start
  233.2 6.5 collective-permute-start
  241.7 6.4 collective-permute-start
  250.0 3.5 fusion.106
  255.2 15.5 %all-to-all-start = ((bf16[64,32,128]{2,0,1:T(8,128)(2,1)}), bf16[64,32,128]{2,0,1:T(8,128)(2,1)S(1)}, u32[]{:S(2)}, u32[]{:S(2)}) async-start(bf16[64,32,128]{2,0,1:T(8,128)(2,1)} %copy.114), calls=%async_computation | async-start | bytes 1048576 | tf_op jit(solution)/shard_map/all_to_all | solution.py:150
  276.2 3.4 reshape.542
  279.6 24.8 %all-to-all-done = bf16[64,32,128]{2,0,1:T(8,128)(2,1)S(1)} async-done(((bf16[64,32,128]{2,0,1:T(8,128)(2,1)}), bf16[64,32,128]{2,0,1:T(8,128)(2,1)S(1)}, u32[]{:S(2)}, u32[]{:S(2)}) %all-to-all-start) | async-done | bytes 524320 | tf_op jit(solution)/shard_map/all_to_all | solution.py:150
  304.4 4.8 all-to-all-start.3
  316.3 94.3 %all-to-all-done.3 = bf16[32,10,2048]{2,1,0:T(8,128)(2,1)} async-done(((bf16[32,10,2048]{2,1,0:T(8,128)(2,1)}), bf16[32,10,2048]{2,1,0:T(8,128)(2,1)}, u32[]{:S(2)}, u32[]{:S(2)}) %all-to-all-start.3) | async-done | bytes 1310752 | tf_op jit(solution)/shard_map/all_to_all | solution.py:195
  410.6 4.9 all-to-all-start.1
  415.5 3.6 reshape.543
  419.1 97.8 %all-to-all-done.1 = bf16[32,10,2048]{2,1,0:T(8,128)(2,1)} async-done(((bf16[32,10,2048]{2,1,0:T(8,128)(2,1)}), bf16[32,10,2048]{2,1,0:T(8,128)(2,1)}, u32[]{:S(2)}, u32[]{:S(2)}) %all-to-all-start.1) | async-done | bytes 1310752 | tf_op jit(solution)/shard_map/all_to_all | solution.py:167
  517.0 3.6 reshape.539
  520.6 6.6 fusion.87
  527.2 4.3 multiply_convert_fusion.1
  538.5 4.8 all-to-all-start.4
  543.3 4.8 fusion.96
  551.5 93.3 %all-to-all-done.4 = bf16[32,10,2048]{2,1,0:T(8,128)(2,1)} async-done(((bf16[32,10,2048]{2,1,0:T(8,128)(2,1)}), bf16[32,10,2048]{2,1,0:T(8,128)(2,1)}, u32[]{:S(2)}, u32[]{:S(2)}) %all-to-all-start.4) | async-done | bytes 1310752 | tf_op jit(solution)/shard_map/all_to_all | solution.py:212
  644.7 4.8 all-to-all-start.2
  649.5 3.6 reshape.545
  656.3 94.6 %all-to-all-done.2 = bf16[32,10,2048]{2,1,0:T(8,128)(2,1)} async-done(((bf16[32,10,2048]{2,1,0:T(8,128)(2,1)}), bf16[32,10,2048]{2,1,0:T(8,128)(2,1)}, u32[]{:S(2)}, u32[]{:S(2)}) %all-to-all-start.2) | async-done | bytes 1310752 | tf_op jit(solution)/shard_map/all_to_all | solution.py:178
  750.9 4.8 all-to-all-start.5
  758.3 3.8 fusion.100
  762.1 27.4 %all-to-all-done.5 = bf16[32,64,128]{2,1,0:T(8,128)(2,1)} async-done(((bf16[32,64,128]{2,1,0:T(8,128)(2,1)}), bf16[32,64,128]{2,1,0:T(8,128)(2,1)}, u32[]{:S(2)}, u32[]{:S(2)}) %all-to-all-start.5) | async-done | bytes 524320 | tf_op jit(solution)/shard_map/all_to_all | solution.py:223
  793.1 73.8 %while.91 = (s32[]{:T(128)}, f32[8,2,32,512]{3,2,1,0:T(8,128)S(1)}, f32[8,2,128,32]{2,3,1,0:T(8,128)}, bf16[8,2,32,512]{3,2,1,0:T(8,128)(2,1)}, f32[8,512]{1,0:T...) while((s32[]{:T(128)}, f32[8,2,32,512]{3,2,1,0:T(8,128)S(1)}, ...), condition=%wide.region_24.25_spmd, body=%wide.region_19.24_spmd.sunk | while | flops 321914432 | bytes 3392437 | solution.py:242
  868.0 18.4 %while.94 = (s32[]{:T(128)}, f32[2]{0:T(128)}, f32[2,128,32]{2,1,0:T(8,128)S(1)}, f32[8,2]{1,0:T(8,128)S(1)}, f32[8,2,128,32]{3,2,1,0:T(8,128)S(1)}, /*index=5*/...) while((s32[]{:T(128)}, f32[2]{0:T(128)}, ...), condition=%wide.region_26.27_spmd.clone, body=%wide.region_25.26_spmd.clone.sunk | while | flops 32776 | bytes 491725 | solution.py:245
  886.4 126.8 %while.95 = (s32[]{:T(128)}, f32[2,128,32]{2,1,0:T(8,128)S(1)}, f32[2]{0:T(128)S(1)}, f32[2,128,32]{2,1,0:T(8,128)S(1)}, s32[]{:T(128)}, /*index=5*/s32[]{:T(128)}) while((s32[]{:T(128)}, f32[2,128,32]{2,1,0:T(8,128)S(1)}, f32[2]{0:T(128)S(1)}, f32[2,128,32]{2,1,0:T(8,128)S(1)}, s32[]{:T(128)}, /*index=5*/s32[]{:T(128)}) %tuple.184), condition=%wide.region_28.29_spmd.clone, body=%wide.region_27.28_spmd.clone.sunk | while | flops 40963 | bytes 196735 | solution.py:68
  888.4 6.7 collective-permute-done.1
  897.1 6.3 collective-permute-done.1
  905.5 6.3 collective-permute-done.1
  913.9 6.3 collective-permute-done.1
  922.3 6.3 collective-permute-done.1
  930.7 6.6 collective-permute-done.1
  939.4 6.3 collective-permute-done.1
  947.7 6.3 collective-permute-done.1
  956.1 6.3 collective-permute-done.1
  964.5 6.3 collective-permute-done.1
  972.9 6.3 collective-permute-done.1
  981.3 6.3 collective-permute-done.1
  989.7 6.7 collective-permute-done.1
  998.4 6.3 collective-permute-done.1
  1006.8 6.3 collective-permute-done.1
  (652 shorter events, 282.7 us)
Async XLA Ops:
  7.2 513.4 %all-gather.3.cloned.1.call-start = ((), (), s32[]{:S(2)}) async-start(), calls=%async_computation.6 | async-start | bytes 6684672 | tf_op jit(solution)/shard_map/all_gather | solution.py:162
  10.1 3.0 copy-start.13
  111.3 1.1 copy-start.5
  125.8 0.6 copy-start.9
  126.5 6.2 collective-permute-start
  132.8 7.4 collective-permute-start
  140.3 8.3 collective-permute-start
  148.7 8.3 collective-permute-start
  157.1 8.3 collective-permute-start
  165.5 8.6 collective-permute-start
  174.2 8.4 collective-permute-start
  182.7 8.3 collective-permute-start
  191.1 8.3 collective-permute-start
  199.5 8.3 collective-permute-start
  207.9 8.3 collective-permute-start
  216.3 8.3 collective-permute-start
  224.6 8.4 collective-permute-start
  233.2 8.4 collective-permute-start
  241.7 8.3 collective-permute-start
  253.5 17.1 %copy-start.10 = (s32[128,2]{0,1:T(2,128)S(1)}, s32[128,2]{0,1:T(2,128)}, u32[]{:S(2)}) copy-start(s32[128,2]{0,1:T(2,128)} %param.28) | copy-start | bytes 3076
  253.5 18.7 %copy-start.11 = (f32[128,2]{0,1:T(2,128)S(1)}, f32[128,2]{0,1:T(2,128)}, u32[]{:S(2)}) copy-start(f32[128,2]{0,1:T(2,128)} %param.29) | copy-start | bytes 3076
  255.2 49.2 %all-to-all-start = ((bf16[64,32,128]{2,0,1:T(8,128)(2,1)}), bf16[64,32,128]{2,0,1:T(8,128)(2,1)S(1)}, u32[]{:S(2)}, u32[]{:S(2)}) async-start(bf16[64,32,128]{2,0,1:T(8,128)(2,1)} %copy.114), calls=%async_computation | async-start | bytes 1048576 | tf_op jit(solution)/shard_map/all_to_all | solution.py:150
  272.3 0.7 copy-start.4
  279.6 30.6 %copy-start.8 = (f32[2048]{0:T(1024)S(1)}, f32[2048]{0:T(1024)}, u32[]{:S(2)}) copy-start(f32[2048]{0:T(1024)} %param.30) | copy-start | bytes 24580
  304.4 106.2 %all-to-all-start.3 = ((bf16[32,10,2048]{2,1,0:T(8,128)(2,1)}), bf16[32,10,2048]{2,1,0:T(8,128)(2,1)}, u32[]{:S(2)}, u32[]{:S(2)}) async-start(bf16[32,10,2048]{2,1,0:T(8,128)(2,1)} %reshape.542), calls=%async_computation.3 | async-start | bytes 4194304 | tf_op jit(solution)/shard_map/all_to_all | solution.py:195
  309.2 218.0 %all-gather.5.cloned.1.call-start = ((), (), s32[]{:S(2)}) async-start(), calls=%async_computation.7 | async-start | bytes 3342336 | tf_op jit(solution)/shard_map/all_gather | solution.py:163
  310.6 0.8 copy-start
  410.6 106.4 %all-to-all-start.1 = ((bf16[32,10,2048]{2,1,0:T(8,128)(2,1)}), bf16[32,10,2048]{2,1,0:T(8,128)(2,1)}, u32[]{:S(2)}, u32[]{:S(2)}) async-start(bf16[32,10,2048]{2,1,0:T(8,128)(2,1)} %reshape.538), calls=%async_computation.1 | async-start | bytes 4194304 | tf_op jit(solution)/shard_map/all_to_all | solution.py:167
  527.2 4.7 copy-start.12
  538.5 106.2 %all-to-all-start.4 = ((bf16[32,10,2048]{2,1,0:T(8,128)(2,1)}), bf16[32,10,2048]{2,1,0:T(8,128)(2,1)}, u32[]{:S(2)}, u32[]{:S(2)}) async-start(bf16[32,10,2048]{2,1,0:T(8,128)(2,1)} %reshape.544), calls=%async_computation.4 | async-start | bytes 4194304 | tf_op jit(solution)/shard_map/all_to_all | solution.py:212
  644.7 106.2 %all-to-all-start.2 = ((bf16[32,10,2048]{2,1,0:T(8,128)(2,1)}), bf16[32,10,2048]{2,1,0:T(8,128)(2,1)}, u32[]{:S(2)}, u32[]{:S(2)}) async-start(bf16[32,10,2048]{2,1,0:T(8,128)(2,1)} %reshape.540), calls=%async_computation.2 | async-start | bytes 4194304 | tf_op jit(solution)/shard_map/all_to_all | solution.py:178
  649.5 3.7 copy-start.3
  750.9 38.6 %all-to-all-start.5 = ((bf16[32,64,128]{2,1,0:T(8,128)(2,1)}), bf16[32,64,128]{2,1,0:T(8,128)(2,1)}, u32[]{:S(2)}, u32[]{:S(2)}) async-start(bf16[32,64,128]{2,1,0:T(8,128)(2,1)} %bitcast.39), calls=%async_computation.5 | async-start | bytes 1048576 | tf_op jit(solution)/shard_map/all_to_all | solution.py:223
  798.1 2.4 copy-start.6
  807.3 2.4 copy-start.6
  816.5 2.4 copy-start.6
  825.8 2.4 copy-start.6
  835.0 2.4 copy-start.6
  844.2 2.4 copy-start.6
  853.5 2.4 copy-start.6
  862.7 2.4 copy-start.6
  866.9 1.0 copy-start.2
  868.0 18.4 %copy-start.1 = (f32[2,128,32]{2,1,0:T(8,128)S(1)}, f32[2,128,32]{2,1,0:T(8,128)}, u32[]{:S(2)}) copy-start(f32[2,128,32]{2,1,0:T(8,128)} %custom-call.5) | copy-start | bytes 98308
  886.4 126.8 %copy-start.7 = (f32[8,2,512]{2,1,0:T(2,128)S(1)}, f32[8,2,512]{2,1,0:T(2,128)}, u32[]{:S(2)}) copy-start(f32[8,2,512]{2,1,0:T(2,128)} %get-tuple-element.348) | copy-start | bytes 98308
  886.5 8.6 collective-permute-start.1
  895.2 8.3 collective-permute-start.1
  903.6 8.3 collective-permute-start.1
  912.0 8.3 collective-permute-start.1
  920.4 8.3 collective-permute-start.1
  928.8 8.5 collective-permute-start.1
  937.4 8.3 collective-permute-start.1
  945.8 8.3 collective-permute-start.1
  954.2 8.3 collective-permute-start.1
  962.6 8.3 collective-permute-start.1
  971.0 8.3 collective-permute-start.1
  979.4 8.3 collective-permute-start.1
  987.8 8.6 collective-permute-start.1
  996.5 8.3 collective-permute-start.1
  1004.9 8.3 collective-permute-start.1
Sparse Core Ops, SparseCore 0:
  11.0 81.0 all-gather.2
  313.0 63.9 all-gather.4
where the time goes:
time: 1030 us; the launch traced here: 1020 us
  waiting for transfers between devices  559 us (54%)
  starting transfers between devices  161 us (16%)
  matrix products  131 us (13%)
  local copies, waits for them, and re-layouts  91.2 us (9%)
  other arithmetic  61.8 us (6%)
  between operations  14.5 us (1%)
    ppermute x30, waiting for transfers between devices, passed_along(): return lax.ppermute(value, axis, pairs)  126 us
    ppermute x30, starting transfers between devices, passed_along(): return lax.ppermute(value, axis, pairs)  121 us
    all_to_all x1, waiting for transfers between devices, per_device(): lax.all_to_all(outgoing, 'exp', split_axis=0, concat_axis=0, tiled=True)  97.8 us
    all_to_all x1, waiting for transfers between devices, per_device(): lax.all_to_all(results.reshape(sources, per_source, feature_count), 'exp'...  94.6 us
    all_to_all x1, waiting for transfers between devices, per_device(): lax.all_to_all(back_in.reshape(n_exp, capacity, -1), 'exp', split_axis=0,...  94.3 us
    all_to_all x1, waiting for transfers between devices, per_device(): lax.all_to_all(back_out.reshape(n_exp, capacity, -1), 'exp', split_axis=0...  93.3 us
    all_to_all x1, waiting for transfers between devices, per_device(): lax.all_to_all(y_grad, 'exp', split_axis=0, concat_axis=1, tiled=True)  27.4 us
    dot_general x8, matrix products, forward_block(): jnp.einsum('hts,hps->hpt', pair_weight * scores[None], x_float, precision...  26.8 us
  transfers between devices with their start and end apart: 38, of which 36 were waited for; matrix products, arithmetic and copies ran while one was open for 16% of the time, Pallas kernels for 0%

commit v1 on v0

v1 whole, which is shorter than its diff:
```python
import jax
import jax.numpy as jnp
from jax import lax
from jax.experimental import pallas as pl
from jax.experimental.pallas import tpu as pltpu
from jax.sharding import PartitionSpec as P

f32 = jnp.float32
bf16 = jnp.bfloat16
i32 = jnp.int32

LANES = 128
SEQ = 4096
CHUNKS = SEQ // LANES
PAIRS = CHUNKS // 2
HP = 64
HEAD = 32
EXPERTS = 32
CAP = 10
SLOTS = EXPERTS * CAP
BLOCK = CAP * PAIRS
ROWS = EXPERTS * BLOCK
WIDTH = 2048
FF = 768
FBLOCKS = WIDTH // LANES
REACH = 4
VMEM_SMALL = 32 * 1024 * 1024
VMEM_LARGE = 48 * 1024 * 1024

LAST = (((1,), (1,)), ((), ()))
FIRST = (((0,), (0,)), ((), ()))


def dot(a, b):
    return jnp.dot(a, b, preferred_element_type=f32)


def dot_last(a, b):
    return lax.dot_general(a, b, LAST, preferred_element_type=f32)


def dot_first(a, b):
    return lax.dot_general(a, b, FIRST, preferred_element_type=f32)


def split3(value):
    high = value.astype(bf16)
    rest = value - high.astype(f32)
    middle = rest.astype(bf16)
    low = (rest - middle.astype(f32)).astype(bf16)
    return high, middle, low


def rows_of(first, second):
    return jnp.concatenate(
        [jnp.broadcast_to(first, (HEAD, LANES)), jnp.broadcast_to(second, (HEAD, LANES))], axis=0
    )


def earlier_mask():
    row = lax.broadcasted_iota(i32, (LANES, LANES), 0)
    col = lax.broadcasted_iota(i32, (LANES, LANES), 1)
    return jnp.where(row < col, 1.0, 0.0).astype(bf16)


def rank_table(first_ids, second_ids, earlier):
    expert = lax.broadcasted_iota(i32, (EXPERTS, LANES), 0).astype(f32)
    picked = (expert == first_ids) | (expert == second_ids)
    rank = dot(jnp.where(picked, 1.0, 0.0).astype(bf16), earlier)
    return jnp.where(picked, rank, -1.0)


def slot_onehot(ranks):
    return jnp.concatenate(
        [jnp.where(ranks == float(c), 1.0, 0.0).astype(bf16) for c in range(CAP)], axis=0
    )


def round_rows(dst_ref, src_ref):
    def step(i, carry):
        at = pl.ds(pl.multiple_of(i * BLOCK, BLOCK), BLOCK)
        dst_ref[at, :] = src_ref[at, :].astype(dst_ref.dtype)
        return carry

    lax.fori_loop(0, ROWS // BLOCK, step, 0)


def call(kernel, outs, args, in_specs, scratch=(), vmem=VMEM_SMALL, flops=0, moved=0, name=None):
    vm = pl.BlockSpec(memory_space=pltpu.VMEM)
    return pl.pallas_call(
        kernel,
        out_shape=tuple(jax.ShapeDtypeStruct(shape, kind) for shape, kind in outs),
        in_specs=in_specs,
        out_specs=tuple(vm for _ in outs),
        scratch_shapes=list(scratch),
        compiler_params=pltpu.CompilerParams(vmem_limit_bytes=vmem),
        cost_estimate=pl.CostEstimate(flops=flops, bytes_accessed=moved, transcendentals=0),
        name=name,
    )(*args)


VM = pl.BlockSpec(memory_space=pltpu.VMEM)
SM = pl.BlockSpec(memory_space=pltpu.SMEM)
HBM = pl.BlockSpec(memory_space=pl.ANY)


def grad_rows_kernel(ids_ref, grad_ref, out_ref, wide_ref):
    ranks = rank_table(ids_ref[0:1, :], ids_ref[1:2, :], earlier_mask())
    select = slot_onehot(ranks)

    def step(fb, carry):
        at = pl.multiple_of(fb * LANES, LANES)
        rows = dot_last(select, grad_ref[pl.ds(at, LANES), :])
        for c in range(CAP):
            wide_ref[pl.ds(c * FBLOCKS + fb, EXPERTS, stride=BLOCK), :] = rows[
                c * EXPERTS : (c + 1) * EXPERTS
            ]
        return carry

    lax.fori_loop(0, FBLOCKS, step, 0)
    round_rows(out_ref, wide_ref)


def tables_kernel(docs_ref, base_ref, decay_ref, x_ref, write_ref, rt_ref, dt_ref, msg_ref):
    decay = decay_ref[...]
    row_i = lax.broadcasted_iota(i32, (LANES, LANES), 0)
    col_i = lax.broadcasted_iota(i32, (LANES, LANES), 1)
    upto = jnp.where(row_i <= col_i, 1.0, 0.0).astype(bf16)
    cum = sum(dot(part, upto) for part in split3(decay))
    rows = 2 * CHUNKS
    chunk_end = jnp.broadcast_to(cum[:, LANES - 1 : LANES], (rows, LANES))
    row_j = lax.broadcasted_iota(i32, (rows, rows), 0)
    col_j = lax.broadcasted_iota(i32, (rows, rows), 1)
    same_head = (row_j >= CHUNKS) == (col_j >= CHUNKS)
    before = jnp.where(same_head & (col_j < row_j), 1.0, 0.0).astype(bf16)
    after = jnp.where(same_head & (col_j > row_j), 1.0, 0.0).astype(bf16)
    parts = split3(chunk_end)
    prefix = sum(dot(before, part) for part in parts)
    suffix = sum(dot(after, part) for part in parts)
    chunk = lax.broadcasted_iota(i32, (rows, LANES), 0)
    chunk = jnp.where(chunk >= CHUNKS, chunk - CHUNKS, chunk)
    token = lax.broadcasted_iota(i32, (rows, LANES), 1)
    place = chunk * LANES + token
    base = base_ref[0]
    doc_start = jnp.full((rows, LANES), -(1 << 20), i32)
    last_start = jnp.int32(-(1 << 20))
    start = -base
    for j in range(docs_ref.shape[0]):
        doc_start = jnp.where(place >= start, jnp.maximum(doc_start, start), doc_start)
        last_start = jnp.where(start <= SEQ - 1, jnp.maximum(last_start, start), last_start)
        start = start + docs_ref[j]
    inner_start = jnp.maximum(doc_start - chunk * LANES, -1)
    inner_float = inner_start.astype(f32)
    inner_last = jnp.broadcast_to(inner_float[:, LANES - 1 : LANES], (rows, LANES))
    to_end = chunk_end - cum
    entering = jnp.where(inner_start < 0, jnp.exp(cum), 0.0)
    leaving = jnp.where(token.astype(f32) >= inner_last, jnp.exp(to_end), 0.0)
    dev_entering = jnp.where(doc_start < 0, jnp.exp(prefix + cum), 0.0)
    dev_leaving = jnp.where(place >= last_start, jnp.exp(to_end + suffix), 0.0)
    for r, value in enumerate(
        (
            cum[:CHUNKS],
            cum[CHUNKS:],
            entering[:CHUNKS],
            entering[CHUNKS:],
            leaving[:CHUNKS],
            leaving[CHUNKS:],
            inner_float[:CHUNKS],
            inner_float[CHUNKS:],
        )
    ):
        rt_ref[pl.ds(r, CHUNKS, stride=8), :] = value
    zero = jnp.zeros((CHUNKS, LANES), f32)
    for r, value in enumerate(
        (
            dev_entering[:CHUNKS],
            dev_entering[CHUNKS:],
            dev_leaving[:CHUNKS],
            dev_leaving[CHUNKS:],
            zero,
            zero,
            zero,
            zero,
        )
    ):
        dt_ref[pl.ds(r, CHUNKS, stride=8), :] = value

    def step(k, acc):
        lanes = pl.ds(pl.multiple_of(k * LANES, LANES), LANES)
        rows_k = dt_ref[pl.ds(pl.multiple_of(k * 8, 8), 8), :]
        scaled = x_ref[:, lanes].astype(f32) * rows_of(rows_k[2:3], rows_k[3:4])
        return acc + dot_last(scaled.astype(bf16), write_ref[:, lanes])

    acc = lax.fori_loop(0, CHUNKS, step, jnp.zeros((HP, LANES), f32), unroll=4)
    msg_ref[0:HP, :] = acc
    through = jnp.concatenate(
        [
            jnp.broadcast_to(dev_entering[CHUNKS - 1 : CHUNKS, LANES - 1 : LANES], (1, LANES)),
            jnp.broadcast_to(dev_entering[rows - 1 : rows, LANES - 1 : LANES], (1, LANES)),
            jnp.zeros((6, LANES), f32),
        ],
        axis=0,
    )
    msg_ref[HP : HP + 8, :] = through


def chained(refs):
    state = refs[-1][0:HP, :]
    for ref in refs[-2::-1]:
        state = ref[0:HP, :] + rows_of(ref[HP : HP + 1, :], ref[HP + 1 : HP + 2, :]) * state
    return state


def forward_kernel(
    expert_ref,
    m1_ref,
    m2_ref,
    m3_ref,
    m4_ref,
    rt_ref,
    x_ref,
    write_ref,
    read_ref,
    ids_ref,
    y_ref,
    pair_ref,
    msg_ref,
    rank_ref,
    weight_ref,
    first_ref,
    wide_ref,
):
    earlier = earlier_mask()
    mine = expert_ref[0].astype(f32)
    is_first = ids_ref[0] == mine
    is_second = ids_ref[1] == mine
    picked = is_first | is_second
    rank = dot(jnp.where(picked, 1.0, 0.0).astype(bf16), earlier)
    rank = jnp.where(picked, rank, -1.0)
    route = jnp.where(is_first, ids_ref[2], jnp.where(is_second, ids_ref[3], 0.0))
    first = jnp.where(is_first, 1.0, 0.0)
    for c in range(CAP):
        here = rank == float(c)
        route_c = jnp.sum(jnp.where(here, route, 0.0), axis=1, keepdims=True)
        first_c = jnp.sum(jnp.where(here, first, 0.0), axis=1, keepdims=True)
        for par in range(2):
            at = (par * CAP + c) * PAIRS
            part = slice(par * PAIRS, (par + 1) * PAIRS)
            weight_ref[at : at + PAIRS, :] = jnp.broadcast_to(route_c[part], (PAIRS, LANES))
            first_ref[at : at + PAIRS, :] = jnp.broadcast_to(first_c[part], (PAIRS, LANES))

    row_i = lax.broadcasted_iota(i32, (LANES, LANES), 0)
    col_i = lax.broadcasted_iota(i32, (LANES, LANES), 1)
    causal = row_i <= col_i
    row_f = row_i.astype(f32)

    def step(k, state):
        lanes = pl.ds(pl.multiple_of(k * LANES, LANES), LANES)
        rows = rt_ref[pl.ds(pl.multiple_of(k * 8, 8), 8), :]
        cols = rows.T
        x = x_ref[:, lanes]
        write = write_ref[:, lanes]
        read = read_ref[:, lanes]
        scores = dot_first(write, read)
        valid = causal & (row_f >= rows[6:7, :])
        inside = []
        for h in range(2):
            gap = rows[h : h + 1, :] - cols[:, h : h + 1]
            pair = jnp.where(valid, jnp.exp(gap) * scores, 0.0).astype(bf16)
            pair_ref[pl.ds(pl.multiple_of((2 * k + h) * LANES, LANES), LANES), :] = pair
            inside.append(dot(x[h * HEAD : (h + 1) * HEAD, :], pair))
        carried = dot(state.astype(bf16), read) * rows_of(rows[2:3], rows[3:4])
        y_ref[:, lanes] = (jnp.concatenate(inside, axis=0) + carried).astype(bf16)
        scaled = (x.astype(f32) * rows_of(rows[4:5], rows[5:6])).astype(bf16)
        through = rows_of(
            jnp.broadcast_to(rows[2:3, LANES - 1 : LANES], (1, LANES)),
            jnp.broadcast_to(rows[3:4, LANES - 1 : LANES], (1, LANES)),
        )
        return through * state + dot_last(scaled, write)

    lax.fori_loop(0, CHUNKS, step, chained((m1_ref, m2_ref, m3_ref, m4_ref)), unroll=4)

    zero = jnp.zeros((HP, LANES), bf16)

    def dispatch(jp, carry):
        tables = []
        for par in range(2):
            j = par * PAIRS + jp
            table = rank_table(
                ids_ref[0, pl.ds(j, 1), :], ids_ref[1, pl.ds(j, 1), :], earlier
            )
            at = pl.multiple_of(jp * 64 + par * EXPERTS, EXPERTS)
            rank_ref[pl.ds(at, EXPERTS), :] = table
            tables.append(table)
        select = slot_onehot(jnp.concatenate(tables, axis=1))
        even = y_ref[:, pl.ds(pl.multiple_of(jp * 2 * LANES, LANES), LANES)]
        odd = y_ref[:, pl.ds(pl.multiple_of(jp * 2 * LANES + LANES, LANES), LANES)]
        both = jnp.concatenate(
            [jnp.concatenate([even, zero], axis=1), jnp.concatenate([zero, odd], axis=1)], axis=0
        )
        rows = dot_last(select, both)
        for c in range(CAP):
            wide_ref[pl.ds(c * PAIRS + jp, EXPERTS, stride=BLOCK), :] = rows[
                c * EXPERTS : (c + 1) * EXPERTS
            ]
        return carry

    lax.fori_loop(0, PAIRS, dispatch, 0)
    round_rows(msg_ref, wide_ref)


def arrived_grad_kernel(
    rows_ref, weight_ref, out_hbm, grad_ref, dhid_ref, wide_ref, scaled_ref, out_ref, sem
):
    fetch = pltpu.make_async_copy(out_hbm, out_ref, sem)
    fetch.start()
    round_rows(wide_ref, rows_ref)

    def unpack(fb, carry):
        lanes = pl.ds(pl.multiple_of(fb * LANES, LANES), LANES)
        for par in range(2):
            for c in range(CAP):
                at = (par * CAP + c) * PAIRS
                rows = wide_ref[
                    pl.ds(par * BLOCK + c * FBLOCKS + fb, PAIRS, stride=2 * BLOCK), :
                ]
                grad_ref[at : at + PAIRS, lanes] = rows.astype(bf16)
                scaled_ref[at : at + PAIRS, lanes] = (
                    rows * weight_ref[at : at + PAIRS, :]
                ).astype(bf16)
        return carry

    lax.fori_loop(0, FBLOCKS, unpack, 0)
    fetch.wait()

    def matmul(i, carry):
        lanes = pl.ds(pl.multiple_of(i * 256, 256), 256)
        dhid_ref[:, lanes] = dot(scaled_ref[...], out_ref[:, lanes])
        return carry

    lax.fori_loop(0, FF // 256, matmul, 0)


def expert_kernel(
    rows_ref,
    gain_ref,
    first_ref,
    grad_ref,
    dhid_ref,
    in_hbm,
    msg_ref,
    normed_ref,
    hidden_ref,
    stats_ref,
    y_ref,
    dcat_ref,
    in_ref,
    sem,
):
    fetch = pltpu.make_async_copy(in_hbm, in_ref, sem)
    fetch.start()
    lane = lax.broadcasted_iota(i32, (BLOCK, LANES), 1)
    low = lane < 64

    def unpack(k, squares):
        lanes = pl.ds(pl.multiple_of(k * LANES, LANES), LANES)
        at = pl.multiple_of(k * 2 * BLOCK, BLOCK)
        a = rows_ref[pl.ds(at, BLOCK), :].astype(f32)
        b = rows_ref[pl.ds(at + BLOCK, BLOCK), :].astype(f32)
        even = jnp.where(low, a, pltpu.roll(b, 64, 1))
        odd = jnp.where(low, pltpu.roll(a, 64, 1), b)
        both = jnp.concatenate([even, odd], axis=0)
        y_ref[:, lanes] = both
        return squares + both * both

    squares = lax.fori_loop(0, FBLOCKS, unpack, jnp.zeros((SLOTS, LANES), f32))
    mean = jnp.sum(squares, axis=1, keepdims=True) * (1.0 / WIDTH)
    rscale = lax.rsqrt(mean + 1e-06)
    rscale_b = jnp.broadcast_to(rscale, (SLOTS, LANES))

    def scale(k, carry):
        lanes = pl.ds(pl.multiple_of(k * LANES, LANES), LANES)
        scaled = y_ref[:, lanes] * gain_ref[:, lanes]
        y_ref[:, lanes] = scaled
        normed_ref[:, lanes] = (scaled * rscale_b).astype(bf16)
        return carry

    lax.fori_loop(0, FBLOCKS, scale, 0)
    fetch.wait()

    def project(i, carry):
        lanes = pl.ds(pl.multiple_of(i * 256, 256), 256)
        lanes_up = pl.ds(pl.multiple_of(FF + i * 256, 256), 256)
        gate = dot(normed_ref[...], in_ref[:, lanes])
        up = dot(normed_ref[...], in_ref[:, lanes_up])
        sigmoid = 1.0 / (1.0 + jnp.exp(-gate))
        swish = gate * sigmoid
        hidden_ref[:, lanes] = (swish * up).astype(bf16)
        dhid = dhid_ref[:, lanes]
        dcat_ref[:, lanes] = (dhid * up * sigmoid * (1.0 + gate * (1.0 - sigmoid))).astype(bf16)
        dcat_ref[:, lanes_up] = (dhid * swish).astype(bf16)
        return carry

    lax.fori_loop(0, FF // 256, project, 0)
    first = first_ref[...]
    first2 = jnp.concatenate([first, first], axis=1)

    def back(i, acc):
        at = pl.multiple_of(i * 256, 256)
        lanes = pl.ds(at, 256)
        grad = dot_last(dcat_ref[...], in_ref[lanes, :]) + first2 * grad_ref[:, lanes].astype(f32)
        product = grad * y_ref[:, lanes]
        for half in range(2):
            part = grad[:, half * LANES : (half + 1) * LANES]
            even, odd = part[:BLOCK], part[BLOCK:]
            row = pl.multiple_of((2 * i + half) * 2 * BLOCK, BLOCK)
            msg_ref[pl.ds(row, BLOCK), :] = jnp.where(low, even, pltpu.roll(odd, 64, 1)).astype(
                bf16
            )
            msg_ref[pl.ds(row + BLOCK, BLOCK), :] = jnp.where(
                low, pltpu.roll(even, 64, 1), odd
            ).astype(bf16)
        return acc + product[:, :LANES] + product[:, LANES:]

    acc = lax.fori_loop(0, WIDTH // 256, back, jnp.zeros((SLOTS, LANES), f32))
    total = jnp.broadcast_to(jnp.sum(acc, axis=1, keepdims=True), (SLOTS, LANES))
    stat_lane = lax.broadcasted_iota(i32, (SLOTS, LANES), 1)
    stats_ref[...] = jnp.where(stat_lane == 0, rscale_b, total)


def expert_out_kernel(
    hidden_ref, normed_ref, weight_ref, first_ref, out_hbm, msg_ref, wide_ref, out_ref, sem
):
    fetch = pltpu.make_async_copy(out_hbm, out_ref, sem)
    fetch.start()
    weight = weight_ref[...]
    weight2 = jnp.concatenate([weight, weight], axis=1)
    first = first_ref[...]
    first2 = jnp.concatenate([first, first], axis=1)
    fetch.wait()

    def matmul(i, carry):
        lanes = pl.ds(pl.multiple_of(i * 256, 256), 256)
        result = dot_last(hidden_ref[...], out_ref[lanes, :])
        result = weight2 * result + first2 * normed_ref[:, lanes].astype(f32)
        for half in range(2):
            part = result[:, half * LANES : (half + 1) * LANES]
            fb = 2 * i + half
            for par in range(2):
                for c in range(CAP):
                    at = (par * CAP + c) * PAIRS
                    wide_ref[
                        pl.ds(par * BLOCK + c * FBLOCKS + fb, PAIRS, stride=2 * BLOCK), :
                    ] = part[at : at + PAIRS]
        return carry

    lax.fori_loop(0, WIDTH // 256, matmul, 0)
    round_rows(msg_ref, wide_ref)


def combine_kernel(ids_ref, rows_ref, out_ref, wide_ref):
    round_rows(wide_ref, rows_ref)
    select = slot_onehot(rank_table(ids_ref[0:1, :], ids_ref[1:2, :], earlier_mask()))

    def step(fb, carry):
        rows = jnp.concatenate(
            [
                wide_ref[pl.ds(c * FBLOCKS + fb, EXPERTS, stride=BLOCK), :].astype(bf16)
                for c in range(CAP)
            ],
            axis=0,
        )
        at = pl.multiple_of(fb * LANES, LANES)
        out_ref[pl.ds(at, LANES), :] = dot_first(rows, select).astype(bf16)
        return carry

    lax.fori_loop(0, FBLOCKS, step, 0)


def grad_kernel(
    rows_ref, rank_ref, stats_ref, y_ref, gain_ref, read_ref, dt_ref, out_ref, msg_ref, wide_ref
):
    round_rows(wide_ref, rows_ref)
    gain = gain_ref[...]

    def step(jp, acc):
        at = pl.multiple_of(jp * 64, 64)
        ranks = rank_ref[pl.ds(at, 64), :]
        select = slot_onehot(jnp.concatenate([ranks[:EXPERTS], ranks[EXPERTS:]], axis=1))
        rows = jnp.concatenate(
            [
                wide_ref[pl.ds(c * PAIRS + jp, EXPERTS, stride=BLOCK), :].astype(bf16)
                for c in range(CAP)
            ],
            axis=0,
        )
        d_both = dot_first(rows, select)
        stats = stats_ref[jp]
        stats_high = stats.astype(bf16)
        stats_low = (stats - stats_high.astype(f32)).astype(bf16)
        per_token = dot(stats_high, select) + dot(stats_low, select)
        for par in range(2):
            lanes = pl.ds(pl.multiple_of((2 * jp + par) * LANES, LANES), LANES)
            part = slice(par * LANES, (par + 1) * LANES)
            rscale = 0.5 * per_token[2 * par : 2 * par + 1, part]
            mean = per_token[2 * par + 1 : 2 * par + 2, part] * (1.0 / WIDTH)
            scaled = gain * d_both[par * HP : (par + 1) * HP, part]
            y = y_ref[:, lanes].astype(f32)
            grad = (rscale * scaled - y * (rscale * rscale * rscale * mean)).astype(bf16)
            out_ref[:, lanes] = grad
            rows_k = dt_ref[pl.ds(pl.multiple_of((2 * jp + par) * 8, 8), 8), :]
            weighted = (grad.astype(f32) * rows_of(rows_k[0:1], rows_k[1:2])).astype(bf16)
            acc = acc + dot_last(weighted, read_ref[:, lanes])
        return acc

    msg_ref[0:HP, :] = lax.fori_loop(0, PAIRS, step, jnp.zeros((HP, LANES), f32))
    last = dt_ref[(CHUNKS - 1) * 8 : CHUNKS * 8, :]
    msg_ref[HP : HP + 8, :] = jnp.broadcast_to(last[:, LANES - 1 : LANES], (8, LANES))


def backward_kernel(
    m1_ref, m2_ref, m3_ref, m4_ref, rt_ref, grad_ref, write_ref, read_ref, pair_ref, out_ref
):
    def step(i, state):
        k = CHUNKS - 1 - i
        lanes = pl.ds(pl.multiple_of(k * LANES, LANES), LANES)
        rows = rt_ref[pl.ds(pl.multiple_of(k * 8, 8), 8), :]
        grad = grad_ref[:, lanes]
        write = write_ref[:, lanes]
        read = read_ref[:, lanes]
        inside = []
        for h in range(2):
            pair = pair_ref[pl.ds(pl.multiple_of((2 * k + h) * LANES, LANES), LANES), :]
            inside.append(dot_last(grad[h * HEAD : (h + 1) * HEAD, :], pair))
        carried = dot(state.astype(bf16), write) * rows_of(rows[4:5], rows[5:6])
        out_ref[:, lanes] = (jnp.concatenate(inside, axis=0) + carried).astype(bf16)
        scaled = (grad.astype(f32) * rows_of(rows[2:3], rows[3:4])).astype(bf16)
        through = rows_of(
            jnp.broadcast_to(rows[2:3, LANES - 1 : LANES], (1, LANES)),
            jnp.broadcast_to(rows[3:4, LANES - 1 : LANES], (1, LANES)),
        )
        return through * state + dot_last(scaled, read)

    lax.fori_loop(0, CHUNKS, step, chained((m1_ref, m2_ref, m3_ref, m4_ref)), unroll=4)


def sent_along(value, by):
    size = lax.axis_size("ctx")
    pairs = [(i, i + by) for i in range(size) if 0 <= i + by < size]
    return lax.ppermute(value, "ctx", pairs)


def exchanged(rows):
    blocks = rows.reshape(EXPERTS, BLOCK, LANES)
    return lax.all_to_all(blocks, "exp", split_axis=0, concat_axis=0, tiled=True).reshape(
        ROWS, LANES
    )


def per_device(
    features,
    write_vectors,
    read_vectors,
    log_decay,
    doc_lengths,
    expert_ids,
    route_weights,
    norm_gain,
    expert_in,
    expert_out,
    out_grad,
):
    me_ctx = lax.axis_index("ctx")
    me_exp = lax.axis_index("exp")
    wide = pltpu.VMEM((ROWS, LANES), f32)
    ids_own = expert_ids.T.astype(f32)
    tokens_own = jnp.concatenate([ids_own, route_weights.T], axis=0)

    (grad_out_rows,) = call(
        grad_rows_kernel,
        [((ROWS, LANES), bf16)],
        (ids_own, out_grad),
        [VM, VM],
        [wide],
        flops=2 * SLOTS * LANES * WIDTH,
        moved=4 << 20,
        name="grad_rows",
    )
    grad_in_rows = exchanged(grad_out_rows)

    weight_in = lax.all_gather(expert_in, "ctx", axis=1, tiled=True)[0]
    weight_out = lax.all_gather(expert_out, "ctx", axis=1, tiled=True)[0]
    tokens = lax.all_gather(tokens_own, "exp", axis=0, tiled=False)
    tokens = tokens.reshape(PAIRS, 2, 4, LANES).transpose(2, 1, 0, 3).reshape(4, CHUNKS, LANES)

    rt, dt, message = call(
        tables_kernel,
        [((CHUNKS * 8, LANES), f32), ((CHUNKS * 8, LANES), f32), ((HP + 8, LANES), f32)],
        (
            doc_lengths,
            (me_ctx * SEQ).astype(i32).reshape(1),
            log_decay.reshape(2 * CHUNKS, LANES),
            features,
            write_vectors,
        ),
        [SM, SM, VM, VM, VM],
        flops=2 * HP * LANES * SEQ,
        moved=3 << 20,
        name="shard_state",
    )
    before = [sent_along(message, d) for d in range(1, REACH + 1)]
    y_heads, pairs, y_out_rows, ranks, slot_weight, slot_first = call(
        forward_kernel,
        [
            ((HP, SEQ), bf16),
            ((2 * CHUNKS * LANES, LANES), bf16),
            ((ROWS, LANES), bf16),
            ((2 * CHUNKS // 2 * EXPERTS, LANES), f32),
            ((SLOTS, LANES), f32),
            ((SLOTS, LANES), f32),
        ],
        (
            me_exp.astype(i32).reshape(1),
            *before,
            rt,
            features,
            write_vectors,
            read_vectors,
            tokens,
        ),
        [SM] + [VM] * 9,
        [wide],
        flops=8 * HP * LANES * SEQ,
        moved=9 << 20,
        name="mixer_forward",
    )
    y_in_rows = exchanged(y_out_rows)

    grad_slots, d_hidden = call(
        arrived_grad_kernel,
        [((SLOTS, WIDTH), bf16), ((SLOTS, FF), f32)],
        (grad_in_rows, slot_weight, weight_out),
        [VM, VM, HBM],
        [wide, pltpu.VMEM((SLOTS, WIDTH), bf16), pltpu.VMEM((WIDTH, FF), bf16), pltpu.SemaphoreType.DMA],
        vmem=VMEM_LARGE,
        flops=2 * SLOTS * FF * WIDTH,
        moved=8 << 20,
        name="hidden_grad",
    )
    back_out_rows, normed, hidden, stats = call(
        expert_kernel,
        [
            ((ROWS, LANES), bf16),
            ((SLOTS, WIDTH), bf16),
            ((SLOTS, FF), bf16),
            ((SLOTS, LANES), f32),
        ],
        (y_in_rows, norm_gain.reshape(1, WIDTH), slot_first, grad_slots, d_hidden, weight_in),
        [VM, VM, VM, VM, VM, HBM],
        [
            pltpu.VMEM((SLOTS, WIDTH), f32),
            pltpu.VMEM((SLOTS, 2 * FF), bf16),
            pltpu.VMEM((WIDTH, 2 * FF), bf16),
            pltpu.SemaphoreType.DMA,
        ],
        vmem=VMEM_LARGE,
        flops=8 * SLOTS * FF * WIDTH,
        moved=14 << 20,
        name="expert",
    )
    back_in_rows = exchanged(back_out_rows)
    all_stats = lax.all_gather(stats[:, :2].T, "exp", axis=0, tiled=False)
    all_stats = all_stats.reshape(EXPERTS, 2, 2, CAP, PAIRS).transpose(4, 2, 1, 3, 0)
    all_stats = jnp.pad(all_stats.reshape(PAIRS, 4, SLOTS), ((0, 0), (0, 4), (0, 0)))

    (result_rows,) = call(
        expert_out_kernel,
        [((ROWS, LANES), bf16)],
        (hidden, normed, slot_weight, slot_first, weight_out),
        [VM, VM, VM, VM, HBM],
        [wide, pltpu.VMEM((WIDTH, FF), bf16), pltpu.SemaphoreType.DMA],
        vmem=VMEM_LARGE,
        flops=2 * SLOTS * FF * WIDTH,
        moved=8 << 20,
        name="expert_out",
    )
    result_rows, back_in_rows = lax.optimization_barrier((result_rows, back_in_rows))
    returned_rows = exchanged(result_rows)

    gain_own = lax.dynamic_slice(norm_gain, (me_exp * HP,), (HP,))
    y_grad, back_message = call(
        grad_kernel,
        [((HP, SEQ), bf16), ((HP + 8, LANES), f32)],
        (
            back_in_rows,
            ranks,
            all_stats,
            y_heads,
            jnp.broadcast_to(gain_own[:, None], (HP, LANES)),
            read_vectors,
            dt,
        ),
        [VM] * 7,
        [wide],
        flops=8 * HP * LANES * SEQ,
        moved=6 << 20,
        name="mixer_grad",
    )
    after = [sent_along(back_message, -d) for d in range(1, REACH + 1)]
    (input_grad,) = call(
        backward_kernel,
        [((HP, SEQ), bf16)],
        (*after, rt, y_grad, write_vectors, read_vectors, pairs),
        [VM] * 9,
        flops=8 * HP * LANES * SEQ,
        moved=6 << 20,
        name="mixer_backward",
    )
    (block_out,) = call(
        combine_kernel,
        [((WIDTH, LANES), bf16)],
        (ids_own, returned_rows),
        [VM, VM],
        [wide],
        flops=2 * SLOTS * LANES * WIDTH,
        moved=4 << 20,
        name="combine",
    )
    return (block_out, input_grad)


def solution(mesh):
    placed = (
        P("exp", "ctx"),
        P(None, "ctx"),
        P(None, "ctx"),
        P("exp", "ctx"),
        P(),
        P(("ctx", "exp"), None),
        P(("ctx", "exp"), None),
        P(),
        P("exp", "ctx", None),
        P("exp", "ctx", None),
        P(None, ("ctx", "exp")),
    )
    return jax.shard_map(
        per_device,
        mesh=mesh,
        in_specs=placed,
        out_specs=(P(None, ("ctx", "exp")), P("exp", "ctx")),
        check_vma=False,
    )
```

time: 1030 us -> 450 us (0.44)
  waiting for transfers between devices: 559 us -> 124 us
  blocking collectives: 0 us -> 146 us
  matrix products: 131 us -> 0 us
  starting transfers between devices: 161 us -> 57.3 us
  Pallas kernels: 0 us -> 67.8 us
  other arithmetic: 61.8 us -> 0.69 us
  local copies, waits for them, and re-layouts: 91.2 us -> 38.1 us
    all_to_all x6 -> x4, waiting for transfers between devices: 432 us -> 116 us  [exchanged(): lax.all_to_all(blocks, 'exp', split_axis=0, concat_axis=0, tiled=True)]
    all_gather x0 -> x2, blocking collectives: none -> 146 us  [the longest x1 83.4 us: per_device(): all_stats = lax.all_gather(stats[:, :2].T, 'exp', axis=0, tiled=False)]
    dot_general x58 -> x0, matrix products: 131 us -> none  [the longest x8 26.8 us: forward_block(): jnp.einsum('hts,hps->hpt', pair_weight * scores[None], x_float, precision...]
    ppermute x30 -> x8, waiting for transfers between devices: 126 us -> 6.08 us  [sent_along(): return lax.ppermute(value, 'ctx', pairs)]
    ppermute x30 -> x8, starting transfers between devices: 121 us -> 23.3 us  [sent_along(): return lax.ppermute(value, 'ctx', pairs)]
    pallas_call x0 -> x9, Pallas kernels: none -> 67.8 us  [call(): pl.pallas_call(kernel, out_shape=tuple((jax.ShapeDtypeStruct(shape, kind)...]
    dynamic_slice x64 -> x1, local copies, waits for them, and re-layouts: 30.7 us -> 0.08 us  [per_device(): gain_own = lax.dynamic_slice(norm_gain, (me_exp * HP,), (HP,))]
    reshape x10 -> x4, local copies, waits for them, and re-layouts: 27.1 us -> 5.02 us  [the longest x2 3.73 us: per_device(): all_stats.reshape(PAIRS, 4, SLOTS)]
  transfers between devices with their start and end apart: 38 -> 14, of which waited for: 36 -> 5; matrix products, arithmetic and copies ran while one was open for 16% -> 2% of each run, Pallas kernels for 0% -> 11%
where the time goes in v1:
time: 450 us; the launch traced here: 448 us
  blocking collectives  146 us (32%)
  waiting for transfers between devices  124 us (28%)
  Pallas kernels  67.8 us (15%)
  starting transfers between devices  57.3 us (13%)
  local copies, waits for them, and re-layouts  38.1 us (8%)
  between operations  14.3 us (3%)
    all_to_all x4, waiting for transfers between devices, exchanged(): lax.all_to_all(blocks, 'exp', split_axis=0, concat_axis=0, tiled=True)  116 us
    all_gather x1, blocking collectives, per_device(): all_stats = lax.all_gather(stats[:, :2].T, 'exp', axis=0, tiled=False)  83.4 us
    pallas_call x9, Pallas kernels, call(): pl.pallas_call(kernel, out_shape=tuple((jax.ShapeDtypeStruct(shape, kind)...  67.8 us
    all_gather x1, blocking collectives, per_device(): tokens = lax.all_gather(tokens_own, 'exp', axis=0, tiled=False)  62.5 us
    all_to_all x4, starting transfers between devices, exchanged(): lax.all_to_all(blocks, 'exp', split_axis=0, concat_axis=0, tiled=True)  33.9 us
    unnamed x74, local copies, waits for them, and re-layouts  30.2 us
    ppermute x8, starting transfers between devices, sent_along(): return lax.ppermute(value, 'ctx', pairs)  23.3 us
  transfers between devices with their start and end apart: 14, of which 5 were waited for; matrix products, arithmetic and copies ran while one was open for 2% of the time, Pallas kernels for 11%

profile of v1, /device:TPU:6, one launch (start us, length us, event | category | flops | bytes accessed | tf_op | source)
XLA Modules:
  0.0 447.7 jit_solution(9032591348333326919)
XLA Ops:
  7.2 0.7 all-gather.7.cloned.1.call-update
  7.9 0.7 all-gather.9.cloned.1.call-update
  8.6 0.7 convert_bitcast_fusion.ids_ref
  9.3 1.0 copy-done.14
  10.4 5.7 %grad_rows.1 = bf16[5120,128]{1,0:T(8,128)(2,1)} custom-call(f32[2,128]{1,0:T(2,128)S(1)} %convert_bitcast_fusion.ids_ref, bf16[2048,128]{1,0:T(8,128)(2,1)S(1)} %copy-done.14), custom_call_target="tpu_custom_call" | custom-call | flops 167772160 | bytes 4194304 | tf_op jit(solution)/shard_map/grad_rows/pallas_call | solution.py:90
  16.1 15.6 %all-to-all-start.1 = ((bf16[32,160,128]{2,1,0:T(8,128)(2,1)}), bf16[32,160,128]{2,1,0:T(8,128)(2,1)S(1)}, u32[]{:S(2)}, u32[]{:S(2)}) async-start(bf16[32,160,128]{2,1,0:T(8,128)(2,1)} %bitcast.11), calls=%async_computation.1 | async-start | bytes 2621440 | tf_op jit(solution)/shard_map/all_to_all | solution.py:555
  32.4 1.1 copy-done.5
  33.5 0.8 copy-done.28
  34.3 3.2 shard_state.1
  38.1 3.4 collective-permute-start
  41.5 4.3 collective-permute-start.1
  45.8 2.8 collective-permute-start.2
  48.7 3.8 collective-permute-start.3
  52.5 62.5 %all-gather.2 = f32[32,4,128]{2,1,0:T(4,128)S(1)} all-gather(f32[1,4,128]{2,1,0:T(4,128)S(1)} %maximum_bitcast_fusion), channel_id=2, replica_groups=mesh['ctx'=16,'exp'=32] {'exp'}, dimensions={0}, use_global_device_ids=true | all-gather | bytes 67584 | tf_op jit(solution)/shard_map/all_gather | solution.py:593
  115.7 1.0 copy-done.6
  116.7 0.8 copy-done.21
  117.6 15.0 %mixer_forward.1 = (bf16[64,4096]{1,0:T(8,128)(2,1)S(1)}, bf16[8192,128]{1,0:T(8,128)(2,1)S(1)}, bf16[5120,128]{1,0:T(8,128)(2,1)S(1)}, f32[1024,128]{1,0:T(8,12...) custom-call(s32[1]{0:T(128)} %bitcast.1.expert_ref, f32[72,128]{1,0:T(8,128)} %collective-permute-done.m1_ref, ...), custom_call_target="tpu_custom_call" | custom-call | flops 268435456 | bytes 9437184 | tf_op jit(solution)/shard_map/mixer_forward/pallas_call | solution.py:90
  132.6 1.3 copy-done.3
  133.9 1.1 copy-done.7
  135.0 0.7 copy-done.11
  135.6 0.8 copy-done.15
  136.4 0.8 copy-done.17
  137.2 0.7 copy-done.22
  137.9 9.6 %all-to-all-start = ((bf16[32,160,128]{2,1,0:T(8,128)(2,1)}), bf16[32,160,128]{2,1,0:T(8,128)(2,1)}, u32[]{:S(2)}, u32[]{:S(2)}) async-start(bf16[32,160,128]{2,1,0:T(8,128)(2,1)} %bitcast.32), calls=%async_computation | async-start | bytes 2621440 | tf_op jit(solution)/shard_map/all_to_all | solution.py:555
  147.6 0.9 copy-done.12
  148.5 3.7 hidden_grad.1
  152.2 1.1 copy-done.30
  153.2 1.0 copy-done.31
  154.2 60.4 %all-to-all-done = bf16[32,160,128]{2,1,0:T(8,128)(2,1)} async-done(((bf16[32,160,128]{2,1,0:T(8,128)(2,1)}), bf16[32,160,128]{2,1,0:T(8,128)(2,1)}, u32[]{:S(2)}, u32[]{:S(2)}) %all-to-all-start) | async-done | bytes 1310752 | tf_op jit(solution)/shard_map/all_to_all | solution.py:555
  214.6 0.9 copy-done.23
  215.6 1.2 copy-done.32
  216.8 11.9 %expert.1 = (bf16[5120,128]{1,0:T(8,128)(2,1)S(1)}, bf16[320,2048]{1,0:T(8,128)(2,1)S(1)}, bf16[320,768]{1,0:T(8,128)(2,1)S(1)}, f32[320,128]{1,0:T(8,128)S(1)}) custom-call(bf16[5120,128]{1,0:T(8,128)(2,1)} %bitcast.9.rows_ref, f32[1,2048]{1,0:T(1,128)S(1)} %bitcast.35, f32[320,128]{1,0:T(8,128)S(1)} %copy-done.23, bf16[320,2048]{1,0:T(8,128)(2,1)} %copy-done.30, ...), custom_call_target="tpu_custom_call" | custom-call | flops 4026531840 | bytes 14680064 | tf_op jit(solution)/shard_map/expert/pallas_call | solution.py:90
  228.6 1.0 copy-done.8
  229.7 1.1 copy-done.9
  230.8 0.8 copy-done.19
  232.2 4.0 all-to-all-start.2
  236.2 1.3 copy-done.10
  237.5 0.9 copy-done.13
  238.4 1.0 copy-done.20
  239.4 0.9 copy-done.24
  240.4 6.8 %expert_out.1 = bf16[5120,128]{1,0:T(8,128)(2,1)S(1)} custom-call(bf16[320,768]{1,0:T(8,128)(2,1)S(1)} %copy-done.20, bf16[320,2048]{1,0:T(8,128)(2,1)S(1)} %copy-done.10, f32[320,128]{1,0:T(8,128)S(1)} %copy-done.13, f32[320,128]{1,0:T(8,128)S(1)} %copy-done.24, bf16[2048,768]{1,0:T(8,128)(2,1)} %bitcast.37), custom_call_target="tpu_custom_call" | custom-call | flops 1006632960 | bytes 8388608 | tf_op jit(solution)/shard_map/expert_out/pallas_call | solution.py:90
  247.2 1.1 copy-done.2
  248.3 55.7 %all-to-all-done.2 = bf16[32,160,128]{2,1,0:T(8,128)(2,1)S(1)} async-done(((bf16[32,160,128]{2,1,0:T(8,128)(2,1)}), bf16[32,160,128]{2,1,0:T(8,128)(2,1)S(1)}, u32[]{:S(2)}, u32[]{:S(2)}) %all-to-all-start.2) | async-done | bytes 1310752 | tf_op jit(solution)/shard_map/all_to_all | solution.py:555
  303.9 4.7 %all-to-all-start.3 = ((bf16[32,160,128]{2,1,0:T(8,128)(2,1)}), bf16[32,160,128]{2,1,0:T(8,128)(2,1)}, u32[]{:S(2)}, u32[]{:S(2)}) async-start(bf16[32,160,128]{2,1,0:T(8,128)(2,1)} %bitcast.30), calls=%async_computation.3 | async-start | bytes 2621440 | tf_op jit(solution)/shard_map/all_to_all | solution.py:555
  308.7 1.6 slice_bitcast_fusion
  310.3 1.0 copy.23
  311.3 83.4 %all-gather.3 = f32[32,2,320]{2,1,0:T(2,128)} all-gather(f32[1,2,320]{2,1,0:T(2,128)S(1)} %copy.23), channel_id=3, replica_groups=mesh['ctx'=16,'exp'=32] {'exp'}, dimensions={0}, use_global_device_ids=true | all-gather | bytes 84480 | tf_op jit(solution)/shard_map/all_gather | solution.py:672
  394.7 1.8 copy.24
  396.5 1.9 copy.27
  398.4 1.9 reshape.79
  400.2 0.9 pad.4.stats_ref
  401.2 1.0 copy-done.16
  402.3 1.0 copy-done.18
  403.3 0.9 copy-done.27
  404.2 8.2 %mixer_grad.1 = (bf16[64,4096]{1,0:T(8,128)(2,1)S(1)}, f32[72,128]{1,0:T(8,128)S(1)}) custom-call(bf16[5120,128]{1,0:T(8,128)(2,1)S(1)} %bitcast.29, f32[1024,128]{1,0:T(8,128)S(1)} %copy-done.18, f32[16,8,320]{2,1,0:T(8,128)S(1)} %pad.4.stats_ref, bf16[64,4096]{1,0:T(8,128)(2,1)S(1)} %copy-done.16, f32[64,128]{1,0:T(8,128)S(1)} %broadcast_in_dim.2.gain_ref, ...), custom_call_target="tpu_custom_call" | custom-call | flops 268435456 | bytes 6291456 | tf_op jit(solution)/shard_map/mixer_grad/pallas_call | solution.py:90
  412.5 2.8 collective-permute-start.4
  415.2 3.0 collective-permute-start.5
  418.3 1.9 collective-permute-start.6
  420.2 1.3 collective-permute-start.7
  421.5 2.0 collective-permute-done.5.m2_ref
  423.5 1.7 collective-permute-done.6.m3_ref
  425.2 2.4 collective-permute-done.7.m4_ref
  427.6 6.1 %mixer_backward.1 = bf16[64,4096]{1,0:T(8,128)(2,1)} custom-call(f32[72,128]{1,0:T(8,128)S(1)} %collective-permute-done.4.m1_ref, f32[72,128]{1,0:T(8,128)S(1)} %collective-permute-done.5.m2_ref, f32[72,128]{1,0:T(8,128)S(1)} %collective-permute-done.6.m3_ref, f32[72,128]{1,0:T(8,128)S(1)} %collective-permute-done.7.m4_ref, ...), custom_call_target="tpu_custom_call" | custom-call | flops 268435456 | bytes 6291456 | tf_op jit(solution)/shard_map/mixer_backward/pallas_call | solution.py:90
  433.7 7.1 %combine.1 = bf16[2048,128]{1,0:T(8,128)(2,1)} custom-call(f32[2,128]{1,0:T(2,128)S(1)} %convert_bitcast_fusion.ids_ref, bf16[5120,128]{1,0:T(8,128)(2,1)} %bitcast.18.rows_ref), custom_call_target="tpu_custom_call" | custom-call | flops 167772160 | bytes 4194304 | tf_op jit(solution)/shard_map/combine/pallas_call | solution.py:90
  (61 shorter events, 2.9 us)
Async XLA Ops:
  7.2 140.4 %all-gather.7.cloned.1.call-start = ((), (), s32[]{:S(2)}) async-start(), calls=%async_computation.4 | async-start | bytes 3342336 | tf_op jit(solution)/shard_map/all_gather | solution.py:592
  7.9 206.7 %all-gather.9.cloned.1.call-start = ((), (), s32[]{:S(2)}) async-start(), calls=%async_computation.5 | async-start | bytes 6684672 | tf_op jit(solution)/shard_map/all_gather | solution.py:591
  9.3 1.0 copy-start.14
  16.1 15.7 %copy-start.34 = (f32[2,4096]{1,0:T(2,128)S(1)}, f32[2,4096]{1,0:T(2,128)}, u32[]{:S(2)}) copy-start(f32[2,4096]{1,0:T(2,128)} %param.14) | copy-start | bytes 98308
  16.1 16.3 %copy-start.1 = (bf16[128,4096]{1,0:T(8,128)(2,1)S(1)}, bf16[128,4096]{1,0:T(8,128)(2,1)}, u32[]{:S(2)}) copy-start(bf16[128,4096]{1,0:T(8,128)(2,1)} %write_ref.5) | copy-start | bytes 3145732
  16.1 16.3 %copy-start.29 = (s32[8]{0:T(128)S(1)}, s32[8]{0:T(128)}, u32[]{:S(2)}) copy-start(s32[8]{0:T(128)} %docs_ref.1) | copy-start | bytes 100
  16.1 36.4 %copy-start.35 = (f32[128,2]{0,1:T(2,128)S(1)}, f32[128,2]{0,1:T(2,128)}, u32[]{:S(2)}) copy-start(f32[128,2]{0,1:T(2,128)} %param.17) | copy-start | bytes 3076
  16.1 121.8 %all-to-all-start.1 = ((bf16[32,160,128]{2,1,0:T(8,128)(2,1)}), bf16[32,160,128]{2,1,0:T(8,128)(2,1)S(1)}, u32[]{:S(2)}, u32[]{:S(2)}) async-start(bf16[32,160,128]{2,1,0:T(8,128)(2,1)} %bitcast.11), calls=%async_computation.1 | async-start | bytes 2621440 | tf_op jit(solution)/shard_map/all_to_all | solution.py:555
  31.8 83.9 %copy-start = (bf16[128,4096]{1,0:T(8,128)(2,1)S(1)}, bf16[128,4096]{1,0:T(8,128)(2,1)}, u32[]{:S(2)}) copy-start(bf16[128,4096]{1,0:T(8,128)(2,1)} %read_ref.5) | copy-start | bytes 3145732
  32.4 1.1 copy-start.5
  33.5 0.8 copy-start.28
  37.5 0.6 copy-start.26
  38.1 77.6 %collective-permute-start = (f32[72,128]{1,0:T(8,128)}, f32[72,128]{1,0:T(8,128)}, u32[]{:S(2)}, u32[]{:S(2)}) collective-permute-start(f32[72,128]{1,0:T(8,128)} %get-tuple-element.21), channel_id=1, source_target_pairs={{0,32},{32,64},{64,96},{96,128},{128,160},{160,192},{192,224},{224... | collective-permute-start | bytes 110600 | tf_op jit(solution)/shard_map/ppermute | solution.py:550
  41.5 74.2 %collective-permute-start.1 = (f32[72,128]{1,0:T(8,128)}, f32[72,128]{1,0:T(8,128)}, u32[]{:S(2)}, u32[]{:S(2)}) collective-permute-start(f32[72,128]{1,0:T(8,128)} %get-tuple-element.21), channel_id=1, source_target_pairs={{0,64},{32,96},{64,128},{96,160},{128,192},{160,224},{192,256},{22... | collective-permute-start | bytes 110600 | tf_op jit(solution)/shard_map/ppermute | solution.py:550
  45.8 69.8 %collective-permute-start.2 = (f32[72,128]{1,0:T(8,128)}, f32[72,128]{1,0:T(8,128)}, u32[]{:S(2)}, u32[]{:S(2)}) collective-permute-start(f32[72,128]{1,0:T(8,128)} %get-tuple-element.21), channel_id=1, source_target_pairs={{0,96},{32,128},{64,160},{96,192},{128,224},{160,256},{192,288},{2... | collective-permute-start | bytes 110600 | tf_op jit(solution)/shard_map/ppermute | solution.py:550
  48.7 67.0 %collective-permute-start.3 = (f32[72,128]{1,0:T(8,128)}, f32[72,128]{1,0:T(8,128)}, u32[]{:S(2)}, u32[]{:S(2)}) collective-permute-start(f32[72,128]{1,0:T(8,128)} %get-tuple-element.21), channel_id=1, source_target_pairs={{0,128},{32,160},{64,192},{96,224},{128,256},{160,288},{192,320},{... | collective-permute-start | bytes 110600 | tf_op jit(solution)/shard_map/ppermute | solution.py:550
  115.7 1.0 copy-start.6
  116.7 0.8 copy-start.21
  132.6 1.3 copy-start.3
  133.9 1.1 copy-start.7
  135.0 0.7 copy-start.11
  135.6 0.8 copy-start.15
  136.4 0.8 copy-start.17
  137.2 0.7 copy-start.22
  137.9 76.7 %all-to-all-start = ((bf16[32,160,128]{2,1,0:T(8,128)(2,1)}), bf16[32,160,128]{2,1,0:T(8,128)(2,1)}, u32[]{:S(2)}, u32[]{:S(2)}) async-start(bf16[32,160,128]{2,1,0:T(8,128)(2,1)} %bitcast.32), calls=%async_computation | async-start | bytes 2621440 | tf_op jit(solution)/shard_map/all_to_all | solution.py:555
  147.5 0.9 copy-start.12
  148.5 66.2 %copy-start.33 = (f32[2048]{0:T(1024)S(1)}, f32[2048]{0:T(1024)}, u32[]{:S(2)}) copy-start(f32[2048]{0:T(1024)} %param.18) | copy-start | bytes 24580
  152.2 1.1 copy-start.30
  153.2 1.0 copy-start.31
  214.6 0.9 copy-start.23
  215.6 1.2 copy-start.32
  228.6 1.1 copy-start.8
  229.7 1.1 copy-start.9
  230.8 0.8 copy-start.19
  231.6 0.7 copy-start.25
  232.2 71.7 %all-to-all-start.2 = ((bf16[32,160,128]{2,1,0:T(8,128)(2,1)}), bf16[32,160,128]{2,1,0:T(8,128)(2,1)S(1)}, u32[]{:S(2)}, u32[]{:S(2)}) async-start(bf16[32,160,128]{2,1,0:T(8,128)(2,1)} %bitcast.33), calls=%async_computation.2 | async-start | bytes 2621440 | tf_op jit(solution)/shard_map/all_to_all | solution.py:555
  236.2 1.3 copy-start.10
  237.5 0.9 copy-start.13
  238.4 1.0 copy-start.20
  239.4 0.9 copy-start.24
  247.2 1.1 copy-start.2
  303.9 129.8 %all-to-all-start.3 = ((bf16[32,160,128]{2,1,0:T(8,128)(2,1)}), bf16[32,160,128]{2,1,0:T(8,128)(2,1)}, u32[]{:S(2)}, u32[]{:S(2)}) async-start(bf16[32,160,128]{2,1,0:T(8,128)(2,1)} %bitcast.30), calls=%async_computation.3 | async-start | bytes 2621440 | tf_op jit(solution)/shard_map/all_to_all | solution.py:555
  401.2 1.0 copy-start.16
  402.3 1.0 copy-start.18
  403.3 0.9 copy-start.27
  404.2 23.4 %copy-start.4 = (bf16[8192,128]{1,0:T(8,128)(2,1)S(1)}, bf16[8192,128]{1,0:T(8,128)(2,1)}, u32[]{:S(2)}) copy-start(bf16[8192,128]{1,0:T(8,128)(2,1)} %copy-done.3) | copy-start | bytes 6291460
  412.5 9.0 %collective-permute-start.4 = (f32[72,128]{1,0:T(8,128)S(1)}, f32[72,128]{1,0:T(8,128)S(1)}, u32[]{:S(2)}, u32[]{:S(2)}) collective-permute-start(f32[72,128]{1,0:T(8,128)S(1)} %get-tuple-element.37), channel_id=1, source_target_pairs={{32,0},{64,32},{96,64},{128,96},{160,128},{192,160},{224,192},{256... | collective-permute-start | bytes 110600 | tf_op jit(solution)/shard_map/ppermute | solution.py:550
  415.2 8.3 %collective-permute-start.5 = (f32[72,128]{1,0:T(8,128)S(1)}, f32[72,128]{1,0:T(8,128)S(1)}, u32[]{:S(2)}, u32[]{:S(2)}) collective-permute-start(f32[72,128]{1,0:T(8,128)S(1)} %get-tuple-element.37), channel_id=1, source_target_pairs={{64,0},{96,32},{128,64},{160,96},{192,128},{224,160},{256,192},{28... | collective-permute-start | bytes 110600 | tf_op jit(solution)/shard_map/ppermute | solution.py:550
  418.3 6.9 %collective-permute-start.6 = (f32[72,128]{1,0:T(8,128)S(1)}, f32[72,128]{1,0:T(8,128)S(1)}, u32[]{:S(2)}, u32[]{:S(2)}) collective-permute-start(f32[72,128]{1,0:T(8,128)S(1)} %get-tuple-element.37), channel_id=1, source_target_pairs={{96,0},{128,32},{160,64},{192,96},{224,128},{256,160},{288,192},{3... | collective-permute-start | bytes 110600 | tf_op jit(solution)/shard_map/ppermute | solution.py:550
  420.2 7.4 %collective-permute-start.7 = (f32[72,128]{1,0:T(8,128)S(1)}, f32[72,128]{1,0:T(8,128)S(1)}, u32[]{:S(2)}, u32[]{:S(2)}) collective-permute-start(f32[72,128]{1,0:T(8,128)S(1)} %get-tuple-element.37), channel_id=1, source_target_pairs={{128,0},{160,32},{192,64},{224,96},{256,128},{288,160},{320,192},{... | collective-permute-start | bytes 110600 | tf_op jit(solution)/shard_map/ppermute | solution.py:550
Sparse Core Ops, SparseCore 0:
  11.0 66.9 all-gather.6
  81.0 76.6 all-gather.8

commit v2 on v1

--- a/solution.py
+++ b/solution.py
@@ -24,8 +24,7 @@
 FF = 768
 FBLOCKS = WIDTH // LANES
 REACH = 4
-VMEM_SMALL = 32 * 1024 * 1024
-VMEM_LARGE = 48 * 1024 * 1024
+VMEM = 60 * 1024 * 1024
 
 LAST = (((1,), (1,)), ((), ()))
 FIRST = (((0,), (0,)), ((), ()))
@@ -82,10 +81,10 @@
         dst_ref[at, :] = src_ref[at, :].astype(dst_ref.dtype)
         return carry
 
-    lax.fori_loop(0, ROWS // BLOCK, step, 0)
-
-
-def call(kernel, outs, args, in_specs, scratch=(), vmem=VMEM_SMALL, flops=0, moved=0, name=None):
+    lax.fori_loop(0, ROWS // BLOCK, step, 0, unroll=4)
+
+
+def call(kernel, outs, args, in_specs, scratch=(), flops=0, moved=0, name=None):
     vm = pl.BlockSpec(memory_space=pltpu.VMEM)
     return pl.pallas_call(
         kernel,
@@ -93,7 +92,7 @@
         in_specs=in_specs,
         out_specs=tuple(vm for _ in outs),
         scratch_shapes=list(scratch),
-        compiler_params=pltpu.CompilerParams(vmem_limit_bytes=vmem),
+        compiler_params=pltpu.CompilerParams(vmem_limit_bytes=VMEM),
         cost_estimate=pl.CostEstimate(flops=flops, bytes_accessed=moved, transcendentals=0),
         name=name,
     )(*args)
@@ -117,7 +116,7 @@
             ]
         return carry
 
-    lax.fori_loop(0, FBLOCKS, step, 0)
+    lax.fori_loop(0, FBLOCKS, step, 0, unroll=4)
     round_rows(out_ref, wide_ref)
 
 
@@ -222,13 +221,13 @@
     write_ref,
     read_ref,
     ids_ref,
-    y_ref,
     pair_ref,
     msg_ref,
     rank_ref,
     weight_ref,
     first_ref,
     wide_ref,
+    y_ref,
 ):
     earlier = earlier_mask()
     mine = expert_ref[0].astype(f32)
@@ -305,7 +304,7 @@
             ]
         return carry
 
-    lax.fori_loop(0, PAIRS, dispatch, 0)
+    lax.fori_loop(0, PAIRS, dispatch, 0, unroll=2)
     round_rows(msg_ref, wide_ref)
 
 
@@ -330,7 +329,7 @@
                 ).astype(bf16)
         return carry
 
-    lax.fori_loop(0, FBLOCKS, unpack, 0)
+    lax.fori_loop(0, FBLOCKS, unpack, 0, unroll=2)
     fetch.wait()
 
     def matmul(i, carry):
@@ -351,8 +350,8 @@
     msg_ref,
     normed_ref,
     hidden_ref,
-    stats_ref,
     y_ref,
+    scaled_ref,
     dcat_ref,
     in_ref,
     sem,
@@ -380,9 +379,7 @@
 
     def scale(k, carry):
         lanes = pl.ds(pl.multiple_of(k * LANES, LANES), LANES)
-        scaled = y_ref[:, lanes] * gain_ref[:, lanes]
-        y_ref[:, lanes] = scaled
-        normed_ref[:, lanes] = (scaled * rscale_b).astype(bf16)
+        normed_ref[:, lanes] = (y_ref[:, lanes] * rscale_b * gain_ref[:, lanes]).astype(bf16)
         return carry
 
     lax.fori_loop(0, FBLOCKS, scale, 0)
@@ -409,23 +406,27 @@
         at = pl.multiple_of(i * 256, 256)
         lanes = pl.ds(at, 256)
         grad = dot_last(dcat_ref[...], in_ref[lanes, :]) + first2 * grad_ref[:, lanes].astype(f32)
-        product = grad * y_ref[:, lanes]
-        for half in range(2):
-            part = grad[:, half * LANES : (half + 1) * LANES]
-            even, odd = part[:BLOCK], part[BLOCK:]
-            row = pl.multiple_of((2 * i + half) * 2 * BLOCK, BLOCK)
-            msg_ref[pl.ds(row, BLOCK), :] = jnp.where(low, even, pltpu.roll(odd, 64, 1)).astype(
-                bf16
-            )
-            msg_ref[pl.ds(row + BLOCK, BLOCK), :] = jnp.where(
-                low, pltpu.roll(even, 64, 1), odd
-            ).astype(bf16)
+        scaled = grad * gain_ref[:, lanes]
+        scaled_ref[:, lanes] = scaled
+        product = scaled * y_ref[:, lanes]
         return acc + product[:, :LANES] + product[:, LANES:]
 
     acc = lax.fori_loop(0, WIDTH // 256, back, jnp.zeros((SLOTS, LANES), f32))
-    total = jnp.broadcast_to(jnp.sum(acc, axis=1, keepdims=True), (SLOTS, LANES))
-    stat_lane = lax.broadcasted_iota(i32, (SLOTS, LANES), 1)
-    stats_ref[...] = jnp.where(stat_lane == 0, rscale_b, total)
+    mean_grad = jnp.sum(acc, axis=1, keepdims=True) * (1.0 / WIDTH)
+    pull = jnp.broadcast_to(rscale * rscale * rscale * mean_grad, (SLOTS, LANES))
+
+    def pack(k, carry):
+        lanes = pl.ds(pl.multiple_of(k * LANES, LANES), LANES)
+        part = rscale_b * scaled_ref[:, lanes] - pull * y_ref[:, lanes]
+        even, odd = part[:BLOCK], part[BLOCK:]
+        row = pl.multiple_of(k * 2 * BLOCK, BLOCK)
+        msg_ref[pl.ds(row, BLOCK), :] = jnp.where(low, even, pltpu.roll(odd, 64, 1)).astype(bf16)
+        msg_ref[pl.ds(row + BLOCK, BLOCK), :] = jnp.where(low, pltpu.roll(even, 64, 1), odd).astype(
+            bf16
+        )
+        return carry
+
+    lax.fori_loop(0, FBLOCKS, pack, 0)
 
 
 def expert_out_kernel(
@@ -474,14 +475,11 @@
         out_ref[pl.ds(at, LANES), :] = dot_first(rows, select).astype(bf16)
         return carry
 
-    lax.fori_loop(0, FBLOCKS, step, 0)
-
-
-def grad_kernel(
-    rows_ref, rank_ref, stats_ref, y_ref, gain_ref, read_ref, dt_ref, out_ref, msg_ref, wide_ref
-):
+    lax.fori_loop(0, FBLOCKS, step, 0, unroll=4)
+
+
+def grad_kernel(rows_ref, rank_ref, read_ref, dt_ref, out_ref, msg_ref, wide_ref):
     round_rows(wide_ref, rows_ref)
-    gain = gain_ref[...]
 
     def step(jp, acc):
         at = pl.multiple_of(jp * 64, 64)
@@ -494,26 +492,17 @@
             ],
             axis=0,
         )
-        d_both = dot_first(rows, select)
-        stats = stats_ref[jp]
-        stats_high = stats.astype(bf16)
-        stats_low = (stats - stats_high.astype(f32)).astype(bf16)
-        per_token = dot(stats_high, select) + dot(stats_low, select)
+        both = dot_first(rows, select)
         for par in range(2):
             lanes = pl.ds(pl.multiple_of((2 * jp + par) * LANES, LANES), LANES)
-            part = slice(par * LANES, (par + 1) * LANES)
-            rscale = 0.5 * per_token[2 * par : 2 * par + 1, part]
-            mean = per_token[2 * par + 1 : 2 * par + 2, part] * (1.0 / WIDTH)
-            scaled = gain * d_both[par * HP : (par + 1) * HP, part]
-            y = y_ref[:, lanes].astype(f32)
-            grad = (rscale * scaled - y * (rscale * rscale * rscale * mean)).astype(bf16)
+            grad = both[par * HP : (par + 1) * HP, par * LANES : (par + 1) * LANES].astype(bf16)
             out_ref[:, lanes] = grad
             rows_k = dt_ref[pl.ds(pl.multiple_of((2 * jp + par) * 8, 8), 8), :]
             weighted = (grad.astype(f32) * rows_of(rows_k[0:1], rows_k[1:2])).astype(bf16)
             acc = acc + dot_last(weighted, read_ref[:, lanes])
         return acc
 
-    msg_ref[0:HP, :] = lax.fori_loop(0, PAIRS, step, jnp.zeros((HP, LANES), f32))
+    msg_ref[0:HP, :] = lax.fori_loop(0, PAIRS, step, jnp.zeros((HP, LANES), f32), unroll=2)
     last = dt_ref[(CHUNKS - 1) * 8 : CHUNKS * 8, :]
     msg_ref[HP : HP + 8, :] = jnp.broadcast_to(last[:, LANES - 1 : LANES], (8, LANES))
 
@@ -575,6 +564,10 @@
     wide = pltpu.VMEM((ROWS, LANES), f32)
     ids_own = expert_ids.T.astype(f32)
     tokens_own = jnp.concatenate([ids_own, route_weights.T], axis=0)
+    tokens = lax.all_to_all(
+        jnp.broadcast_to(tokens_own[None], (EXPERTS, 4, LANES)), "exp", 0, 0, tiled=True
+    )
+    tokens = tokens.reshape(PAIRS, 2, 4, LANES).transpose(2, 1, 0, 3).reshape(4, CHUNKS, LANES)
 
     (grad_out_rows,) = call(
         grad_rows_kernel,
@@ -590,9 +583,6 @@
 
     weight_in = lax.all_gather(expert_in, "ctx", axis=1, tiled=True)[0]
     weight_out = lax.all_gather(expert_out, "ctx", axis=1, tiled=True)[0]
-    tokens = lax.all_gather(tokens_own, "exp", axis=0, tiled=False)
-    tokens = tokens.reshape(PAIRS, 2, 4, LANES).transpose(2, 1, 0, 3).reshape(4, CHUNKS, LANES)
-
     rt, dt, message = call(
         tables_kernel,
         [((CHUNKS * 8, LANES), f32), ((CHUNKS * 8, LANES), f32), ((HP + 8, LANES), f32)],
@@ -609,10 +599,9 @@
         name="shard_state",
     )
     before = [sent_along(message, d) for d in range(1, REACH + 1)]
-    y_heads, pairs, y_out_rows, ranks, slot_weight, slot_first = call(
+    pairs, y_out_rows, ranks, slot_weight, slot_first = call(
         forward_kernel,
         [
-            ((HP, SEQ), bf16),
             ((2 * CHUNKS * LANES, LANES), bf16),
             ((ROWS, LANES), bf16),
             ((2 * CHUNKS // 2 * EXPERTS, LANES), f32),
@@ -629,7 +618,7 @@
             tokens,
         ),
         [SM] + [VM] * 9,
-        [wide],
+        [wide, pltpu.VMEM((HP, SEQ), bf16)],
         flops=8 * HP * LANES * SEQ,
         moved=9 << 20,
         name="mixer_forward",
@@ -642,36 +631,31 @@
         (grad_in_rows, slot_weight, weight_out),
         [VM, VM, HBM],
         [wide, pltpu.VMEM((SLOTS, WIDTH), bf16), pltpu.VMEM((WIDTH, FF), bf16), pltpu.SemaphoreType.DMA],
-        vmem=VMEM_LARGE,
         flops=2 * SLOTS * FF * WIDTH,
         moved=8 << 20,
         name="hidden_grad",
     )
-    back_out_rows, normed, hidden, stats = call(
+    back_out_rows, normed, hidden = call(
         expert_kernel,
         [
             ((ROWS, LANES), bf16),
             ((SLOTS, WIDTH), bf16),
             ((SLOTS, FF), bf16),
-            ((SLOTS, LANES), f32),
         ],
         (y_in_rows, norm_gain.reshape(1, WIDTH), slot_first, grad_slots, d_hidden, weight_in),
         [VM, VM, VM, VM, VM, HBM],
         [
             pltpu.VMEM((SLOTS, WIDTH), f32),
+            pltpu.VMEM((SLOTS, WIDTH), f32),
             pltpu.VMEM((SLOTS, 2 * FF), bf16),
             pltpu.VMEM((WIDTH, 2 * FF), bf16),
             pltpu.SemaphoreType.DMA,
         ],
-        vmem=VMEM_LARGE,
         flops=8 * SLOTS * FF * WIDTH,
         moved=14 << 20,
         name="expert",
     )
     back_in_rows = exchanged(back_out_rows)
-    all_stats = lax.all_gather(stats[:, :2].T, "exp", axis=0, tiled=False)
-    all_stats = all_stats.reshape(EXPERTS, 2, 2, CAP, PAIRS).transpose(4, 2, 1, 3, 0)
-    all_stats = jnp.pad(all_stats.reshape(PAIRS, 4, SLOTS), ((0, 0), (0, 4), (0, 0)))
 
     (result_rows,) = call(
         expert_out_kernel,
@@ -679,28 +663,17 @@
         (hidden, normed, slot_weight, slot_first, weight_out),
         [VM, VM, VM, VM, HBM],
         [wide, pltpu.VMEM((WIDTH, FF), bf16), pltpu.SemaphoreType.DMA],
-        vmem=VMEM_LARGE,
         flops=2 * SLOTS * FF * WIDTH,
         moved=8 << 20,
         name="expert_out",
     )
-    result_rows, back_in_rows = lax.optimization_barrier((result_rows, back_in_rows))
     returned_rows = exchanged(result_rows)
 
-    gain_own = lax.dynamic_slice(norm_gain, (me_exp * HP,), (HP,))
     y_grad, back_message = call(
         grad_kernel,
         [((HP, SEQ), bf16), ((HP + 8, LANES), f32)],
-        (
-            back_in_rows,
-            ranks,
-            all_stats,
-            y_heads,
-            jnp.broadcast_to(gain_own[:, None], (HP, LANES)),
-            read_vectors,
-            dt,
-        ),
-        [VM] * 7,
+        (back_in_rows, ranks, read_vectors, dt),
+        [VM] * 4,
         [wide],
         flops=8 * HP * LANES * SEQ,
         moved=6 << 20,
@@ -716,6 +689,7 @@
         moved=6 << 20,
         name="mixer_backward",
     )
+    returned_rows, input_grad = lax.optimization_barrier((returned_rows, input_grad))
     (block_out,) = call(
         combine_kernel,
         [((WIDTH, LANES), bf16)],

time: 450 us -> 360 us (0.80)
  blocking collectives: 146 us -> 0 us
  waiting for transfers between devices: 124 us -> 205 us
  local copies, waits for them, and re-layouts: 38.1 us -> 7.51 us
  Pallas kernels: 67.8 us -> 76.7 us
    all_gather x2 -> x0, blocking collectives: 146 us -> none  [the longest x1 83.4 us: per_device(): all_stats = lax.all_gather(stats[:, :2].T, 'exp', axis=0, tiled=False)]
    all_to_all x4, waiting for transfers between devices: 116 us -> 186 us  [exchanged(): lax.all_to_all(blocks, 'exp', split_axis=0, concat_axis=0, tiled=True)]
    unnamed x74 -> x28, local copies, waits for them, and re-layouts: 30.2 us -> 5.58 us
    all_to_all x4, starting transfers between devices: 33.9 us -> 15.9 us  [exchanged(): lax.all_to_all(blocks, 'exp', split_axis=0, concat_axis=0, tiled=True)]
    all_to_all x0 -> x1, starting transfers between devices: none -> 15.5 us  [per_device(): lax.all_to_all(jnp.broadcast_to(tokens_own[None], (EXPERTS, 4, LANES)), '...]
    all_to_all x0 -> x1, waiting for transfers between devices: none -> 9.33 us  [per_device(): lax.all_to_all(jnp.broadcast_to(tokens_own[None], (EXPERTS, 4, LANES)), '...]
    pallas_call x9, Pallas kernels: 67.8 us -> 76.7 us  [call(): pl.pallas_call(kernel, out_shape=tuple((jax.ShapeDtypeStruct(shape, kind)...]
  transfers between devices with their start and end apart: 14 -> 15, of which waited for: 5 -> 9; matrix products, arithmetic and copies ran while one was open for 2% -> 1% of each run, Pallas kernels for 11% -> 16%
where the time goes in v2:
time: 360 us; the launch traced here: 359 us
  waiting for transfers between devices  205 us (57%)
  Pallas kernels  76.7 us (21%)
  starting transfers between devices  54.3 us (15%)
  between operations  14.3 us (4%)
  local copies, waits for them, and re-layouts  7.51 us (2%)
    all_to_all x4, waiting for transfers between devices, exchanged(): lax.all_to_all(blocks, 'exp', split_axis=0, concat_axis=0, tiled=True)  186 us
    pallas_call x9, Pallas kernels, call(): pl.pallas_call(kernel, out_shape=tuple((jax.ShapeDtypeStruct(shape, kind)...  76.7 us
    ppermute x8, starting transfers between devices, sent_along(): return lax.ppermute(value, 'ctx', pairs)  22.8 us
    all_to_all x4, starting transfers between devices, exchanged(): lax.all_to_all(blocks, 'exp', split_axis=0, concat_axis=0, tiled=True)  15.9 us
    all_to_all x1, starting transfers between devices, per_device(): lax.all_to_all(jnp.broadcast_to(tokens_own[None], (EXPERTS, 4, LANES)), '...  15.5 us
    all_to_all x1, waiting for transfers between devices, per_device(): lax.all_to_all(jnp.broadcast_to(tokens_own[None], (EXPERTS, 4, LANES)), '...  9.33 us
    ppermute x8, waiting for transfers between devices, sent_along(): return lax.ppermute(value, 'ctx', pairs)  8.35 us
  transfers between devices with their start and end apart: 15, of which 9 were waited for; matrix products, arithmetic and copies ran while one was open for 1% of the time, Pallas kernels for 16%

profile of v2, /device:TPU:6, one launch (start us, length us, event | category | flops | bytes accessed | tf_op | source)
XLA Modules:
  0.0 358.9 jit_solution(10119460269877092177)
XLA Ops:
  7.2 0.0 all-gather.3.cloned.1.call-start
  7.2 0.7 all-gather.3.cloned.1.call-update
  7.9 0.0 all-gather.5.cloned.1.call-start
  7.9 0.7 all-gather.5.cloned.1.call-update
  8.6 0.7 convert_bitcast_fusion.ids_ref
  9.3 0.0 copy-start.13
  9.3 0.7 pad_maximum_fusion
  10.0 0.6 broadcast_in_dim.2
  10.7 15.5 %all-to-all-start = ((f32[32,4,128]{2,1,0:T(4,128)}), f32[32,4,128]{2,1,0:T(4,128)S(1)}, u32[]{:S(2)}, u32[]{:S(2)}) async-start(f32[32,4,128]{2,1,0:T(4,128)} %broadcast_in_dim.2), calls=%async_computation | async-start | bytes 131072 | tf_op jit(solution)/shard_map/all_to_all | solution.py:567
  26.1 0.0 copy-done.13
  26.2 5.1 %grad_rows.1 = bf16[5120,128]{1,0:T(8,128)(2,1)} custom-call(f32[2,128]{1,0:T(2,128)} %copy-done.13, bf16[2048,128]{1,0:T(8,128)(2,1)} %grad_ref.1), custom_call_target="tpu_custom_call" | custom-call | flops 167772160 | bytes 4194304 | tf_op jit(solution)/shard_map/grad_rows/pallas_call | solution.py:89
  31.2 9.3 %all-to-all-done = f32[32,4,128]{2,1,0:T(4,128)S(1)} async-done(((f32[32,4,128]{2,1,0:T(4,128)}), f32[32,4,128]{2,1,0:T(4,128)S(1)}, u32[]{:S(2)}, u32[]{:S(2)}) %all-to-all-start) | async-done | bytes 65568 | tf_op jit(solution)/shard_map/all_to_all | solution.py:567
  40.6 0.0 copy-start.12
  40.6 4.1 %all-to-all-start.2 = ((bf16[32,160,128]{2,1,0:T(8,128)(2,1)}), bf16[32,160,128]{2,1,0:T(8,128)(2,1)S(1)}, u32[]{:S(2)}, u32[]{:S(2)}) async-start(bf16[32,160,128]{2,1,0:T(8,128)(2,1)} %bitcast.22), calls=%async_computation.2 | async-start | bytes 2621440 | tf_op jit(solution)/shard_map/all_to_all | solution.py:544
  44.7 0.0 copy-done.12
  44.7 0.6 reshape.49.decay_ref
  45.3 4.1 %shard_state.1 = (f32[256,128]{1,0:T(8,128)}, f32[256,128]{1,0:T(8,128)}, f32[72,128]{1,0:T(8,128)}) custom-call(s32[8]{0:T(128)} %docs_ref.1, s32[1]{0:T(128)} %bitcast.2.base_ref, f32[64,128]{1,0:T(8,128)} %reshape.49.decay_ref, bf16[64,4096]{1,0:T(8,128)(2,1)} %x_ref.3, bf16[128,4096]{1,0:T(8,128)(2,1)} %write_ref.5), custom_call_target="tpu_custom_call" | custom-call | flops 67108864 | bytes 3145728 | tf_op jit(solution)/shard_map/shard_state/pallas_call | solution.py:89
  49.4 3.5 collective-permute-start.3
  52.9 3.7 %collective-permute-start.2 = (f32[72,128]{1,0:T(8,128)}, f32[72,128]{1,0:T(8,128)S(1)}, u32[]{:S(2)}, u32[]{:S(2)}) collective-permute-start(f32[72,128]{1,0:T(8,128)} %get-tuple-element.19), channel_id=1, source_target_pairs={{0,96},{32,128},{64,160},{96,192},{128,224},{160,256},{192,288},{2... | collective-permute-start | bytes 110600 | tf_op jit(solution)/shard_map/ppermute | solution.py:539
  56.6 3.7 %collective-permute-start.1 = (f32[72,128]{1,0:T(8,128)}, f32[72,128]{1,0:T(8,128)S(1)}, u32[]{:S(2)}, u32[]{:S(2)}) collective-permute-start(f32[72,128]{1,0:T(8,128)} %get-tuple-element.19), channel_id=1, source_target_pairs={{0,64},{32,96},{64,128},{96,160},{128,192},{160,224},{192,256},{22... | collective-permute-start | bytes 110600 | tf_op jit(solution)/shard_map/ppermute | solution.py:539
  60.4 4.0 %collective-permute-start = (f32[72,128]{1,0:T(8,128)}, f32[72,128]{1,0:T(8,128)S(1)}, u32[]{:S(2)}, u32[]{:S(2)}) collective-permute-start(f32[72,128]{1,0:T(8,128)} %get-tuple-element.19), channel_id=1, source_target_pairs={{0,32},{32,64},{64,96},{96,128},{128,160},{160,192},{192,224},{224... | collective-permute-start | bytes 110600 | tf_op jit(solution)/shard_map/ppermute | solution.py:539
  64.4 0.6 copy.15
  65.0 0.0 collective-permute-done.3.m4_ref
  65.0 0.0 collective-permute-done.2.m3_ref
  65.0 0.0 copy-start.5
  65.1 0.0 collective-permute-done.1.m2_ref
  65.1 0.0 copy-start.6
  65.1 2.1 collective-permute-done.m1_ref
  67.2 0.0 copy-done.4
  67.2 0.0 copy-done.5
  67.2 0.0 copy-done.6
  67.2 0.6 copy-done.7
  67.8 16.1 %mixer_forward.1 = (bf16[8192,128]{1,0:T(8,128)(2,1)}, bf16[5120,128]{1,0:T(8,128)(2,1)}, f32[1024,128]{1,0:T(8,128)}, f32[320,128]{1,0:T(8,128)}, f32[320,128]{1,0:T(8,128)}) custom-call(s32[1]{0:T(128)} %bitcast.1.expert_ref, f32[72,128]{1,0:T(8,128)} %copy-done.7, f32[72,128]{1,0:T(8,128)} %copy-done.6, f32[72,128]{1,0:T(8,128)} %copy-done.5, ...), custom_call_target="tpu_custom_call" | custom-call | flops 268435456 | bytes 9437184 | tf_op jit(solution)/shard_map/mixer_forward/pallas_call | solution.py:89
  83.9 28.5 %all-to-all-done.2 = bf16[32,160,128]{2,1,0:T(8,128)(2,1)S(1)} async-done(((bf16[32,160,128]{2,1,0:T(8,128)(2,1)}), bf16[32,160,128]{2,1,0:T(8,128)(2,1)S(1)}, u32[]{:S(2)}, u32[]{:S(2)}) %all-to-all-start.2) | async-done | bytes 1310752 | tf_op jit(solution)/shard_map/all_to_all | solution.py:544
  112.4 1.1 copy-done.2
  113.5 4.0 %all-to-all-start.1 = ((bf16[32,160,128]{2,1,0:T(8,128)(2,1)}), bf16[32,160,128]{2,1,0:T(8,128)(2,1)S(1)}, u32[]{:S(2)}, u32[]{:S(2)}) async-start(bf16[32,160,128]{2,1,0:T(8,128)(2,1)} %bitcast.27), calls=%async_computation.1 | async-start | bytes 2621440 | tf_op jit(solution)/shard_map/all_to_all | solution.py:544
  117.5 0.0 all-gather.3.cloned.1.call-done
  117.5 5.8 %hidden_grad.1 = (bf16[320,2048]{1,0:T(8,128)(2,1)}, f32[320,768]{1,0:T(8,128)}) custom-call(bf16[5120,128]{1,0:T(8,128)(2,1)} %bitcast.25, f32[320,128]{1,0:T(8,128)} %get-tuple-element.23.weight_ref, bf16[2048,768]{1,0:T(8,128)(2,1)} %bitcast.20), custom_call_target="tpu_custom_call" | custom-call | flops 1006632960 | bytes 8388608 | tf_op jit(solution)/shard_map/hidden_grad/pallas_call | solution.py:89
  123.3 61.9 %all-to-all-done.1 = bf16[32,160,128]{2,1,0:T(8,128)(2,1)S(1)} async-done(((bf16[32,160,128]{2,1,0:T(8,128)(2,1)}), bf16[32,160,128]{2,1,0:T(8,128)(2,1)S(1)}, u32[]{:S(2)}, u32[]{:S(2)}) %all-to-all-start.1) | async-done | bytes 1310752 | tf_op jit(solution)/shard_map/all_to_all | solution.py:544
  185.2 1.1 copy-done.3
  186.3 15.3 %expert.1 = (bf16[5120,128]{1,0:T(8,128)(2,1)}, bf16[320,2048]{1,0:T(8,128)(2,1)}, bf16[320,768]{1,0:T(8,128)(2,1)}) custom-call(bf16[5120,128]{1,0:T(8,128)(2,1)} %bitcast.28, f32[1,2048]{1,0:T(1,128)} %bitcast.34, f32[320,128]{1,0:T(8,128)} %get-tuple-element.22.first_ref, bf16[320,2048]{1,0:T(8,128)(2,1)} %get-tuple-element.24.grad_ref, ...), custom_call_target="tpu_custom_call" | custom-call | flops 4026531840 | bytes 14680064 | tf_op jit(solution)/shard_map/expert/pallas_call | solution.py:89
  201.6 4.0 %all-to-all-start.4 = ((bf16[32,160,128]{2,1,0:T(8,128)(2,1)}), bf16[32,160,128]{2,1,0:T(8,128)(2,1)S(1)}, u32[]{:S(2)}, u32[]{:S(2)}) async-start(bf16[32,160,128]{2,1,0:T(8,128)(2,1)} %bitcast.29), calls=%async_computation.4 | async-start | bytes 2621440 | tf_op jit(solution)/shard_map/all_to_all | solution.py:544
  205.6 9.3 %expert_out.1 = bf16[5120,128]{1,0:T(8,128)(2,1)} custom-call(bf16[320,768]{1,0:T(8,128)(2,1)} %get-tuple-element.26.hidden_ref, bf16[320,2048]{1,0:T(8,128)(2,1)} %get-tuple-element.27.normed_ref, f32[320,128]{1,0:T(8,128)} %get-tuple-element.23.weight_ref, f32[320,128]{1,0:T(8,128)} %get-tuple-element.22.first_ref, bf16[2048,768]{1,0:T(8,128)(2,1)} %bitcast.21), custom_call_target="tpu_custom_call" | custom-call | flops 1006632960 | bytes 8388608 | tf_op jit(solution)/shard_map/expert_out/pallas_call | solution.py:89
  214.9 58.4 %all-to-all-done.4 = bf16[32,160,128]{2,1,0:T(8,128)(2,1)S(1)} async-done(((bf16[32,160,128]{2,1,0:T(8,128)(2,1)}), bf16[32,160,128]{2,1,0:T(8,128)(2,1)S(1)}, u32[]{:S(2)}, u32[]{:S(2)}) %all-to-all-start.4) | async-done | bytes 1310752 | tf_op jit(solution)/shard_map/all_to_all | solution.py:544
  273.3 1.1 copy-done.1
  274.4 3.9 %all-to-all-start.3 = ((bf16[32,160,128]{2,1,0:T(8,128)(2,1)}), bf16[32,160,128]{2,1,0:T(8,128)(2,1)S(1)}, u32[]{:S(2)}, u32[]{:S(2)}) async-start(bf16[32,160,128]{2,1,0:T(8,128)(2,1)} %bitcast.26), calls=%async_computation.3 | async-start | bytes 2621440 | tf_op jit(solution)/shard_map/all_to_all | solution.py:544
  278.4 7.5 %mixer_grad.1 = (bf16[64,4096]{1,0:T(8,128)(2,1)}, f32[72,128]{1,0:T(8,128)}) custom-call(bf16[5120,128]{1,0:T(8,128)(2,1)} %bitcast.24, f32[1024,128]{1,0:T(8,128)} %get-tuple-element.29.rank_ref, bf16[128,4096]{1,0:T(8,128)(2,1)} %read_ref.5, f32[256,128]{1,0:T(8,128)} %get-tuple-element.30.dt_ref), custom_call_target="tpu_custom_call" | custom-call | flops 268435456 | bytes 6291456 | tf_op jit(solution)/shard_map/mixer_grad/pallas_call | solution.py:89
  285.8 1.3 collective-permute-start.7
  287.1 2.4 collective-permute-start.6
  289.5 2.2 collective-permute-start.5
  291.7 1.9 collective-permute-start.4
  293.7 0.0 collective-permute-done.7.m4_ref
  293.7 0.0 copy-start.8
  293.7 0.4 collective-permute-done.6.m3_ref
  294.1 3.9 %collective-permute-done.5.m2_ref = f32[72,128]{1,0:T(8,128)S(1)} collective-permute-done((f32[72,128]{1,0:T(8,128)}, f32[72,128]{1,0:T(8,128)S(1)}, u32[]{:S(2)}, u32[]{:S(2)}) %collective-permute-start.5) | collective-permute-done | bytes 36896 | tf_op jit(solution)/shard_map/ppermute | solution.py:539
  298.0 1.9 collective-permute-done.4.m1_ref
  299.9 0.0 copy-done.8
  299.9 0.0 copy-done.9
  299.9 0.0 copy-done.10
  299.9 0.6 copy-done.11
  300.5 8.7 %mixer_backward.1 = bf16[64,4096]{1,0:T(8,128)(2,1)} custom-call(f32[72,128]{1,0:T(8,128)} %copy-done.11, f32[72,128]{1,0:T(8,128)} %copy-done.10, f32[72,128]{1,0:T(8,128)} %copy-done.9, f32[72,128]{1,0:T(8,128)} %copy-done.8, f32[256,128]{1,0:T(8,128)} %get-tuple-element.20.rt_ref, bf16[64,4096]{1,0:T(8,128)(2,1)} %get-tuple-element.32.grad_ref, ...), custom_call_target="tpu_custom_call" | custom-call | flops 268435456 | bytes 6291456 | tf_op jit(solution)/shard_map/mixer_backward/pallas_call | solution.py:89
  309.2 36.9 %all-to-all-done.3 = bf16[32,160,128]{2,1,0:T(8,128)(2,1)S(1)} async-done(((bf16[32,160,128]{2,1,0:T(8,128)(2,1)}), bf16[32,160,128]{2,1,0:T(8,128)(2,1)S(1)}, u32[]{:S(2)}, u32[]{:S(2)}) %all-to-all-start.3) | async-done | bytes 1310752 | tf_op jit(solution)/shard_map/all_to_all | solution.py:544
  346.1 1.1 copy-done
  347.2 4.9 %combine.1 = bf16[2048,128]{1,0:T(8,128)(2,1)} custom-call(f32[2,128]{1,0:T(2,128)} %copy-done.13, bf16[5120,128]{1,0:T(8,128)(2,1)} %bitcast.23), custom_call_target="tpu_custom_call" | custom-call | flops 167772160 | bytes 4194304 | tf_op jit(solution)/shard_map/combine/pallas_call | solution.py:89
  (11 shorter events, 0.0 us)
Async XLA Ops:
  7.2 110.3 %all-gather.3.cloned.1.call-start = ((), (), s32[]{:S(2)}) async-start(), calls=%async_computation.5 | async-start | bytes 3342336 | tf_op jit(solution)/shard_map/all_gather | solution.py:585
  7.9 177.3 %all-gather.5.cloned.1.call-start = ((), (), s32[]{:S(2)}) async-start(), calls=%async_computation.6 | async-start | bytes 6684672 | tf_op jit(solution)/shard_map/all_gather | solution.py:584
  9.3 16.8 %copy-start.13 = (f32[2,128]{1,0:T(2,128)}, f32[2,128]{1,0:T(2,128)S(1)}, u32[]{:S(2)}) copy-start(f32[2,128]{1,0:T(2,128)S(1)} %convert_bitcast_fusion.ids_ref) | copy-start | bytes 3076
  10.7 29.9 %all-to-all-start = ((f32[32,4,128]{2,1,0:T(4,128)}), f32[32,4,128]{2,1,0:T(4,128)S(1)}, u32[]{:S(2)}, u32[]{:S(2)}) async-start(f32[32,4,128]{2,1,0:T(4,128)} %broadcast_in_dim.2), calls=%async_computation | async-start | bytes 131072 | tf_op jit(solution)/shard_map/all_to_all | solution.py:567
  40.6 4.1 %copy-start.12 = (f32[2,4096]{1,0:T(2,128)S(1)}, f32[2,4096]{1,0:T(2,128)}, u32[]{:S(2)}) copy-start(f32[2,4096]{1,0:T(2,128)} %param.14) | copy-start | bytes 98308
  40.6 71.8 %all-to-all-start.2 = ((bf16[32,160,128]{2,1,0:T(8,128)(2,1)}), bf16[32,160,128]{2,1,0:T(8,128)(2,1)S(1)}, u32[]{:S(2)}, u32[]{:S(2)}) async-start(bf16[32,160,128]{2,1,0:T(8,128)(2,1)} %bitcast.22), calls=%async_computation.2 | async-start | bytes 2621440 | tf_op jit(solution)/shard_map/all_to_all | solution.py:544
  49.4 15.6 %collective-permute-start.3 = (f32[72,128]{1,0:T(8,128)}, f32[72,128]{1,0:T(8,128)S(1)}, u32[]{:S(2)}, u32[]{:S(2)}) collective-permute-start(f32[72,128]{1,0:T(8,128)} %get-tuple-element.19), channel_id=1, source_target_pairs={{0,128},{32,160},{64,192},{96,224},{128,256},{160,288},{192,320},{... | collective-permute-start | bytes 110600 | tf_op jit(solution)/shard_map/ppermute | solution.py:539
  52.9 12.2 %collective-permute-start.2 = (f32[72,128]{1,0:T(8,128)}, f32[72,128]{1,0:T(8,128)S(1)}, u32[]{:S(2)}, u32[]{:S(2)}) collective-permute-start(f32[72,128]{1,0:T(8,128)} %get-tuple-element.19), channel_id=1, source_target_pairs={{0,96},{32,128},{64,160},{96,192},{128,224},{160,256},{192,288},{2... | collective-permute-start | bytes 110600 | tf_op jit(solution)/shard_map/ppermute | solution.py:539
  56.6 8.4 %collective-permute-start.1 = (f32[72,128]{1,0:T(8,128)}, f32[72,128]{1,0:T(8,128)S(1)}, u32[]{:S(2)}, u32[]{:S(2)}) collective-permute-start(f32[72,128]{1,0:T(8,128)} %get-tuple-element.19), channel_id=1, source_target_pairs={{0,64},{32,96},{64,128},{96,160},{128,192},{160,224},{192,256},{22... | collective-permute-start | bytes 110600 | tf_op jit(solution)/shard_map/ppermute | solution.py:539
  60.4 6.8 %collective-permute-start = (f32[72,128]{1,0:T(8,128)}, f32[72,128]{1,0:T(8,128)S(1)}, u32[]{:S(2)}, u32[]{:S(2)}) collective-permute-start(f32[72,128]{1,0:T(8,128)} %get-tuple-element.19), channel_id=1, source_target_pairs={{0,32},{32,64},{64,96},{96,128},{128,160},{160,192},{192,224},{224... | collective-permute-start | bytes 110600 | tf_op jit(solution)/shard_map/ppermute | solution.py:539
  65.0 2.2 copy-start.4
  65.0 2.2 copy-start.5
  65.1 2.1 copy-start.6
  67.2 0.6 copy-start.7
  112.4 1.1 copy-start.2
  113.5 71.7 %all-to-all-start.1 = ((bf16[32,160,128]{2,1,0:T(8,128)(2,1)}), bf16[32,160,128]{2,1,0:T(8,128)(2,1)S(1)}, u32[]{:S(2)}, u32[]{:S(2)}) async-start(bf16[32,160,128]{2,1,0:T(8,128)(2,1)} %bitcast.27), calls=%async_computation.1 | async-start | bytes 2621440 | tf_op jit(solution)/shard_map/all_to_all | solution.py:544
  185.2 1.1 copy-start.3
  201.6 71.7 %all-to-all-start.4 = ((bf16[32,160,128]{2,1,0:T(8,128)(2,1)}), bf16[32,160,128]{2,1,0:T(8,128)(2,1)S(1)}, u32[]{:S(2)}, u32[]{:S(2)}) async-start(bf16[32,160,128]{2,1,0:T(8,128)(2,1)} %bitcast.29), calls=%async_computation.4 | async-start | bytes 2621440 | tf_op jit(solution)/shard_map/all_to_all | solution.py:544
  273.3 1.1 copy-start.1
  274.4 71.7 %all-to-all-start.3 = ((bf16[32,160,128]{2,1,0:T(8,128)(2,1)}), bf16[32,160,128]{2,1,0:T(8,128)(2,1)S(1)}, u32[]{:S(2)}, u32[]{:S(2)}) async-start(bf16[32,160,128]{2,1,0:T(8,128)(2,1)} %bitcast.26), calls=%async_computation.3 | async-start | bytes 2621440 | tf_op jit(solution)/shard_map/all_to_all | solution.py:544
  285.8 7.8 %collective-permute-start.7 = (f32[72,128]{1,0:T(8,128)}, f32[72,128]{1,0:T(8,128)S(1)}, u32[]{:S(2)}, u32[]{:S(2)}) collective-permute-start(f32[72,128]{1,0:T(8,128)} %get-tuple-element.31), channel_id=1, source_target_pairs={{128,0},{160,32},{192,64},{224,96},{256,128},{288,160},{320,192},{... | collective-permute-start | bytes 110600 | tf_op jit(solution)/shard_map/ppermute | solution.py:539
  287.1 7.0 %collective-permute-start.6 = (f32[72,128]{1,0:T(8,128)}, f32[72,128]{1,0:T(8,128)S(1)}, u32[]{:S(2)}, u32[]{:S(2)}) collective-permute-start(f32[72,128]{1,0:T(8,128)} %get-tuple-element.31), channel_id=1, source_target_pairs={{96,0},{128,32},{160,64},{192,96},{224,128},{256,160},{288,192},{3... | collective-permute-start | bytes 110600 | tf_op jit(solution)/shard_map/ppermute | solution.py:539
  289.5 8.5 %collective-permute-start.5 = (f32[72,128]{1,0:T(8,128)}, f32[72,128]{1,0:T(8,128)S(1)}, u32[]{:S(2)}, u32[]{:S(2)}) collective-permute-start(f32[72,128]{1,0:T(8,128)} %get-tuple-element.31), channel_id=1, source_target_pairs={{64,0},{96,32},{128,64},{160,96},{192,128},{224,160},{256,192},{28... | collective-permute-start | bytes 110600 | tf_op jit(solution)/shard_map/ppermute | solution.py:539
  291.7 8.2 %collective-permute-start.4 = (f32[72,128]{1,0:T(8,128)}, f32[72,128]{1,0:T(8,128)S(1)}, u32[]{:S(2)}, u32[]{:S(2)}) collective-permute-start(f32[72,128]{1,0:T(8,128)} %get-tuple-element.31), channel_id=1, source_target_pairs={{32,0},{64,32},{96,64},{128,96},{160,128},{192,160},{224,192},{256... | collective-permute-start | bytes 110600 | tf_op jit(solution)/shard_map/ppermute | solution.py:539
  293.7 6.2 %copy-start.8 = (f32[72,128]{1,0:T(8,128)}, f32[72,128]{1,0:T(8,128)S(1)}, u32[]{:S(2)}) copy-start(f32[72,128]{1,0:T(8,128)S(1)} %collective-permute-done.7.m4_ref) | copy-start | bytes 110596
  294.1 5.8 %copy-start.9 = (f32[72,128]{1,0:T(8,128)}, f32[72,128]{1,0:T(8,128)S(1)}, u32[]{:S(2)}) copy-start(f32[72,128]{1,0:T(8,128)S(1)} %collective-permute-done.6.m3_ref) | copy-start | bytes 110596
  298.0 1.9 copy-start.10
  299.9 0.6 copy-start.11
  346.1 1.1 copy-start
Sparse Core Ops, SparseCore 0:
  11.0 66.9 all-gather.2
  81.0 76.4 all-gather.4

commit v3 on v2

--- a/solution.py
+++ b/solution.py
@@ -16,6 +16,7 @@
 HP = 64
 HEAD = 32
 EXPERTS = 32
+CHIPS = 16
 CAP = 10
 SLOTS = EXPERTS * CAP
 BLOCK = CAP * PAIRS
@@ -62,8 +63,11 @@
     return jnp.where(row < col, 1.0, 0.0).astype(bf16)
 
 
-def rank_table(first_ids, second_ids, earlier):
-    expert = lax.broadcasted_iota(i32, (EXPERTS, LANES), 0).astype(f32)
+def rank_table(first_ids, second_ids, earlier, experts=EXPERTS, core=None):
+    expert = lax.broadcasted_iota(i32, (experts, LANES), 0)
+    if core is not None:
+        expert = 2 * expert + core
+    expert = expert.astype(f32)
     picked = (expert == first_ids) | (expert == second_ids)
     rank = dot(jnp.where(picked, 1.0, 0.0).astype(bf16), earlier)
     return jnp.where(picked, rank, -1.0)
@@ -103,17 +107,26 @@
 HBM = pl.BlockSpec(memory_space=pl.ANY)
 
 
-def grad_rows_kernel(ids_ref, grad_ref, out_ref, wide_ref):
-    ranks = rank_table(ids_ref[0:1, :], ids_ref[1:2, :], earlier_mask())
-    select = slot_onehot(ranks)
+def grad_rows_kernel(core_ref, own_ids_ref, their_ids_ref, own_ref, their_ref, out_ref, wide_ref):
+    core = core_ref[0]
+    earlier = earlier_mask()
+
+    def select_of(ids_ref):
+        return slot_onehot(rank_table(ids_ref[0:1, :], ids_ref[1:2, :], earlier, CHIPS, core))
+
+    own_select, their_select = select_of(own_ids_ref), select_of(their_ids_ref)
 
     def step(fb, carry):
-        at = pl.multiple_of(fb * LANES, LANES)
-        rows = dot_last(select, grad_ref[pl.ds(at, LANES), :])
-        for c in range(CAP):
-            wide_ref[pl.ds(c * FBLOCKS + fb, EXPERTS, stride=BLOCK), :] = rows[
-                c * EXPERTS : (c + 1) * EXPERTS
-            ]
+        feats = pl.ds(pl.multiple_of(fb * LANES, LANES), LANES)
+        for select, grad_ref, side in (
+            (own_select, own_ref, core),
+            (their_select, their_ref, 1 - core),
+        ):
+            rows = dot_last(select, grad_ref[feats, :])
+            for c in range(CAP):
+                wide_ref[pl.ds(side * BLOCK + c * FBLOCKS + fb, CHIPS, stride=2 * BLOCK), :] = rows[
+                    c * CHIPS : (c + 1) * CHIPS
+                ]
         return carry
 
     lax.fori_loop(0, FBLOCKS, step, 0, unroll=4)
@@ -211,43 +224,8 @@
 
 
 def forward_kernel(
-    expert_ref,
-    m1_ref,
-    m2_ref,
-    m3_ref,
-    m4_ref,
-    rt_ref,
-    x_ref,
-    write_ref,
-    read_ref,
-    ids_ref,
-    pair_ref,
-    msg_ref,
-    rank_ref,
-    weight_ref,
-    first_ref,
-    wide_ref,
-    y_ref,
+    m1_ref, m2_ref, m3_ref, m4_ref, rt_ref, x_ref, write_ref, read_ref, y_ref, pair_ref
 ):
-    earlier = earlier_mask()
-    mine = expert_ref[0].astype(f32)
-    is_first = ids_ref[0] == mine
-    is_second = ids_ref[1] == mine
-    picked = is_first | is_second
-    rank = dot(jnp.where(picked, 1.0, 0.0).astype(bf16), earlier)
-    rank = jnp.where(picked, rank, -1.0)
-    route = jnp.where(is_first, ids_ref[2], jnp.where(is_second, ids_ref[3], 0.0))
-    first = jnp.where(is_first, 1.0, 0.0)
-    for c in range(CAP):
-        here = rank == float(c)
-        route_c = jnp.sum(jnp.where(here, route, 0.0), axis=1, keepdims=True)
-        first_c = jnp.sum(jnp.where(here, first, 0.0), axis=1, keepdims=True)
-        for par in range(2):
-            at = (par * CAP + c) * PAIRS
-            part = slice(par * PAIRS, (par + 1) * PAIRS)
-            weight_ref[at : at + PAIRS, :] = jnp.broadcast_to(route_c[part], (PAIRS, LANES))
-            first_ref[at : at + PAIRS, :] = jnp.broadcast_to(first_c[part], (PAIRS, LANES))
-
     row_i = lax.broadcasted_iota(i32, (LANES, LANES), 0)
     col_i = lax.broadcasted_iota(i32, (LANES, LANES), 1)
     causal = row_i <= col_i
@@ -279,32 +257,50 @@
 
     lax.fori_loop(0, CHUNKS, step, chained((m1_ref, m2_ref, m3_ref, m4_ref)), unroll=4)
 
-    zero = jnp.zeros((HP, LANES), bf16)
-
-    def dispatch(jp, carry):
-        tables = []
+
+def dispatch_kernel(
+    expert_ref, own_ref, their_ref, ids_ref, msg_ref, rank_ref, weight_ref, first_ref, wide_ref
+):
+    core = lax.rem(expert_ref[0], 2)
+    earlier = earlier_mask()
+    mine = expert_ref[0].astype(f32)
+    is_first = ids_ref[0] == mine
+    is_second = ids_ref[1] == mine
+    picked = is_first | is_second
+    rank = dot(jnp.where(picked, 1.0, 0.0).astype(bf16), earlier)
+    rank = jnp.where(picked, rank, -1.0)
+    route = jnp.where(is_first, ids_ref[2], jnp.where(is_second, ids_ref[3], 0.0))
+    first = jnp.where(is_first, 1.0, 0.0)
+    for c in range(CAP):
+        here = rank == float(c)
+        route_c = jnp.sum(jnp.where(here, route, 0.0), axis=1, keepdims=True)
+        first_c = jnp.sum(jnp.where(here, first, 0.0), axis=1, keepdims=True)
+        for par in range(2):
+            at = (par * CAP + c) * PAIRS
+            part = slice(par * PAIRS, (par + 1) * PAIRS)
+            weight_ref[at : at + PAIRS, :] = jnp.broadcast_to(route_c[part], (PAIRS, LANES))
+            first_ref[at : at + PAIRS, :] = jnp.broadcast_to(first_c[part], (PAIRS, LANES))
+
+    def step(jp, carry):
         for par in range(2):
             j = par * PAIRS + jp
             table = rank_table(
-                ids_ref[0, pl.ds(j, 1), :], ids_ref[1, pl.ds(j, 1), :], earlier
+                ids_ref[0, pl.ds(j, 1), :], ids_ref[1, pl.ds(j, 1), :], earlier, CHIPS, core
             )
-            at = pl.multiple_of(jp * 64 + par * EXPERTS, EXPERTS)
-            rank_ref[pl.ds(at, EXPERTS), :] = table
-            tables.append(table)
-        select = slot_onehot(jnp.concatenate(tables, axis=1))
-        even = y_ref[:, pl.ds(pl.multiple_of(jp * 2 * LANES, LANES), LANES)]
-        odd = y_ref[:, pl.ds(pl.multiple_of(jp * 2 * LANES + LANES, LANES), LANES)]
-        both = jnp.concatenate(
-            [jnp.concatenate([even, zero], axis=1), jnp.concatenate([zero, odd], axis=1)], axis=0
-        )
-        rows = dot_last(select, both)
-        for c in range(CAP):
-            wide_ref[pl.ds(c * PAIRS + jp, EXPERTS, stride=BLOCK), :] = rows[
-                c * EXPERTS : (c + 1) * EXPERTS
-            ]
-        return carry
-
-    lax.fori_loop(0, PAIRS, dispatch, 0, unroll=2)
+            rank_ref[pl.ds(pl.multiple_of((2 * jp + par) * CHIPS, CHIPS), CHIPS), :] = table
+            lanes = pl.ds(pl.multiple_of((2 * jp + par) * LANES, LANES), LANES)
+            own = own_ref[:, lanes]
+            their = their_ref[:, lanes]
+            both = jnp.concatenate(
+                [jnp.where(core == 0, own, their), jnp.where(core == 0, their, own)], axis=0
+            )
+            rows = dot_last(slot_onehot(table), both)
+            for c in range(CAP):
+                at = par * BLOCK + c * PAIRS + jp
+                wide_ref[pl.ds(at, CHIPS, stride=2 * BLOCK), :] = rows[c * CHIPS : (c + 1) * CHIPS]
+        return carry
+
+    lax.fori_loop(0, PAIRS, step, 0, unroll=2)
     round_rows(msg_ref, wide_ref)
 
 
@@ -358,21 +354,14 @@
 ):
     fetch = pltpu.make_async_copy(in_hbm, in_ref, sem)
     fetch.start()
-    lane = lax.broadcasted_iota(i32, (BLOCK, LANES), 1)
-    low = lane < 64
 
     def unpack(k, squares):
         lanes = pl.ds(pl.multiple_of(k * LANES, LANES), LANES)
-        at = pl.multiple_of(k * 2 * BLOCK, BLOCK)
-        a = rows_ref[pl.ds(at, BLOCK), :].astype(f32)
-        b = rows_ref[pl.ds(at + BLOCK, BLOCK), :].astype(f32)
-        even = jnp.where(low, a, pltpu.roll(b, 64, 1))
-        odd = jnp.where(low, pltpu.roll(a, 64, 1), b)
-        both = jnp.concatenate([even, odd], axis=0)
-        y_ref[:, lanes] = both
-        return squares + both * both
-
-    squares = lax.fori_loop(0, FBLOCKS, unpack, jnp.zeros((SLOTS, LANES), f32))
+        y = rows_ref[pl.ds(pl.multiple_of(k * SLOTS, SLOTS), SLOTS), :].astype(f32)
+        y_ref[:, lanes] = y
+        return squares + y * y
+
+    squares = lax.fori_loop(0, FBLOCKS, unpack, jnp.zeros((SLOTS, LANES), f32), unroll=2)
     mean = jnp.sum(squares, axis=1, keepdims=True) * (1.0 / WIDTH)
     rscale = lax.rsqrt(mean + 1e-06)
     rscale_b = jnp.broadcast_to(rscale, (SLOTS, LANES))
@@ -382,7 +371,7 @@
         normed_ref[:, lanes] = (y_ref[:, lanes] * rscale_b * gain_ref[:, lanes]).astype(bf16)
         return carry
 
-    lax.fori_loop(0, FBLOCKS, scale, 0)
+    lax.fori_loop(0, FBLOCKS, scale, 0, unroll=4)
     fetch.wait()
 
     def project(i, carry):
@@ -418,15 +407,10 @@
     def pack(k, carry):
         lanes = pl.ds(pl.multiple_of(k * LANES, LANES), LANES)
         part = rscale_b * scaled_ref[:, lanes] - pull * y_ref[:, lanes]
-        even, odd = part[:BLOCK], part[BLOCK:]
-        row = pl.multiple_of(k * 2 * BLOCK, BLOCK)
-        msg_ref[pl.ds(row, BLOCK), :] = jnp.where(low, even, pltpu.roll(odd, 64, 1)).astype(bf16)
-        msg_ref[pl.ds(row + BLOCK, BLOCK), :] = jnp.where(low, pltpu.roll(even, 64, 1), odd).astype(
-            bf16
-        )
-        return carry
-
-    lax.fori_loop(0, FBLOCKS, pack, 0)
+        msg_ref[pl.ds(pl.multiple_of(k * SLOTS, SLOTS), SLOTS), :] = part.astype(bf16)
+        return carry
+
+    lax.fori_loop(0, FBLOCKS, pack, 0, unroll=4)
 
 
 def expert_out_kernel(
@@ -478,31 +462,43 @@
     lax.fori_loop(0, FBLOCKS, step, 0, unroll=4)
 
 
-def grad_kernel(rows_ref, rank_ref, read_ref, dt_ref, out_ref, msg_ref, wide_ref):
+def slot_sums_kernel(core_ref, rows_ref, rank_ref, own_ref, their_ref, wide_ref):
     round_rows(wide_ref, rows_ref)
-
-    def step(jp, acc):
-        at = pl.multiple_of(jp * 64, 64)
-        ranks = rank_ref[pl.ds(at, 64), :]
-        select = slot_onehot(jnp.concatenate([ranks[:EXPERTS], ranks[EXPERTS:]], axis=1))
-        rows = jnp.concatenate(
-            [
-                wide_ref[pl.ds(c * PAIRS + jp, EXPERTS, stride=BLOCK), :].astype(bf16)
-                for c in range(CAP)
-            ],
-            axis=0,
-        )
-        both = dot_first(rows, select)
+    core = core_ref[0]
+
+    def step(jp, carry):
         for par in range(2):
+            ranks = rank_ref[pl.ds(pl.multiple_of((2 * jp + par) * CHIPS, CHIPS), CHIPS), :]
+            rows = jnp.concatenate(
+                [
+                    wide_ref[
+                        pl.ds(par * BLOCK + c * PAIRS + jp, CHIPS, stride=2 * BLOCK), :
+                    ].astype(bf16)
+                    for c in range(CAP)
+                ],
+                axis=0,
+            )
+            sums = dot_first(rows, slot_onehot(ranks))
+            low, high = sums[:HP], sums[HP:]
             lanes = pl.ds(pl.multiple_of((2 * jp + par) * LANES, LANES), LANES)
-            grad = both[par * HP : (par + 1) * HP, par * LANES : (par + 1) * LANES].astype(bf16)
-            out_ref[:, lanes] = grad
-            rows_k = dt_ref[pl.ds(pl.multiple_of((2 * jp + par) * 8, 8), 8), :]
-            weighted = (grad.astype(f32) * rows_of(rows_k[0:1], rows_k[1:2])).astype(bf16)
-            acc = acc + dot_last(weighted, read_ref[:, lanes])
-        return acc
-
-    msg_ref[0:HP, :] = lax.fori_loop(0, PAIRS, step, jnp.zeros((HP, LANES), f32), unroll=2)
+            own_ref[:, lanes] = jnp.where(core == 0, low, high)
+            their_ref[:, lanes] = jnp.where(core == 0, high, low).astype(bf16)
+        return carry
+
+    lax.fori_loop(0, PAIRS, step, 0, unroll=2)
+
+
+def grad_kernel(own_ref, their_ref, read_ref, dt_ref, out_ref, msg_ref):
+    def step(k, acc):
+        lanes = pl.ds(pl.multiple_of(k * LANES, LANES), LANES)
+        grad = (own_ref[:, lanes] + their_ref[:, lanes].astype(f32)).astype(bf16)
+        out_ref[:, lanes] = grad
+        rows_k = dt_ref[pl.ds(pl.multiple_of(k * 8, 8), 8), :]
+        weighted = (grad.astype(f32) * rows_of(rows_k[0:1], rows_k[1:2])).astype(bf16)
+        return acc + dot_last(weighted, read_ref[:, lanes])
+
+    acc = lax.fori_loop(0, CHUNKS, step, jnp.zeros((HP, LANES), f32), unroll=4)
+    msg_ref[0:HP, :] = acc
     last = dt_ref[(CHUNKS - 1) * 8 : CHUNKS * 8, :]
     msg_ref[HP : HP + 8, :] = jnp.broadcast_to(last[:, LANES - 1 : LANES], (8, LANES))
 
@@ -546,6 +542,18 @@
     )
 
 
+def exchanged_by_core(rows):
+    blocks = rows.reshape(CHIPS, SLOTS, LANES)
+    groups = [list(range(core, EXPERTS, 2)) for core in range(2)]
+    return lax.all_to_all(
+        blocks, "exp", split_axis=0, concat_axis=0, tiled=True, axis_index_groups=groups
+    ).reshape(ROWS, LANES)
+
+
+def from_other_core(value):
+    return lax.ppermute(value, "exp", [(i, i ^ 1) for i in range(EXPERTS)])
+
+
 def per_device(
     features,
     write_vectors,
@@ -569,17 +577,21 @@
     )
     tokens = tokens.reshape(PAIRS, 2, 4, LANES).transpose(2, 1, 0, 3).reshape(4, CHUNKS, LANES)
 
+    me_core = lax.rem(me_exp, 2).astype(i32).reshape(1)
+
+    their_ids = from_other_core(ids_own)
+    their_grad = from_other_core(out_grad)
     (grad_out_rows,) = call(
         grad_rows_kernel,
         [((ROWS, LANES), bf16)],
-        (ids_own, out_grad),
-        [VM, VM],
+        (me_core, ids_own, their_ids, out_grad, their_grad),
+        [SM] + [VM] * 4,
         [wide],
         flops=2 * SLOTS * LANES * WIDTH,
         moved=4 << 20,
         name="grad_rows",
     )
-    grad_in_rows = exchanged(grad_out_rows)
+    grad_in_rows = exchanged_by_core(grad_out_rows)
 
     weight_in = lax.all_gather(expert_in, "ctx", axis=1, tiled=True)[0]
     weight_out = lax.all_gather(expert_out, "ctx", axis=1, tiled=True)[0]
@@ -599,31 +611,32 @@
         name="shard_state",
     )
     before = [sent_along(message, d) for d in range(1, REACH + 1)]
-    pairs, y_out_rows, ranks, slot_weight, slot_first = call(
+    y_own, pairs = call(
         forward_kernel,
+        [((HP, SEQ), bf16), ((2 * CHUNKS * LANES, LANES), bf16)],
+        (*before, rt, features, write_vectors, read_vectors),
+        [VM] * 8,
+        flops=8 * HP * LANES * SEQ,
+        moved=9 << 20,
+        name="mixer_forward",
+    )
+    y_their = from_other_core(y_own)
+    y_out_rows, ranks, slot_weight, slot_first = call(
+        dispatch_kernel,
         [
-            ((2 * CHUNKS * LANES, LANES), bf16),
             ((ROWS, LANES), bf16),
-            ((2 * CHUNKS // 2 * EXPERTS, LANES), f32),
+            ((CHUNKS * CHIPS, LANES), f32),
             ((SLOTS, LANES), f32),
             ((SLOTS, LANES), f32),
         ],
-        (
-            me_exp.astype(i32).reshape(1),
-            *before,
-            rt,
-            features,
-            write_vectors,
-            read_vectors,
-            tokens,
-        ),
-        [SM] + [VM] * 9,
-        [wide, pltpu.VMEM((HP, SEQ), bf16)],
-        flops=8 * HP * LANES * SEQ,
-        moved=9 << 20,
-        name="mixer_forward",
-    )
-    y_in_rows = exchanged(y_out_rows)
+        (me_exp.astype(i32).reshape(1), y_own, y_their, tokens),
+        [SM] + [VM] * 3,
+        [wide],
+        flops=4 * HP * SLOTS * SEQ,
+        moved=4 << 20,
+        name="dispatch",
+    )
+    y_in_rows = exchanged_by_core(y_out_rows)
 
     grad_slots, d_hidden = call(
         arrived_grad_kernel,
@@ -655,7 +668,7 @@
         moved=14 << 20,
         name="expert",
     )
-    back_in_rows = exchanged(back_out_rows)
+    back_in_rows = exchanged_by_core(back_out_rows)
 
     (result_rows,) = call(
         expert_out_kernel,
@@ -669,12 +682,21 @@
     )
     returned_rows = exchanged(result_rows)
 
+    own_sums, their_sums = call(
+        slot_sums_kernel,
+        [((HP, SEQ), f32), ((HP, SEQ), bf16)],
+        (me_core, back_in_rows, ranks),
+        [SM, VM, VM],
+        [wide],
+        flops=4 * HP * SLOTS * SEQ,
+        moved=4 << 20,
+        name="slot_sums",
+    )
     y_grad, back_message = call(
         grad_kernel,
         [((HP, SEQ), bf16), ((HP + 8, LANES), f32)],
-        (back_in_rows, ranks, read_vectors, dt),
+        (own_sums, from_other_core(their_sums), read_vectors, dt),
         [VM] * 4,
-        [wide],
         flops=8 * HP * LANES * SEQ,
         moved=6 << 20,
         name="mixer_grad",

time: 360 us -> 357 us (level)
  waiting for transfers between devices: 205 us -> 172 us
  starting transfers between devices: 54.3 us -> 76.7 us
  Pallas kernels: 76.7 us -> 81.3 us
    all_to_all x4 -> x1, waiting for transfers between devices: 186 us -> 29.1 us  [exchanged(): lax.all_to_all(blocks, 'exp', split_axis=0, concat_axis=0, tiled=True)]
    all_to_all x0 -> x3, waiting for transfers between devices: none -> 123 us  [exchanged_by_core(): lax.all_to_all(blocks, 'exp', split_axis=0, concat_axis=0, tiled=True, ax...]
    all_to_all x0 -> x3, starting transfers between devices: none -> 23.8 us  [exchanged_by_core(): lax.all_to_all(blocks, 'exp', split_axis=0, concat_axis=0, tiled=True, ax...]
    all_to_all x4 -> x1, starting transfers between devices: 15.9 us -> 6.37 us  [exchanged(): lax.all_to_all(blocks, 'exp', split_axis=0, concat_axis=0, tiled=True)]
    ppermute x0 -> x4, starting transfers between devices: none -> 8.18 us  [from_other_core(): return lax.ppermute(value, 'exp', [(i, i ^ 1) for i in range(EXPERTS)])]
    pallas_call x9 -> x11, Pallas kernels: 76.7 us -> 81.3 us  [call(): pl.pallas_call(kernel, out_shape=tuple((jax.ShapeDtypeStruct(shape, kind)...]
    ppermute x0 -> x4, waiting for transfers between devices: none -> 4.1 us  [from_other_core(): return lax.ppermute(value, 'exp', [(i, i ^ 1) for i in range(EXPERTS)])]
    all_to_all x1, waiting for transfers between devices: 9.33 us -> 5.24 us  [per_device(): lax.all_to_all(jnp.broadcast_to(tokens_own[None], (EXPERTS, 4, LANES)), '...]
  transfers between devices with their start and end apart: 15 -> 19, of which waited for: 9 -> 13; matrix products, arithmetic and copies ran while one was open for 1% -> 1% of each run, Pallas kernels for 16% -> 18%
where the time goes in v3:
time: 357 us; the launch traced here: 355 us
  waiting for transfers between devices  172 us (48%)
  Pallas kernels  81.3 us (23%)
  starting transfers between devices  76.7 us (21%)
  between operations  14.3 us (4%)
  local copies, waits for them, and re-layouts  9.88 us (3%)
    all_to_all x3, waiting for transfers between devices, exchanged_by_core(): lax.all_to_all(blocks, 'exp', split_axis=0, concat_axis=0, tiled=True, ax...  123 us
    pallas_call x11, Pallas kernels, call(): pl.pallas_call(kernel, out_shape=tuple((jax.ShapeDtypeStruct(shape, kind)...  81.3 us
    all_to_all x1, waiting for transfers between devices, exchanged(): lax.all_to_all(blocks, 'exp', split_axis=0, concat_axis=0, tiled=True)  29.1 us
    all_to_all x3, starting transfers between devices, exchanged_by_core(): lax.all_to_all(blocks, 'exp', split_axis=0, concat_axis=0, tiled=True, ax...  23.8 us
    ppermute x8, starting transfers between devices, sent_along(): return lax.ppermute(value, 'ctx', pairs)  22.8 us
    all_to_all x1, starting transfers between devices, per_device(): lax.all_to_all(jnp.broadcast_to(tokens_own[None], (EXPERTS, 4, LANES)), '...  15.6 us
    ppermute x8, waiting for transfers between devices, sent_along(): return lax.ppermute(value, 'ctx', pairs)  8.99 us
    ppermute x4, starting transfers between devices, from_other_core(): return lax.ppermute(value, 'exp', [(i, i ^ 1) for i in range(EXPERTS)])  8.18 us
  transfers between devices with their start and end apart: 19, of which 13 were waited for; matrix products, arithmetic and copies ran while one was open for 1% of the time, Pallas kernels for 18%

profile of v3, /device:TPU:6, one launch (start us, length us, event | category | flops | bytes accessed | tf_op | source)
XLA Modules:
  0.0 355.1 jit_solution(16996498088800270783)
XLA Ops:
  7.2 0.0 all-gather.3.cloned.1.call-start
  7.2 0.7 all-gather.3.cloned.1.call-update
  7.9 0.0 all-gather.5.cloned.1.call-start
  7.9 0.7 all-gather.5.cloned.1.call-update
  8.6 1.9 collective-permute-start.6
  10.6 0.7 convert_bitcast_fusion.own_ids_ref.ids_ref
  11.3 0.7 pad_maximum_fusion
  11.9 0.6 broadcast_in_dim.2
  12.6 15.6 %all-to-all-start = ((f32[32,4,128]{2,1,0:T(4,128)}), f32[32,4,128]{2,1,0:T(4,128)S(1)}, u32[]{:S(2)}, u32[]{:S(2)}) async-start(f32[32,4,128]{2,1,0:T(4,128)} %broadcast_in_dim.2), calls=%async_computation | async-start | bytes 131072 | tf_op jit(solution)/shard_map/all_to_all | solution.py:575
  28.2 2.2 collective-permute-start.5
  30.4 0.8 collective-permute-done.5.their_ids_ref
  31.2 0.0 collective-permute-done.6.their_ref
  31.2 0.5 copy-done.16
  31.7 0.3 copy-done.4
  32.0 5.3 %grad_rows.1 = bf16[5120,128]{1,0:T(8,128)(2,1)} custom-call(s32[1]{0:T(128)} %bitcast.10.core_ref, f32[2,128]{1,0:T(2,128)} %copy-done.15, f32[2,128]{1,0:T(2,128)} %copy-done.16, bf16[2048,128]{1,0:T(8,128)(2,1)} %own_ref.1, bf16[2048,128]{1,0:T(8,128)(2,1)} %copy-done.4), custom_call_target="tpu_custom_call" | custom-call | flops 167772160 | bytes 4194304 | tf_op jit(solution)/shard_map/grad_rows/pallas_call | solution.py:93
  37.4 5.2 %all-to-all-done = f32[32,4,128]{2,1,0:T(4,128)S(1)} async-done(((f32[32,4,128]{2,1,0:T(4,128)}), f32[32,4,128]{2,1,0:T(4,128)S(1)}, u32[]{:S(2)}, u32[]{:S(2)}) %all-to-all-start) | async-done | bytes 65568 | tf_op jit(solution)/shard_map/all_to_all | solution.py:575
  42.6 6.8 %all-to-all-start.2 = ((bf16[16,320,128]{2,1,0:T(8,128)(2,1)}), bf16[16,320,128]{2,1,0:T(8,128)(2,1)S(1)}, u32[]{:S(2)}, u32[]{:S(2)}) async-start(bf16[16,320,128]{2,1,0:T(8,128)(2,1)} %bitcast.23), calls=%async_computation.2 | async-start | bytes 2621440 | tf_op jit(solution)/shard_map/all_to_all | solution.py:548
  49.4 0.6 reshape.52.decay_ref
  50.1 4.1 %shard_state.1 = (f32[256,128]{1,0:T(8,128)}, f32[256,128]{1,0:T(8,128)}, f32[72,128]{1,0:T(8,128)}) custom-call(s32[8]{0:T(128)} %docs_ref.1, s32[1]{0:T(128)} %bitcast.2.base_ref, f32[64,128]{1,0:T(8,128)} %reshape.52.decay_ref, bf16[64,4096]{1,0:T(8,128)(2,1)} %x_ref.3, bf16[128,4096]{1,0:T(8,128)(2,1)} %write_ref.5), custom_call_target="tpu_custom_call" | custom-call | flops 67108864 | bytes 3145728 | tf_op jit(solution)/shard_map/shard_state/pallas_call | solution.py:93
  54.1 3.5 collective-permute-start.3
  57.6 3.8 %collective-permute-start.2 = (f32[72,128]{1,0:T(8,128)}, f32[72,128]{1,0:T(8,128)S(1)}, u32[]{:S(2)}, u32[]{:S(2)}) collective-permute-start(f32[72,128]{1,0:T(8,128)} %get-tuple-element.22), channel_id=1, source_target_pairs={{0,96},{32,128},{64,160},{96,192},{128,224},{160,256},{192,288},{2... | collective-permute-start | bytes 110600 | tf_op jit(solution)/shard_map/ppermute | solution.py:535
  61.4 3.7 %collective-permute-start.1 = (f32[72,128]{1,0:T(8,128)}, f32[72,128]{1,0:T(8,128)S(1)}, u32[]{:S(2)}, u32[]{:S(2)}) collective-permute-start(f32[72,128]{1,0:T(8,128)} %get-tuple-element.22), channel_id=1, source_target_pairs={{0,64},{32,96},{64,128},{96,160},{128,192},{160,224},{192,256},{22... | collective-permute-start | bytes 110600 | tf_op jit(solution)/shard_map/ppermute | solution.py:535
  65.1 4.0 %collective-permute-start = (f32[72,128]{1,0:T(8,128)}, f32[72,128]{1,0:T(8,128)S(1)}, u32[]{:S(2)}, u32[]{:S(2)}) collective-permute-start(f32[72,128]{1,0:T(8,128)} %get-tuple-element.22), channel_id=1, source_target_pairs={{0,32},{32,64},{64,96},{96,128},{128,160},{160,192},{192,224},{224... | collective-permute-start | bytes 110600 | tf_op jit(solution)/shard_map/ppermute | solution.py:535
  69.1 0.0 collective-permute-done.3.m4_ref
  69.2 0.3 collective-permute-done.1.m2_ref
  69.5 2.4 collective-permute-done.m1_ref
  71.9 0.6 copy-done.9
  72.5 11.0 %mixer_forward.1 = (bf16[64,4096]{1,0:T(8,128)(2,1)}, bf16[8192,128]{1,0:T(8,128)(2,1)}) custom-call(f32[72,128]{1,0:T(8,128)} %copy-done.9, f32[72,128]{1,0:T(8,128)} %copy-done.8, f32[72,128]{1,0:T(8,128)} %copy-done.7, f32[72,128]{1,0:T(8,128)} %copy-done.6, f32[256,128]{1,0:T(8,128)} %get-tuple-element.23.rt_ref, bf16[64,4096]{1,0:T(8,128)(2,1)} %x_ref.3, ...), custom_call_target="tpu_custom_call" | custom-call | flops 268435456 | bytes 9437184 | tf_op jit(solution)/shard_map/mixer_forward/pallas_call | solution.py:93
  83.5 1.9 collective-permute-start.4
  85.5 0.6 copy.15
  86.1 1.4 collective-permute-done.4.their_ref
  87.5 0.8 copy-done.17
  88.3 8.3 %dispatch.1 = (bf16[5120,128]{1,0:T(8,128)(2,1)}, f32[512,128]{1,0:T(8,128)}, f32[320,128]{1,0:T(8,128)}, f32[320,128]{1,0:T(8,128)}) custom-call(s32[1]{0:T(128)} %bitcast.1.expert_ref, bf16[64,4096]{1,0:T(8,128)(2,1)} %get-tuple-element.24.own_ref, bf16[64,4096]{1,0:T(8,128)(2,1)} %copy-done.17, f32[4,32,128]{2,1,0:T(8,128)} %bitcast.32), custom_call_target="tpu_custom_call" | custom-call | flops 335544320 | bytes 4194304 | tf_op jit(solution)/shard_map/dispatch/pallas_call | solution.py:93
  96.6 13.8 %all-to-all-done.2 = bf16[16,320,128]{2,1,0:T(8,128)(2,1)S(1)} async-done(((bf16[16,320,128]{2,1,0:T(8,128)(2,1)}), bf16[16,320,128]{2,1,0:T(8,128)(2,1)S(1)}, u32[]{:S(2)}, u32[]{:S(2)}) %all-to-all-start.2) | async-done | bytes 1310752 | tf_op jit(solution)/shard_map/all_to_all | solution.py:548
  110.4 1.1 copy-done.2
  111.5 8.5 %all-to-all-start.1 = ((bf16[16,320,128]{2,1,0:T(8,128)(2,1)}), bf16[16,320,128]{2,1,0:T(8,128)(2,1)S(1)}, u32[]{:S(2)}, u32[]{:S(2)}) async-start(bf16[16,320,128]{2,1,0:T(8,128)(2,1)} %bitcast.28), calls=%async_computation.1 | async-start | bytes 2621440 | tf_op jit(solution)/shard_map/all_to_all | solution.py:548
  120.0 0.0 all-gather.3.cloned.1.call-done
  120.0 5.8 %hidden_grad.1 = (bf16[320,2048]{1,0:T(8,128)(2,1)}, f32[320,768]{1,0:T(8,128)}) custom-call(bf16[5120,128]{1,0:T(8,128)(2,1)} %bitcast.26, f32[320,128]{1,0:T(8,128)} %get-tuple-element.27.weight_ref, bf16[2048,768]{1,0:T(8,128)(2,1)} %bitcast.21), custom_call_target="tpu_custom_call" | custom-call | flops 1006632960 | bytes 8388608 | tf_op jit(solution)/shard_map/hidden_grad/pallas_call | solution.py:93
  125.9 55.0 %all-to-all-done.1 = bf16[16,320,128]{2,1,0:T(8,128)(2,1)S(1)} async-done(((bf16[16,320,128]{2,1,0:T(8,128)(2,1)}), bf16[16,320,128]{2,1,0:T(8,128)(2,1)S(1)}, u32[]{:S(2)}, u32[]{:S(2)}) %all-to-all-start.1) | async-done | bytes 1310752 | tf_op jit(solution)/shard_map/all_to_all | solution.py:548
  180.9 1.1 copy-done.3
  182.0 14.1 %expert.1 = (bf16[5120,128]{1,0:T(8,128)(2,1)}, bf16[320,2048]{1,0:T(8,128)(2,1)}, bf16[320,768]{1,0:T(8,128)(2,1)}) custom-call(bf16[5120,128]{1,0:T(8,128)(2,1)} %bitcast.29, f32[1,2048]{1,0:T(1,128)} %bitcast.35, f32[320,128]{1,0:T(8,128)} %get-tuple-element.26.first_ref, bf16[320,2048]{1,0:T(8,128)(2,1)} %get-tuple-element.28.grad_ref, ...), custom_call_target="tpu_custom_call" | custom-call | flops 4026531840 | bytes 14680064 | tf_op jit(solution)/shard_map/expert/pallas_call | solution.py:93
  196.1 8.5 %all-to-all-start.4 = ((bf16[16,320,128]{2,1,0:T(8,128)(2,1)}), bf16[16,320,128]{2,1,0:T(8,128)(2,1)S(1)}, u32[]{:S(2)}, u32[]{:S(2)}) async-start(bf16[16,320,128]{2,1,0:T(8,128)(2,1)} %bitcast.30), calls=%async_computation.4 | async-start | bytes 2621440 | tf_op jit(solution)/shard_map/all_to_all | solution.py:548
  204.6 9.3 %expert_out.1 = bf16[5120,128]{1,0:T(8,128)(2,1)} custom-call(bf16[320,768]{1,0:T(8,128)(2,1)} %get-tuple-element.30.hidden_ref, bf16[320,2048]{1,0:T(8,128)(2,1)} %get-tuple-element.31.normed_ref, f32[320,128]{1,0:T(8,128)} %get-tuple-element.27.weight_ref, f32[320,128]{1,0:T(8,128)} %get-tuple-element.26.first_ref, bf16[2048,768]{1,0:T(8,128)(2,1)} %bitcast.22), custom_call_target="tpu_custom_call" | custom-call | flops 1006632960 | bytes 8388608 | tf_op jit(solution)/shard_map/expert_out/pallas_call | solution.py:93
  213.9 53.8 %all-to-all-done.4 = bf16[16,320,128]{2,1,0:T(8,128)(2,1)S(1)} async-done(((bf16[16,320,128]{2,1,0:T(8,128)(2,1)}), bf16[16,320,128]{2,1,0:T(8,128)(2,1)S(1)}, u32[]{:S(2)}, u32[]{:S(2)}) %all-to-all-start.4) | async-done | bytes 1310752 | tf_op jit(solution)/shard_map/all_to_all | solution.py:548
  267.8 1.1 copy-done.1
  268.8 6.4 %all-to-all-start.3 = ((bf16[32,160,128]{2,1,0:T(8,128)(2,1)}), bf16[32,160,128]{2,1,0:T(8,128)(2,1)S(1)}, u32[]{:S(2)}, u32[]{:S(2)}) async-start(bf16[32,160,128]{2,1,0:T(8,128)(2,1)} %bitcast.27), calls=%async_computation.3 | async-start | bytes 2621440 | tf_op jit(solution)/shard_map/all_to_all | solution.py:540
  275.2 5.7 %slot_sums.1 = (f32[64,4096]{1,0:T(8,128)}, bf16[64,4096]{1,0:T(8,128)(2,1)}) custom-call(s32[1]{0:T(128)} %bitcast.10.core_ref, bf16[5120,128]{1,0:T(8,128)(2,1)} %bitcast.25, f32[512,128]{1,0:T(8,128)} %get-tuple-element.33.rank_ref), custom_call_target="tpu_custom_call" | custom-call | flops 335544320 | bytes 4194304 | tf_op jit(solution)/shard_map/slot_sums/pallas_call | solution.py:93
  280.9 2.2 collective-permute-start.7
  283.1 1.8 collective-permute-done.7.their_ref
  284.9 0.8 copy-done.5
  285.7 4.2 %mixer_grad.1 = (bf16[64,4096]{1,0:T(8,128)(2,1)}, f32[72,128]{1,0:T(8,128)}) custom-call(f32[64,4096]{1,0:T(8,128)} %get-tuple-element.34.own_ref, bf16[64,4096]{1,0:T(8,128)(2,1)} %copy-done.5, bf16[128,4096]{1,0:T(8,128)(2,1)} %read_ref.5, f32[256,128]{1,0:T(8,128)} %get-tuple-element.36.dt_ref), custom_call_target="tpu_custom_call" | custom-call | flops 268435456 | bytes 6291456 | tf_op jit(solution)/shard_map/mixer_grad/pallas_call | solution.py:93
  289.8 1.3 collective-permute-start.11
  291.1 2.3 collective-permute-start.10
  293.4 2.3 collective-permute-start.9
  295.8 1.9 collective-permute-start.8
  297.7 0.0 collective-permute-done.11.m4_ref
  297.7 0.4 collective-permute-done.10.m3_ref
  298.1 3.8 %collective-permute-done.9.m2_ref = f32[72,128]{1,0:T(8,128)S(1)} collective-permute-done((f32[72,128]{1,0:T(8,128)}, f32[72,128]{1,0:T(8,128)S(1)}, u32[]{:S(2)}, u32[]{:S(2)}) %collective-permute-start.9) | collective-permute-done | bytes 36896 | tf_op jit(solution)/shard_map/ppermute | solution.py:535
  301.9 2.0 collective-permute-done.8.m1_ref
  303.9 0.6 copy-done.13
  304.5 8.7 %mixer_backward.1 = bf16[64,4096]{1,0:T(8,128)(2,1)} custom-call(f32[72,128]{1,0:T(8,128)} %copy-done.13, f32[72,128]{1,0:T(8,128)} %copy-done.12, f32[72,128]{1,0:T(8,128)} %copy-done.11, f32[72,128]{1,0:T(8,128)} %copy-done.10, f32[256,128]{1,0:T(8,128)} %get-tuple-element.23.rt_ref, bf16[64,4096]{1,0:T(8,128)(2,1)} %get-tuple-element.38.grad_ref, ...), custom_call_target="tpu_custom_call" | custom-call | flops 268435456 | bytes 6291456 | tf_op jit(solution)/shard_map/mixer_backward/pallas_call | solution.py:93
  313.2 29.1 %all-to-all-done.3 = bf16[32,160,128]{2,1,0:T(8,128)(2,1)S(1)} async-done(((bf16[32,160,128]{2,1,0:T(8,128)(2,1)}), bf16[32,160,128]{2,1,0:T(8,128)(2,1)S(1)}, u32[]{:S(2)}, u32[]{:S(2)}) %all-to-all-start.3) | async-done | bytes 1310752 | tf_op jit(solution)/shard_map/all_to_all | solution.py:540
  342.3 1.1 copy-done
  343.4 4.9 %combine.1 = bf16[2048,128]{1,0:T(8,128)(2,1)} custom-call(f32[2,128]{1,0:T(2,128)} %copy-done.15, bf16[5120,128]{1,0:T(8,128)(2,1)} %bitcast.24), custom_call_target="tpu_custom_call" | custom-call | flops 167772160 | bytes 4194304 | tf_op jit(solution)/shard_map/combine/pallas_call | solution.py:93
  (29 shorter events, 0.1 us)
Async XLA Ops:
  7.2 112.9 %all-gather.3.cloned.1.call-start = ((), (), s32[]{:S(2)}) async-start(), calls=%async_computation.5 | async-start | bytes 3342336 | tf_op jit(solution)/shard_map/all_gather | solution.py:597
  7.9 173.0 %all-gather.5.cloned.1.call-start = ((), (), s32[]{:S(2)}) async-start(), calls=%async_computation.6 | async-start | bytes 6684672 | tf_op jit(solution)/shard_map/all_gather | solution.py:596
  8.6 22.6 %collective-permute-start.6 = (bf16[2048,128]{1,0:T(8,128)(2,1)}, bf16[2048,128]{1,0:T(8,128)(2,1)S(1)}, u32[]{:S(2)}, u32[]{:S(2)}) collective-permute-start(bf16[2048,128]{1,0:T(8,128)(2,1)} %own_ref.1), channel_id=1, source_target_pairs={{0,1},{1,0},{2,3},{3,2},{4,5},{5,4},{6,7},{7,6},{8,9},{9,8},{10,11... | collective-permute-start | bytes 1572872 | tf_op jit(solution)/shard_map/ppermute | solution.py:554
  11.3 20.0 %copy-start.15 = (f32[2,128]{1,0:T(2,128)}, f32[2,128]{1,0:T(2,128)S(1)}, u32[]{:S(2)}) copy-start(f32[2,128]{1,0:T(2,128)S(1)} %convert_bitcast_fusion.own_ids_ref.ids_ref) | copy-start | bytes 3076
  12.6 30.0 %all-to-all-start = ((f32[32,4,128]{2,1,0:T(4,128)}), f32[32,4,128]{2,1,0:T(4,128)S(1)}, u32[]{:S(2)}, u32[]{:S(2)}) async-start(f32[32,4,128]{2,1,0:T(4,128)} %broadcast_in_dim.2), calls=%async_computation | async-start | bytes 131072 | tf_op jit(solution)/shard_map/all_to_all | solution.py:575
  28.2 3.0 collective-permute-start.5
  31.2 0.5 copy-start.16
  31.2 0.8 copy-start.4
  42.6 6.8 %copy-start.14 = (f32[2,4096]{1,0:T(2,128)S(1)}, f32[2,4096]{1,0:T(2,128)}, u32[]{:S(2)}) copy-start(f32[2,4096]{1,0:T(2,128)} %param.14) | copy-start | bytes 98308
  42.6 67.8 %all-to-all-start.2 = ((bf16[16,320,128]{2,1,0:T(8,128)(2,1)}), bf16[16,320,128]{2,1,0:T(8,128)(2,1)S(1)}, u32[]{:S(2)}, u32[]{:S(2)}) async-start(bf16[16,320,128]{2,1,0:T(8,128)(2,1)} %bitcast.23), calls=%async_computation.2 | async-start | bytes 2621440 | tf_op jit(solution)/shard_map/all_to_all | solution.py:548
  54.1 15.0 %collective-permute-start.3 = (f32[72,128]{1,0:T(8,128)}, f32[72,128]{1,0:T(8,128)S(1)}, u32[]{:S(2)}, u32[]{:S(2)}) collective-permute-start(f32[72,128]{1,0:T(8,128)} %get-tuple-element.22), channel_id=1, source_target_pairs={{0,128},{32,160},{64,192},{96,224},{128,256},{160,288},{192,320},{... | collective-permute-start | bytes 110600 | tf_op jit(solution)/shard_map/ppermute | solution.py:535
  57.6 11.5 %collective-permute-start.2 = (f32[72,128]{1,0:T(8,128)}, f32[72,128]{1,0:T(8,128)S(1)}, u32[]{:S(2)}, u32[]{:S(2)}) collective-permute-start(f32[72,128]{1,0:T(8,128)} %get-tuple-element.22), channel_id=1, source_target_pairs={{0,96},{32,128},{64,160},{96,192},{128,224},{160,256},{192,288},{2... | collective-permute-start | bytes 110600 | tf_op jit(solution)/shard_map/ppermute | solution.py:535
  61.4 8.1 %collective-permute-start.1 = (f32[72,128]{1,0:T(8,128)}, f32[72,128]{1,0:T(8,128)S(1)}, u32[]{:S(2)}, u32[]{:S(2)}) collective-permute-start(f32[72,128]{1,0:T(8,128)} %get-tuple-element.22), channel_id=1, source_target_pairs={{0,64},{32,96},{64,128},{96,160},{128,192},{160,224},{192,256},{22... | collective-permute-start | bytes 110600 | tf_op jit(solution)/shard_map/ppermute | solution.py:535
  65.1 6.8 %collective-permute-start = (f32[72,128]{1,0:T(8,128)}, f32[72,128]{1,0:T(8,128)S(1)}, u32[]{:S(2)}, u32[]{:S(2)}) collective-permute-start(f32[72,128]{1,0:T(8,128)} %get-tuple-element.22), channel_id=1, source_target_pairs={{0,32},{32,64},{64,96},{96,128},{128,160},{160,192},{192,224},{224... | collective-permute-start | bytes 110600 | tf_op jit(solution)/shard_map/ppermute | solution.py:535
  69.1 2.8 copy-start.6
  69.2 2.8 copy-start.7
  69.5 2.5 copy-start.8
  71.9 0.6 copy-start.9
  83.5 4.0 %collective-permute-start.4 = (bf16[64,4096]{1,0:T(8,128)(2,1)}, bf16[64,4096]{1,0:T(8,128)(2,1)S(1)}, u32[]{:S(2)}, u32[]{:S(2)}) collective-permute-start(bf16[64,4096]{1,0:T(8,128)(2,1)} %get-tuple-element.24.own_ref), channel_id=1, source_target_pairs={{0,1},{1,0},{2,3},{3,2},{4,5},{5,4},{6,7},{7,6},{8,9},{9,8},{10,11... | collective-permute-start | bytes 1572872 | tf_op jit(solution)/shard_map/ppermute | solution.py:554
  87.5 0.8 copy-start.17
  110.4 1.1 copy-start.2
  111.5 69.3 %all-to-all-start.1 = ((bf16[16,320,128]{2,1,0:T(8,128)(2,1)}), bf16[16,320,128]{2,1,0:T(8,128)(2,1)S(1)}, u32[]{:S(2)}, u32[]{:S(2)}) async-start(bf16[16,320,128]{2,1,0:T(8,128)(2,1)} %bitcast.28), calls=%async_computation.1 | async-start | bytes 2621440 | tf_op jit(solution)/shard_map/all_to_all | solution.py:548
  180.9 1.1 copy-start.3
  196.1 71.7 %all-to-all-start.4 = ((bf16[16,320,128]{2,1,0:T(8,128)(2,1)}), bf16[16,320,128]{2,1,0:T(8,128)(2,1)S(1)}, u32[]{:S(2)}, u32[]{:S(2)}) async-start(bf16[16,320,128]{2,1,0:T(8,128)(2,1)} %bitcast.30), calls=%async_computation.4 | async-start | bytes 2621440 | tf_op jit(solution)/shard_map/all_to_all | solution.py:548
  267.7 1.1 copy-start.1
  268.8 73.5 %all-to-all-start.3 = ((bf16[32,160,128]{2,1,0:T(8,128)(2,1)}), bf16[32,160,128]{2,1,0:T(8,128)(2,1)S(1)}, u32[]{:S(2)}, u32[]{:S(2)}) async-start(bf16[32,160,128]{2,1,0:T(8,128)(2,1)} %bitcast.27), calls=%async_computation.3 | async-start | bytes 2621440 | tf_op jit(solution)/shard_map/all_to_all | solution.py:540
  280.9 4.0 %collective-permute-start.7 = (bf16[64,4096]{1,0:T(8,128)(2,1)}, bf16[64,4096]{1,0:T(8,128)(2,1)S(1)}, u32[]{:S(2)}, u32[]{:S(2)}) collective-permute-start(bf16[64,4096]{1,0:T(8,128)(2,1)} %get-tuple-element.35), channel_id=1, source_target_pairs={{0,1},{1,0},{2,3},{3,2},{4,5},{5,4},{6,7},{7,6},{8,9},{9,8},{10,11... | collective-permute-start | bytes 1572872 | tf_op jit(solution)/shard_map/ppermute | solution.py:554
  284.9 0.8 copy-start.5
  289.8 7.8 %collective-permute-start.11 = (f32[72,128]{1,0:T(8,128)}, f32[72,128]{1,0:T(8,128)S(1)}, u32[]{:S(2)}, u32[]{:S(2)}) collective-permute-start(f32[72,128]{1,0:T(8,128)} %get-tuple-element.37), channel_id=1, source_target_pairs={{128,0},{160,32},{192,64},{224,96},{256,128},{288,160},{320,192},{... | collective-permute-start | bytes 110600 | tf_op jit(solution)/shard_map/ppermute | solution.py:535
  291.1 7.0 %collective-permute-start.10 = (f32[72,128]{1,0:T(8,128)}, f32[72,128]{1,0:T(8,128)S(1)}, u32[]{:S(2)}, u32[]{:S(2)}) collective-permute-start(f32[72,128]{1,0:T(8,128)} %get-tuple-element.37), channel_id=1, source_target_pairs={{96,0},{128,32},{160,64},{192,96},{224,128},{256,160},{288,192},{3... | collective-permute-start | bytes 110600 | tf_op jit(solution)/shard_map/ppermute | solution.py:535
  293.4 8.5 %collective-permute-start.9 = (f32[72,128]{1,0:T(8,128)}, f32[72,128]{1,0:T(8,128)S(1)}, u32[]{:S(2)}, u32[]{:S(2)}) collective-permute-start(f32[72,128]{1,0:T(8,128)} %get-tuple-element.37), channel_id=1, source_target_pairs={{64,0},{96,32},{128,64},{160,96},{192,128},{224,160},{256,192},{28... | collective-permute-start | bytes 110600 | tf_op jit(solution)/shard_map/ppermute | solution.py:535
  295.8 8.2 %collective-permute-start.8 = (f32[72,128]{1,0:T(8,128)}, f32[72,128]{1,0:T(8,128)S(1)}, u32[]{:S(2)}, u32[]{:S(2)}) collective-permute-start(f32[72,128]{1,0:T(8,128)} %get-tuple-element.37), channel_id=1, source_target_pairs={{32,0},{64,32},{96,64},{128,96},{160,128},{192,160},{224,192},{256... | collective-permute-start | bytes 110600 | tf_op jit(solution)/shard_map/ppermute | solution.py:535
  297.7 6.2 %copy-start.10 = (f32[72,128]{1,0:T(8,128)}, f32[72,128]{1,0:T(8,128)S(1)}, u32[]{:S(2)}) copy-start(f32[72,128]{1,0:T(8,128)S(1)} %collective-permute-done.11.m4_ref) | copy-start | bytes 110596
  298.1 5.8 %copy-start.11 = (f32[72,128]{1,0:T(8,128)}, f32[72,128]{1,0:T(8,128)S(1)}, u32[]{:S(2)}) copy-start(f32[72,128]{1,0:T(8,128)S(1)} %collective-permute-done.10.m3_ref) | copy-start | bytes 110596
  301.9 2.0 copy-start.12
  303.9 0.6 copy-start.13
  342.3 1.1 copy-start
Sparse Core Ops, SparseCore 0:
  11.0 68.0 all-gather.2
  82.1 76.7 all-gather.4

commit v4 on v3

--- a/solution.py
+++ b/solution.py
@@ -25,7 +25,10 @@
 FF = 768
 FBLOCKS = WIDTH // LANES
 REACH = 4
+EARLY = 14
+STEPS = (0, 8, 7, 9, 6, 10, 5, 11, 4, 12, 3, 13, 2, 14, 1, 15)
 VMEM = 60 * 1024 * 1024
+VMEM_PART = 40 * 1024 * 1024
 
 LAST = (((1,), (1,)), ((), ()))
 FIRST = (((0,), (0,)), ((), ()))
@@ -88,7 +91,19 @@
     lax.fori_loop(0, ROWS // BLOCK, step, 0, unroll=4)
 
 
-def call(kernel, outs, args, in_specs, scratch=(), flops=0, moved=0, name=None):
+def send_rows(out_refs, wide_ref, chip):
+    for d, ref in zip(STEPS, out_refs):
+        at = pl.multiple_of(lax.rem(chip + d, CHIPS) * SLOTS, SLOTS)
+        ref[...] = wide_ref[pl.ds(at, SLOTS), :].astype(ref.dtype)
+
+
+def take_rows(wide_ref, in_refs, chip):
+    for d, ref in zip(STEPS, in_refs):
+        at = pl.multiple_of(lax.rem(chip + CHIPS - d, CHIPS) * SLOTS, SLOTS)
+        wide_ref[pl.ds(at, SLOTS), :] = ref[...].astype(wide_ref.dtype)
+
+
+def call(kernel, outs, args, in_specs, scratch=(), flops=0, moved=0, name=None, vmem=VMEM):
     vm = pl.BlockSpec(memory_space=pltpu.VMEM)
     return pl.pallas_call(
         kernel,
@@ -96,7 +111,7 @@
         in_specs=in_specs,
         out_specs=tuple(vm for _ in outs),
         scratch_shapes=list(scratch),
-        compiler_params=pltpu.CompilerParams(vmem_limit_bytes=VMEM),
+        compiler_params=pltpu.CompilerParams(vmem_limit_bytes=vmem),
         cost_estimate=pl.CostEstimate(flops=flops, bytes_accessed=moved, transcendentals=0),
         name=name,
     )(*args)
@@ -107,8 +122,8 @@
 HBM = pl.BlockSpec(memory_space=pl.ANY)
 
 
-def grad_rows_kernel(core_ref, own_ids_ref, their_ids_ref, own_ref, their_ref, out_ref, wide_ref):
-    core = core_ref[0]
+def grad_rows_kernel(expert_ref, own_ids_ref, their_ids_ref, own_ref, their_ref, out_ref, wide_ref):
+    core = lax.rem(expert_ref[0], 2)
     earlier = earlier_mask()
 
     def select_of(ids_ref):
@@ -258,9 +273,9 @@
     lax.fori_loop(0, CHUNKS, step, chained((m1_ref, m2_ref, m3_ref, m4_ref)), unroll=4)
 
 
-def dispatch_kernel(
-    expert_ref, own_ref, their_ref, ids_ref, msg_ref, rank_ref, weight_ref, first_ref, wide_ref
-):
+def dispatch_kernel(expert_ref, own_ref, their_ref, ids_ref, *refs):
+    out_refs = refs[:CHIPS]
+    rank_ref, weight_ref, first_ref, wide_ref = refs[CHIPS:]
     core = lax.rem(expert_ref[0], 2)
     earlier = earlier_mask()
     mine = expert_ref[0].astype(f32)
@@ -301,7 +316,7 @@
         return carry
 
     lax.fori_loop(0, PAIRS, step, 0, unroll=2)
-    round_rows(msg_ref, wide_ref)
+    send_rows(out_refs, wide_ref, lax.div(expert_ref[0], 2))
 
 
 def arrived_grad_kernel(
@@ -336,32 +351,20 @@
     lax.fori_loop(0, FF // 256, matmul, 0)
 
 
-def expert_kernel(
-    rows_ref,
-    gain_ref,
-    first_ref,
-    grad_ref,
-    dhid_ref,
-    in_hbm,
-    msg_ref,
-    normed_ref,
-    hidden_ref,
-    y_ref,
-    scaled_ref,
-    dcat_ref,
-    in_ref,
-    sem,
-):
+def expert_kernel(expert_ref, *refs):
+    rows_refs = refs[:CHIPS]
+    gain_ref, first_ref, grad_ref, dhid_ref, in_hbm = refs[CHIPS : CHIPS + 5]
+    out_refs = refs[CHIPS + 5 : 2 * CHIPS + 5]
+    normed_ref, hidden_ref, y_ref, scaled_ref, dcat_ref, in_ref, sem = refs[2 * CHIPS + 5 :]
+    chip = lax.div(expert_ref[0], 2)
     fetch = pltpu.make_async_copy(in_hbm, in_ref, sem)
     fetch.start()
-
-    def unpack(k, squares):
-        lanes = pl.ds(pl.multiple_of(k * LANES, LANES), LANES)
-        y = rows_ref[pl.ds(pl.multiple_of(k * SLOTS, SLOTS), SLOTS), :].astype(f32)
-        y_ref[:, lanes] = y
-        return squares + y * y
-
-    squares = lax.fori_loop(0, FBLOCKS, unpack, jnp.zeros((SLOTS, LANES), f32), unroll=2)
+    squares = jnp.zeros((SLOTS, LANES), f32)
+    for d, rows_ref in zip(STEPS, rows_refs):
+        at = pl.multiple_of(lax.rem(chip + CHIPS - d, CHIPS) * LANES, LANES)
+        y = rows_ref[...].astype(f32)
+        y_ref[:, pl.ds(at, LANES)] = y
+        squares = squares + y * y
     mean = jnp.sum(squares, axis=1, keepdims=True) * (1.0 / WIDTH)
     rscale = lax.rsqrt(mean + 1e-06)
     rscale_b = jnp.broadcast_to(rscale, (SLOTS, LANES))
@@ -404,13 +407,10 @@
     mean_grad = jnp.sum(acc, axis=1, keepdims=True) * (1.0 / WIDTH)
     pull = jnp.broadcast_to(rscale * rscale * rscale * mean_grad, (SLOTS, LANES))
 
-    def pack(k, carry):
-        lanes = pl.ds(pl.multiple_of(k * LANES, LANES), LANES)
+    for d, out_ref in zip(STEPS, out_refs):
+        lanes = pl.ds(pl.multiple_of(lax.rem(chip + d, CHIPS) * LANES, LANES), LANES)
         part = rscale_b * scaled_ref[:, lanes] - pull * y_ref[:, lanes]
-        msg_ref[pl.ds(pl.multiple_of(k * SLOTS, SLOTS), SLOTS), :] = part.astype(bf16)
-        return carry
-
-    lax.fori_loop(0, FBLOCKS, pack, 0, unroll=4)
+        out_ref[...] = part.astype(bf16)
 
 
 def expert_out_kernel(
@@ -462,9 +462,11 @@
     lax.fori_loop(0, FBLOCKS, step, 0, unroll=4)
 
 
-def slot_sums_kernel(core_ref, rows_ref, rank_ref, own_ref, their_ref, wide_ref):
-    round_rows(wide_ref, rows_ref)
-    core = core_ref[0]
+def slot_sums_kernel(expert_ref, *refs):
+    in_refs = refs[:CHIPS]
+    rank_ref, own_ref, their_ref, wide_ref = refs[CHIPS:]
+    take_rows(wide_ref, in_refs, lax.div(expert_ref[0], 2))
+    core = lax.rem(expert_ref[0], 2)
 
     def step(jp, carry):
         for par in range(2):
@@ -550,6 +552,14 @@
     ).reshape(ROWS, LANES)
 
 
+def shifted(blocks):
+    moved = [blocks[0]]
+    for d, block in zip(STEPS[1:], blocks[1:]):
+        pairs = [(i, (i + 2 * d) % EXPERTS) for i in range(EXPERTS)]
+        moved.append(lax.ppermute(block, "exp", pairs))
+    return moved
+
+
 def from_other_core(value):
     return lax.ppermute(value, "exp", [(i, i ^ 1) for i in range(EXPERTS)])
 
@@ -577,14 +587,15 @@
     )
     tokens = tokens.reshape(PAIRS, 2, 4, LANES).transpose(2, 1, 0, 3).reshape(4, CHUNKS, LANES)
 
-    me_core = lax.rem(me_exp, 2).astype(i32).reshape(1)
+    me = me_exp.astype(i32).reshape(1)
+    parts = [((SLOTS, LANES), bf16)] * CHIPS
 
     their_ids = from_other_core(ids_own)
     their_grad = from_other_core(out_grad)
     (grad_out_rows,) = call(
         grad_rows_kernel,
         [((ROWS, LANES), bf16)],
-        (me_core, ids_own, their_ids, out_grad, their_grad),
+        (me, ids_own, their_ids, out_grad, their_grad),
         [SM] + [VM] * 4,
         [wide],
         flops=2 * SLOTS * LANES * WIDTH,
@@ -621,22 +632,22 @@
         name="mixer_forward",
     )
     y_their = from_other_core(y_own)
-    y_out_rows, ranks, slot_weight, slot_first = call(
+    *y_out_rows, ranks, slot_weight, slot_first = call(
         dispatch_kernel,
         [
-            ((ROWS, LANES), bf16),
+            *parts,
             ((CHUNKS * CHIPS, LANES), f32),
             ((SLOTS, LANES), f32),
             ((SLOTS, LANES), f32),
         ],
-        (me_exp.astype(i32).reshape(1), y_own, y_their, tokens),
+        (me, y_own, y_their, tokens),
         [SM] + [VM] * 3,
         [wide],
         flops=4 * HP * SLOTS * SEQ,
         moved=4 << 20,
         name="dispatch",
     )
-    y_in_rows = exchanged_by_core(y_out_rows)
+    y_in_rows = shifted(y_out_rows)
 
     grad_slots, d_hidden = call(
         arrived_grad_kernel,
@@ -648,15 +659,23 @@
         moved=8 << 20,
         name="hidden_grad",
     )
-    back_out_rows, normed, hidden = call(
+    *back_out_rows, normed, hidden = call(
         expert_kernel,
         [
-            ((ROWS, LANES), bf16),
+            *parts,
             ((SLOTS, WIDTH), bf16),
             ((SLOTS, FF), bf16),
         ],
-        (y_in_rows, norm_gain.reshape(1, WIDTH), slot_first, grad_slots, d_hidden, weight_in),
-        [VM, VM, VM, VM, VM, HBM],
+        (
+            me,
+            *y_in_rows,
+            norm_gain.reshape(1, WIDTH),
+            slot_first,
+            grad_slots,
+            d_hidden,
+            weight_in,
+        ),
+        [SM] + [VM] * (CHIPS + 4) + [HBM],
         [
             pltpu.VMEM((SLOTS, WIDTH), f32),
             pltpu.VMEM((SLOTS, WIDTH), f32),
@@ -667,8 +686,9 @@
         flops=8 * SLOTS * FF * WIDTH,
         moved=14 << 20,
         name="expert",
-    )
-    back_in_rows = exchanged_by_core(back_out_rows)
+        vmem=VMEM_PART,
+    )
+    back_in_rows = shifted(back_out_rows)
 
     (result_rows,) = call(
         expert_out_kernel,
@@ -680,17 +700,23 @@
         moved=8 << 20,
         name="expert_out",
     )
+    early = slice(1, 1 + EARLY)
+    result_rows, *first_in = lax.optimization_barrier(
+        (result_rows, *back_in_rows[early])
+    )
+    back_in_rows[early] = first_in
     returned_rows = exchanged(result_rows)
 
     own_sums, their_sums = call(
         slot_sums_kernel,
         [((HP, SEQ), f32), ((HP, SEQ), bf16)],
-        (me_core, back_in_rows, ranks),
-        [SM, VM, VM],
+        (me, *back_in_rows, ranks),
+        [SM] + [VM] * (CHIPS + 1),
         [wide],
         flops=4 * HP * SLOTS * SEQ,
         moved=4 << 20,
         name="slot_sums",
+        vmem=VMEM_PART,
     )
     y_grad, back_message = call(
         grad_kernel,

time: 357 us -> 413 us (1.16)
  starting transfers between devices: 76.7 us -> 225 us
  waiting for transfers between devices: 172 us -> 77 us
  Pallas kernels: 81.3 us -> 73.6 us
  local copies, waits for them, and re-layouts: 9.88 us -> 15.7 us
    ppermute x0 -> x30, starting transfers between devices: none -> 159 us  [shifted(): moved.append(lax.ppermute(block, 'exp', pairs))]
    all_to_all x3 -> x1, waiting for transfers between devices: 123 us -> 0.01 us  [exchanged_by_core(): lax.all_to_all(blocks, 'exp', split_axis=0, concat_axis=0, tiled=True, ax...]
    ppermute x0 -> x30, waiting for transfers between devices: none -> 57.4 us  [shifted(): moved.append(lax.ppermute(block, 'exp', pairs))]
    all_to_all x1, waiting for transfers between devices: 29.1 us -> 0.01 us  [exchanged(): lax.all_to_all(blocks, 'exp', split_axis=0, concat_axis=0, tiled=True)]
    all_to_all x3 -> x1, starting transfers between devices: 23.8 us -> 6.75 us  [exchanged_by_core(): lax.all_to_all(blocks, 'exp', split_axis=0, concat_axis=0, tiled=True, ax...]
    pallas_call x11, Pallas kernels: 81.3 us -> 73.6 us  [call(): pl.pallas_call(kernel, out_shape=tuple((jax.ShapeDtypeStruct(shape, kind)...]
    unnamed x36 -> x52, local copies, waits for them, and re-layouts: 7.95 us -> 13.8 us
    all_to_all x1, starting transfers between devices: 6.37 us -> 12.2 us  [exchanged(): lax.all_to_all(blocks, 'exp', split_axis=0, concat_axis=0, tiled=True)]
  transfers between devices with their start and end apart: 19 -> 47, of which waited for: 13 -> 11; matrix products, arithmetic and copies ran while one was open for 1% -> 1% of each run, Pallas kernels for 18% -> 15%
where the time goes in v4:
time: 413 us; the launch traced here: 408 us
  starting transfers between devices  225 us (54%)
  waiting for transfers between devices  77 us (19%)
  Pallas kernels  73.6 us (18%)
  local copies, waits for them, and re-layouts  15.7 us (4%)
  between operations  14.8 us (4%)
    ppermute x30, starting transfers between devices, shifted(): moved.append(lax.ppermute(block, 'exp', pairs))  159 us
    pallas_call x11, Pallas kernels, call(): pl.pallas_call(kernel, out_shape=tuple((jax.ShapeDtypeStruct(shape, kind)...  73.6 us
    ppermute x30, waiting for transfers between devices, shifted(): moved.append(lax.ppermute(block, 'exp', pairs))  57.4 us
    ppermute x8, starting transfers between devices, sent_along(): return lax.ppermute(value, 'ctx', pairs)  23.6 us
    all_to_all x1, starting transfers between devices, per_device(): lax.all_to_all(jnp.broadcast_to(tokens_own[None], (EXPERTS, 4, LANES)), '...  15.6 us
    unnamed x52, local copies, waits for them, and re-layouts  13.8 us
    all_to_all x1, starting transfers between devices, exchanged(): lax.all_to_all(blocks, 'exp', split_axis=0, concat_axis=0, tiled=True)  12.2 us
    ppermute x8, waiting for transfers between devices, sent_along(): return lax.ppermute(value, 'ctx', pairs)  8.78 us
  transfers between devices with their start and end apart: 47, of which 11 were waited for; matrix products, arithmetic and copies ran while one was open for 1% of the time, Pallas kernels for 15%

profile of v4, /device:TPU:6, one launch (start us, length us, event | category | flops | bytes accessed | tf_op | source)
XLA Modules:
  0.0 407.7 jit_solution(7359023719935329280)
XLA Ops:
  8.6 1.9 collective-permute-start.21
  12.6 15.6 %all-to-all-start = ((f32[32,4,128]{2,1,0:T(4,128)}), f32[32,4,128]{2,1,0:T(4,128)S(1)}, u32[]{:S(2)}, u32[]{:S(2)}) async-start(f32[32,4,128]{2,1,0:T(4,128)} %broadcast_in_dim.2), calls=%async_computation | async-start | bytes 131072 | tf_op jit(solution)/shard_map/all_to_all | solution.py:585
  28.2 2.2 collective-permute-start.20
  32.0 5.3 %grad_rows.1 = bf16[5120,128]{1,0:T(8,128)(2,1)} custom-call(s32[1]{0:T(128)} %bitcast.1.expert_ref, f32[2,128]{1,0:T(2,128)} %copy-done.23, f32[2,128]{1,0:T(2,128)} %copy-done.24, bf16[2048,128]{1,0:T(8,128)(2,1)} %own_ref.1, bf16[2048,128]{1,0:T(8,128)(2,1)} %copy-done.12), custom_call_target="tpu_custom_call" | custom-call | flops 167772160 | bytes 4194304 | tf_op jit(solution)/shard_map/grad_rows/pallas_call | solution.py:108
  37.3 5.3 %all-to-all-done = f32[32,4,128]{2,1,0:T(4,128)S(1)} async-done(((f32[32,4,128]{2,1,0:T(4,128)}), f32[32,4,128]{2,1,0:T(4,128)S(1)}, u32[]{:S(2)}, u32[]{:S(2)}) %all-to-all-start) | async-done | bytes 65568 | tf_op jit(solution)/shard_map/all_to_all | solution.py:585
  42.6 6.7 %all-to-all-start.1 = ((bf16[16,320,128]{2,1,0:T(8,128)(2,1)}), bf16[16,320,128]{2,1,0:T(8,128)(2,1)S(1)}, u32[]{:S(2)}, u32[]{:S(2)}) async-start(bf16[16,320,128]{2,1,0:T(8,128)(2,1)} %bitcast.20), calls=%async_computation.1 | async-start | bytes 2621440 | tf_op jit(solution)/shard_map/all_to_all | solution.py:550
  50.0 4.1 shard_state.1
  54.1 3.5 collective-permute-start.3
  57.6 3.8 collective-permute-start.2
  61.3 3.7 collective-permute-start.1
  65.1 4.0 collective-permute-start
  69.3 2.6 collective-permute-done.m1_ref
  72.5 11.0 %mixer_forward.1 = (bf16[64,4096]{1,0:T(8,128)(2,1)}, bf16[8192,128]{1,0:T(8,128)(2,1)}) custom-call(f32[72,128]{1,0:T(8,128)} %copy-done.17, f32[72,128]{1,0:T(8,128)} %copy-done.16, f32[72,128]{1,0:T(8,128)} %copy-done.15, f32[72,128]{1,0:T(8,128)} %copy-done.14, f32[256,128]{1,0:T(8,128)} %get-tuple-element.68.rt_ref, bf16[64,4096]{1,0:T(8,128)(2,1)} %x_ref.3, ...), custom_call_target="tpu_custom_call" | custom-call | flops 268435456 | bytes 9437184 | tf_op jit(solution)/shard_map/mixer_forward/pallas_call | solution.py:108
  83.5 1.9 collective-permute-start.4
  86.1 1.4 collective-permute-done.4.their_ref
  88.3 8.3 %dispatch.1 = (bf16[320,128]{1,0:T(8,128)(2,1)}, bf16[320,128]{1,0:T(8,128)(2,1)}, bf16[320,128]{1,0:T(8,128)(2,1)}, bf16[320,128]{1,0:T(8,128)(2,1)}, bf16[320,...) custom-call(s32[1]{0:T(128)} %bitcast.1.expert_ref, ...), custom_call_target="tpu_custom_call" | custom-call | flops 335544320 | bytes 4194304 | tf_op jit(solution)/shard_map/dispatch/pallas_call | solution.py:108
  96.6 12.5 %collective-permute-start.5 = (bf16[320,128]{1,0:T(8,128)(2,1)}, bf16[320,128]{1,0:T(8,128)(2,1)S(1)}, u32[]{:S(2)}, u32[]{:S(2)}) collective-permute-start(bf16[320,128]{1,0:T(8,128)(2,1)} %get-tuple-element.71), channel_id=1, source_target_pairs={{0,16},{1,17},{2,18},{3,19},{4,20},{5,21},{6,22},{7,23},{8,24},{9,... | collective-permute-start | bytes 245768 | tf_op jit(solution)/shard_map/ppermute | solution.py:559
  109.1 2.2 collective-permute-start.6
  111.3 11.5 %collective-permute-start.7 = (bf16[320,128]{1,0:T(8,128)(2,1)}, bf16[320,128]{1,0:T(8,128)(2,1)S(1)}, u32[]{:S(2)}, u32[]{:S(2)}) collective-permute-start(bf16[320,128]{1,0:T(8,128)(2,1)} %get-tuple-element.73), channel_id=1, source_target_pairs={{0,18},{1,19},{2,20},{3,21},{4,22},{5,23},{6,24},{7,25},{8,26},{9,... | collective-permute-start | bytes 245768 | tf_op jit(solution)/shard_map/ppermute | solution.py:559
  122.8 2.2 collective-permute-start.8
  125.0 10.6 %collective-permute-start.9 = (bf16[320,128]{1,0:T(8,128)(2,1)}, bf16[320,128]{1,0:T(8,128)(2,1)S(1)}, u32[]{:S(2)}, u32[]{:S(2)}) collective-permute-start(bf16[320,128]{1,0:T(8,128)(2,1)} %get-tuple-element.75), channel_id=1, source_target_pairs={{0,20},{1,21},{2,22},{3,23},{4,24},{5,25},{6,26},{7,27},{8,28},{9,... | collective-permute-start | bytes 245768 | tf_op jit(solution)/shard_map/ppermute | solution.py:559
  135.6 1.7 collective-permute-done.5.refs_1_
  137.3 1.9 collective-permute-start.10
  139.2 9.9 %collective-permute-start.11 = (bf16[320,128]{1,0:T(8,128)(2,1)}, bf16[320,128]{1,0:T(8,128)(2,1)S(1)}, u32[]{:S(2)}, u32[]{:S(2)}) collective-permute-start(bf16[320,128]{1,0:T(8,128)(2,1)} %get-tuple-element.77), channel_id=1, source_target_pairs={{0,22},{1,23},{2,24},{3,25},{4,26},{5,27},{6,28},{7,29},{8,30},{9,... | collective-permute-start | bytes 245768 | tf_op jit(solution)/shard_map/ppermute | solution.py:559
  149.1 2.4 collective-permute-start.12
  151.6 7.3 %collective-permute-start.13 = (bf16[320,128]{1,0:T(8,128)(2,1)}, bf16[320,128]{1,0:T(8,128)(2,1)S(1)}, u32[]{:S(2)}, u32[]{:S(2)}) collective-permute-start(bf16[320,128]{1,0:T(8,128)(2,1)} %get-tuple-element.79), channel_id=1, source_target_pairs={{0,24},{1,25},{2,26},{3,27},{4,28},{5,29},{6,30},{7,31},{8,0},{9,1... | collective-permute-start | bytes 245768 | tf_op jit(solution)/shard_map/ppermute | solution.py:559
  158.9 1.9 collective-permute-start.14
  160.9 6.9 %collective-permute-start.15 = (bf16[320,128]{1,0:T(8,128)(2,1)}, bf16[320,128]{1,0:T(8,128)(2,1)S(1)}, u32[]{:S(2)}, u32[]{:S(2)}) collective-permute-start(bf16[320,128]{1,0:T(8,128)(2,1)} %get-tuple-element.81), channel_id=1, source_target_pairs={{0,26},{1,27},{2,28},{3,29},{4,30},{5,31},{6,0},{7,1},{8,2},{9,3},... | collective-permute-start | bytes 245768 | tf_op jit(solution)/shard_map/ppermute | solution.py:559
  167.8 1.9 collective-permute-start.16
  169.8 6.0 %collective-permute-start.17 = (bf16[320,128]{1,0:T(8,128)(2,1)}, bf16[320,128]{1,0:T(8,128)(2,1)S(1)}, u32[]{:S(2)}, u32[]{:S(2)}) collective-permute-start(bf16[320,128]{1,0:T(8,128)(2,1)} %get-tuple-element.83), channel_id=1, source_target_pairs={{0,28},{1,29},{2,30},{3,31},{4,0},{5,1},{6,2},{7,3},{8,4},{9,5},{1... | collective-permute-start | bytes 245768 | tf_op jit(solution)/shard_map/ppermute | solution.py:559
  175.8 1.9 collective-permute-start.18
  177.7 5.1 %collective-permute-start.19 = (bf16[320,128]{1,0:T(8,128)(2,1)}, bf16[320,128]{1,0:T(8,128)(2,1)S(1)}, u32[]{:S(2)}, u32[]{:S(2)}) collective-permute-start(bf16[320,128]{1,0:T(8,128)(2,1)} %get-tuple-element.85), channel_id=1, source_target_pairs={{0,30},{1,31},{2,0},{3,1},{4,2},{5,3},{6,4},{7,5},{8,6},{9,7},{10,... | collective-permute-start | bytes 245768 | tf_op jit(solution)/shard_map/ppermute | solution.py:559
  184.0 5.9 %hidden_grad.1 = (bf16[320,2048]{1,0:T(8,128)(2,1)}, f32[320,768]{1,0:T(8,128)}) custom-call(bf16[5120,128]{1,0:T(8,128)(2,1)} %bitcast.22, f32[320,128]{1,0:T(8,128)} %get-tuple-element.87.weight_ref, bf16[2048,768]{1,0:T(8,128)(2,1)} %bitcast.18), custom_call_target="tpu_custom_call" | custom-call | flops 1006632960 | bytes 8388608 | tf_op jit(solution)/shard_map/hidden_grad/pallas_call | solution.py:108
  190.0 2.8 copy-done.5
  195.3 8.9 %expert.1 = (bf16[320,128]{1,0:T(8,128)(2,1)S(1)}, bf16[320,128]{1,0:T(8,128)(2,1)S(1)}, bf16[320,128]{1,0:T(8,128)(2,1)S(1)}, bf16[320,128]{1,0:T(8,128)(2,1)S(...) custom-call(s32[1]{0:T(128)} %bitcast.1.expert_ref, ...), custom_call_target="tpu_custom_call" | custom-call | flops 4026531840 | bytes 14680064 | tf_op jit(solution)/shard_map/expert/pallas_call | solution.py:108
  206.0 1.9 collective-permute-start.22
  207.9 10.0 %collective-permute-start.23 = (bf16[320,128]{1,0:T(8,128)(2,1)S(1)}, bf16[320,128]{1,0:T(8,128)(2,1)S(1)}, u32[]{:S(2)}, u32[]{:S(2)}) collective-permute-start(bf16[320,128]{1,0:T(8,128)(2,1)S(1)} %get-tuple-element.93), channel_id=1, source_target_pairs={{0,14},{1,15},{2,16},{3,17},{4,18},{5,19},{6,20},{7,21},{8,22},{9,... | collective-permute-start | bytes 245768 | tf_op jit(solution)/shard_map/ppermute | solution.py:559
  217.9 3.7 collective-permute-start.24
  221.6 7.9 %collective-permute-start.25 = (bf16[320,128]{1,0:T(8,128)(2,1)S(1)}, bf16[320,128]{1,0:T(8,128)(2,1)S(1)}, u32[]{:S(2)}, u32[]{:S(2)}) collective-permute-start(bf16[320,128]{1,0:T(8,128)(2,1)S(1)} %get-tuple-element.95), channel_id=1, source_target_pairs={{0,12},{1,13},{2,14},{3,15},{4,16},{5,17},{6,18},{7,19},{8,20},{9,... | collective-permute-start | bytes 245768 | tf_op jit(solution)/shard_map/ppermute | solution.py:559
  229.4 4.9 %collective-permute-start.26 = (bf16[320,128]{1,0:T(8,128)(2,1)S(1)}, bf16[320,128]{1,0:T(8,128)(2,1)S(1)}, u32[]{:S(2)}, u32[]{:S(2)}) collective-permute-start(bf16[320,128]{1,0:T(8,128)(2,1)S(1)} %get-tuple-element.96), channel_id=1, source_target_pairs={{0,20},{1,21},{2,22},{3,23},{4,24},{5,25},{6,26},{7,27},{8,28},{9,... | collective-permute-start | bytes 245768 | tf_op jit(solution)/shard_map/ppermute | solution.py:559
  234.4 7.0 %collective-permute-start.27 = (bf16[320,128]{1,0:T(8,128)(2,1)S(1)}, bf16[320,128]{1,0:T(8,128)(2,1)S(1)}, u32[]{:S(2)}, u32[]{:S(2)}) collective-permute-start(bf16[320,128]{1,0:T(8,128)(2,1)S(1)} %get-tuple-element.97), channel_id=1, source_target_pairs={{0,10},{1,11},{2,12},{3,13},{4,14},{5,15},{6,16},{7,17},{8,18},{9,... | collective-permute-start | bytes 245768 | tf_op jit(solution)/shard_map/ppermute | solution.py:559
  241.4 4.9 %collective-permute-start.28 = (bf16[320,128]{1,0:T(8,128)(2,1)S(1)}, bf16[320,128]{1,0:T(8,128)(2,1)S(1)}, u32[]{:S(2)}, u32[]{:S(2)}) collective-permute-start(bf16[320,128]{1,0:T(8,128)(2,1)S(1)} %get-tuple-element.98), channel_id=1, source_target_pairs={{0,22},{1,23},{2,24},{3,25},{4,26},{5,27},{6,28},{7,29},{8,30},{9,... | collective-permute-start | bytes 245768 | tf_op jit(solution)/shard_map/ppermute | solution.py:559
  246.3 7.3 %collective-permute-start.29 = (bf16[320,128]{1,0:T(8,128)(2,1)S(1)}, bf16[320,128]{1,0:T(8,128)(2,1)S(1)}, u32[]{:S(2)}, u32[]{:S(2)}) collective-permute-start(bf16[320,128]{1,0:T(8,128)(2,1)S(1)} %get-tuple-element.99), channel_id=1, source_target_pairs={{0,8},{1,9},{2,10},{3,11},{4,12},{5,13},{6,14},{7,15},{8,16},{9,17... | collective-permute-start | bytes 245768 | tf_op jit(solution)/shard_map/ppermute | solution.py:559
  253.6 2.5 collective-permute-start.30
  256.0 5.2 %collective-permute-start.31 = (bf16[320,128]{1,0:T(8,128)(2,1)S(1)}, bf16[320,128]{1,0:T(8,128)(2,1)S(1)}, u32[]{:S(2)}, u32[]{:S(2)}) collective-permute-start(bf16[320,128]{1,0:T(8,128)(2,1)S(1)} %get-tuple-element.101), channel_id=1, source_target_pairs={{0,6},{1,7},{2,8},{3,9},{4,10},{5,11},{6,12},{7,13},{8,14},{9,15},... | collective-permute-start | bytes 245768 | tf_op jit(solution)/shard_map/ppermute | solution.py:559
  261.2 3.7 collective-permute-start.32
  264.9 3.8 collective-permute-start.33
  268.8 4.1 %collective-permute-start.34 = (bf16[320,128]{1,0:T(8,128)(2,1)S(1)}, bf16[320,128]{1,0:T(8,128)(2,1)S(1)}, u32[]{:S(2)}, u32[]{:S(2)}) collective-permute-start(bf16[320,128]{1,0:T(8,128)(2,1)S(1)} %get-tuple-element.104), channel_id=1, source_target_pairs={{0,28},{1,29},{2,30},{3,31},{4,0},{5,1},{6,2},{7,3},{8,4},{9,5},{1... | collective-permute-start | bytes 245768 | tf_op jit(solution)/shard_map/ppermute | solution.py:559
  272.9 2.8 collective-permute-start.35
  275.7 9.3 %expert_out.1 = bf16[5120,128]{1,0:T(8,128)(2,1)} custom-call(bf16[320,768]{1,0:T(8,128)(2,1)} %copy-done.2, bf16[320,2048]{1,0:T(8,128)(2,1)} %copy-done, f32[320,128]{1,0:T(8,128)} %get-tuple-element.87.weight_ref, f32[320,128]{1,0:T(8,128)} %get-tuple-element.86.refs_17_.first_ref, bf16[2048,768]{1,0:T(8,128)(2,1)} %bitcast.19), custom_call_target="tpu_custom_call" | custom-call | flops 1006632960 | bytes 8388608 | tf_op jit(solution)/shard_map/expert_out/pallas_call | solution.py:108
  285.1 12.2 %all-to-all-start.2 = ((bf16[32,160,128]{2,1,0:T(8,128)(2,1)}), bf16[32,160,128]{2,1,0:T(8,128)(2,1)S(1)}, u32[]{:S(2)}, u32[]{:S(2)}) async-start(bf16[32,160,128]{2,1,0:T(8,128)(2,1)} %bitcast.23), calls=%async_computation.2 | async-start | bytes 2621440 | tf_op jit(solution)/shard_map/all_to_all | solution.py:542
  297.3 5.0 %collective-permute-start.36 = (bf16[320,128]{1,0:T(8,128)(2,1)S(1)}, bf16[320,128]{1,0:T(8,128)(2,1)S(1)}, u32[]{:S(2)}, u32[]{:S(2)}) collective-permute-start(bf16[320,128]{1,0:T(8,128)(2,1)S(1)} %get-tuple-element.122), channel_id=1, source_target_pairs={{0,30},{1,31},{2,0},{3,1},{4,2},{5,3},{6,4},{7,5},{8,6},{9,7},{10,... | collective-permute-start | bytes 245768 | tf_op jit(solution)/shard_map/ppermute | solution.py:559
  302.3 55.6 %collective-permute-done.36.refs_15_ = bf16[320,128]{1,0:T(8,128)(2,1)S(1)} collective-permute-done((bf16[320,128]{1,0:T(8,128)(2,1)S(1)}, bf16[320,128]{1,0:T(8,128)(2,1)S(1)}, u32[]{:S(2)}, u32[]{:S(2)}) %collective-permute-start.36) | collective-permute-done | bytes 81952 | tf_op jit(solution)/shard_map/ppermute | solution.py:559
  357.9 3.2 slot_sums.1
  362.2 1.9 collective-permute-start.37
  364.1 1.9 collective-permute-done.37.their_ref
  366.8 4.2 %mixer_grad.1 = (bf16[64,4096]{1,0:T(8,128)(2,1)}, f32[72,128]{1,0:T(8,128)}) custom-call(f32[64,4096]{1,0:T(8,128)} %copy-done.1, bf16[64,4096]{1,0:T(8,128)(2,1)} %copy-done.13, bf16[128,4096]{1,0:T(8,128)(2,1)} %read_ref.5, f32[256,128]{1,0:T(8,128)} %get-tuple-element.126.dt_ref), custom_call_target="tpu_custom_call" | custom-call | flops 268435456 | bytes 6291456 | tf_op jit(solution)/shard_map/mixer_grad/pallas_call | solution.py:108
  372.2 3.3 collective-permute-start.40
  375.5 1.9 collective-permute-start.39
  377.5 2.1 collective-permute-start.38
  379.9 4.1 %collective-permute-done.39.m2_ref = f32[72,128]{1,0:T(8,128)S(1)} collective-permute-done((f32[72,128]{1,0:T(8,128)}, f32[72,128]{1,0:T(8,128)S(1)}, u32[]{:S(2)}, u32[]{:S(2)}) %collective-permute-start.39) | collective-permute-done | bytes 36896 | tf_op jit(solution)/shard_map/ppermute | solution.py:537
  384.0 1.6 collective-permute-done.38.m1_ref
  386.2 8.7 %mixer_backward.1 = bf16[64,4096]{1,0:T(8,128)(2,1)} custom-call(f32[72,128]{1,0:T(8,128)} %copy-done.21, f32[72,128]{1,0:T(8,128)} %copy-done.20, f32[72,128]{1,0:T(8,128)} %copy-done.19, f32[72,128]{1,0:T(8,128)} %copy-done.18, f32[256,128]{1,0:T(8,128)} %get-tuple-element.68.rt_ref, bf16[64,4096]{1,0:T(8,128)(2,1)} %get-tuple-element.128.grad_ref, ...), custom_call_target="tpu_custom_call" | custom-call | flops 268435456 | bytes 6291456 | tf_op jit(solution)/shard_map/mixer_backward/pallas_call | solution.py:108
  396.0 4.9 %combine.1 = bf16[2048,128]{1,0:T(8,128)(2,1)} custom-call(f32[2,128]{1,0:T(2,128)} %copy-done.23, bf16[5120,128]{1,0:T(8,128)(2,1)} %bitcast.21), custom_call_target="tpu_custom_call" | custom-call | flops 167772160 | bytes 4194304 | tf_op jit(solution)/shard_map/combine/pallas_call | solution.py:108
  (101 shorter events, 18.4 us)
Async XLA Ops:
  7.2 175.8 %all-gather.3.cloned.1.call-start = ((), (), s32[]{:S(2)}) async-start(), calls=%async_computation.3 | async-start | bytes 3342336 | tf_op jit(solution)/shard_map/all_gather | solution.py:608
  7.9 182.0 %all-gather.5.cloned.1.call-start = ((), (), s32[]{:S(2)}) async-start(), calls=%async_computation.4 | async-start | bytes 6684672 | tf_op jit(solution)/shard_map/all_gather | solution.py:607
  8.6 22.6 %collective-permute-start.21 = (bf16[2048,128]{1,0:T(8,128)(2,1)}, bf16[2048,128]{1,0:T(8,128)(2,1)S(1)}, u32[]{:S(2)}, u32[]{:S(2)}) collective-permute-start(bf16[2048,128]{1,0:T(8,128)(2,1)} %own_ref.1), channel_id=1, source_target_pairs={{0,1},{1,0},{2,3},{3,2},{4,5},{5,4},{6,7},{7,6},{8,9},{9,8},{10,11... | collective-permute-start | bytes 1572872 | tf_op jit(solution)/shard_map/ppermute | solution.py:564
  11.3 20.0 %copy-start.23 = (f32[2,128]{1,0:T(2,128)}, f32[2,128]{1,0:T(2,128)S(1)}, u32[]{:S(2)}) copy-start(f32[2,128]{1,0:T(2,128)S(1)} %convert_bitcast_fusion.own_ids_ref.ids_ref) | copy-start | bytes 3076
  12.6 30.0 %all-to-all-start = ((f32[32,4,128]{2,1,0:T(4,128)}), f32[32,4,128]{2,1,0:T(4,128)S(1)}, u32[]{:S(2)}, u32[]{:S(2)}) async-start(f32[32,4,128]{2,1,0:T(4,128)} %broadcast_in_dim.2), calls=%async_computation | async-start | bytes 131072 | tf_op jit(solution)/shard_map/all_to_all | solution.py:585
  28.2 3.0 collective-permute-start.20
  42.6 6.8 %copy-start.22 = (f32[2,4096]{1,0:T(2,128)S(1)}, f32[2,4096]{1,0:T(2,128)}, u32[]{:S(2)}) copy-start(f32[2,4096]{1,0:T(2,128)} %param.14) | copy-start | bytes 98308
  42.6 140.3 %all-to-all-start.1 = ((bf16[16,320,128]{2,1,0:T(8,128)(2,1)}), bf16[16,320,128]{2,1,0:T(8,128)(2,1)S(1)}, u32[]{:S(2)}, u32[]{:S(2)}) async-start(bf16[16,320,128]{2,1,0:T(8,128)(2,1)} %bitcast.20), calls=%async_computation.1 | async-start | bytes 2621440 | tf_op jit(solution)/shard_map/all_to_all | solution.py:550
  54.1 15.0 %collective-permute-start.3 = (f32[72,128]{1,0:T(8,128)}, f32[72,128]{1,0:T(8,128)S(1)}, u32[]{:S(2)}, u32[]{:S(2)}) collective-permute-start(f32[72,128]{1,0:T(8,128)} %get-tuple-element.67), channel_id=1, source_target_pairs={{0,128},{32,160},{64,192},{96,224},{128,256},{160,288},{192,320},{... | collective-permute-start | bytes 110600 | tf_op jit(solution)/shard_map/ppermute | solution.py:537
  57.6 11.5 %collective-permute-start.2 = (f32[72,128]{1,0:T(8,128)}, f32[72,128]{1,0:T(8,128)S(1)}, u32[]{:S(2)}, u32[]{:S(2)}) collective-permute-start(f32[72,128]{1,0:T(8,128)} %get-tuple-element.67), channel_id=1, source_target_pairs={{0,96},{32,128},{64,160},{96,192},{128,224},{160,256},{192,288},{2... | collective-permute-start | bytes 110600 | tf_op jit(solution)/shard_map/ppermute | solution.py:537
  61.3 7.9 %collective-permute-start.1 = (f32[72,128]{1,0:T(8,128)}, f32[72,128]{1,0:T(8,128)S(1)}, u32[]{:S(2)}, u32[]{:S(2)}) collective-permute-start(f32[72,128]{1,0:T(8,128)} %get-tuple-element.67), channel_id=1, source_target_pairs={{0,64},{32,96},{64,128},{96,160},{128,192},{160,224},{192,256},{22... | collective-permute-start | bytes 110600 | tf_op jit(solution)/shard_map/ppermute | solution.py:537
  65.1 6.8 %collective-permute-start = (f32[72,128]{1,0:T(8,128)}, f32[72,128]{1,0:T(8,128)S(1)}, u32[]{:S(2)}, u32[]{:S(2)}) collective-permute-start(f32[72,128]{1,0:T(8,128)} %get-tuple-element.67), channel_id=1, source_target_pairs={{0,32},{32,64},{64,96},{96,128},{128,160},{160,192},{192,224},{224... | collective-permute-start | bytes 110600 | tf_op jit(solution)/shard_map/ppermute | solution.py:537
  69.1 2.8 copy-start.14
  69.1 2.8 copy-start.15
  69.3 2.7 copy-start.16
  83.5 4.0 collective-permute-start.4
  96.6 40.7 %collective-permute-start.5 = (bf16[320,128]{1,0:T(8,128)(2,1)}, bf16[320,128]{1,0:T(8,128)(2,1)S(1)}, u32[]{:S(2)}, u32[]{:S(2)}) collective-permute-start(bf16[320,128]{1,0:T(8,128)(2,1)} %get-tuple-element.71), channel_id=1, source_target_pairs={{0,16},{1,17},{2,18},{3,19},{4,20},{5,21},{6,22},{7,23},{8,24},{9,... | collective-permute-start | bytes 245768 | tf_op jit(solution)/shard_map/ppermute | solution.py:559
  109.1 30.1 %collective-permute-start.6 = (bf16[320,128]{1,0:T(8,128)(2,1)}, bf16[320,128]{1,0:T(8,128)(2,1)S(1)}, u32[]{:S(2)}, u32[]{:S(2)}) collective-permute-start(bf16[320,128]{1,0:T(8,128)(2,1)} %get-tuple-element.72), channel_id=1, source_target_pairs={{0,14},{1,15},{2,16},{3,17},{4,18},{5,19},{6,20},{7,21},{8,22},{9,... | collective-permute-start | bytes 245768 | tf_op jit(solution)/shard_map/ppermute | solution.py:559
  111.3 37.8 %collective-permute-start.7 = (bf16[320,128]{1,0:T(8,128)(2,1)}, bf16[320,128]{1,0:T(8,128)(2,1)S(1)}, u32[]{:S(2)}, u32[]{:S(2)}) collective-permute-start(bf16[320,128]{1,0:T(8,128)(2,1)} %get-tuple-element.73), channel_id=1, source_target_pairs={{0,18},{1,19},{2,20},{3,21},{4,22},{5,23},{6,24},{7,25},{8,26},{9,... | collective-permute-start | bytes 245768 | tf_op jit(solution)/shard_map/ppermute | solution.py:559
  122.8 28.8 %collective-permute-start.8 = (bf16[320,128]{1,0:T(8,128)(2,1)}, bf16[320,128]{1,0:T(8,128)(2,1)S(1)}, u32[]{:S(2)}, u32[]{:S(2)}) collective-permute-start(bf16[320,128]{1,0:T(8,128)(2,1)} %get-tuple-element.74), channel_id=1, source_target_pairs={{0,12},{1,13},{2,14},{3,15},{4,16},{5,17},{6,18},{7,19},{8,20},{9,... | collective-permute-start | bytes 245768 | tf_op jit(solution)/shard_map/ppermute | solution.py:559
  125.0 33.9 %collective-permute-start.9 = (bf16[320,128]{1,0:T(8,128)(2,1)}, bf16[320,128]{1,0:T(8,128)(2,1)S(1)}, u32[]{:S(2)}, u32[]{:S(2)}) collective-permute-start(bf16[320,128]{1,0:T(8,128)(2,1)} %get-tuple-element.75), channel_id=1, source_target_pairs={{0,20},{1,21},{2,22},{3,23},{4,24},{5,25},{6,26},{7,27},{8,28},{9,... | collective-permute-start | bytes 245768 | tf_op jit(solution)/shard_map/ppermute | solution.py:559
  137.3 23.6 %collective-permute-start.10 = (bf16[320,128]{1,0:T(8,128)(2,1)}, bf16[320,128]{1,0:T(8,128)(2,1)S(1)}, u32[]{:S(2)}, u32[]{:S(2)}) collective-permute-start(bf16[320,128]{1,0:T(8,128)(2,1)} %get-tuple-element.76), channel_id=1, source_target_pairs={{0,10},{1,11},{2,12},{3,13},{4,14},{5,15},{6,16},{7,17},{8,18},{9,... | collective-permute-start | bytes 245768 | tf_op jit(solution)/shard_map/ppermute | solution.py:559
  139.2 28.6 %collective-permute-start.11 = (bf16[320,128]{1,0:T(8,128)(2,1)}, bf16[320,128]{1,0:T(8,128)(2,1)S(1)}, u32[]{:S(2)}, u32[]{:S(2)}) collective-permute-start(bf16[320,128]{1,0:T(8,128)(2,1)} %get-tuple-element.77), channel_id=1, source_target_pairs={{0,22},{1,23},{2,24},{3,25},{4,26},{5,27},{6,28},{7,29},{8,30},{9,... | collective-permute-start | bytes 245768 | tf_op jit(solution)/shard_map/ppermute | solution.py:559
  149.1 20.6 %collective-permute-start.12 = (bf16[320,128]{1,0:T(8,128)(2,1)}, bf16[320,128]{1,0:T(8,128)(2,1)S(1)}, u32[]{:S(2)}, u32[]{:S(2)}) collective-permute-start(bf16[320,128]{1,0:T(8,128)(2,1)} %get-tuple-element.78), channel_id=1, source_target_pairs={{0,8},{1,9},{2,10},{3,11},{4,12},{5,13},{6,14},{7,15},{8,16},{9,17... | collective-permute-start | bytes 245768 | tf_op jit(solution)/shard_map/ppermute | solution.py:559
  151.6 24.2 %collective-permute-start.13 = (bf16[320,128]{1,0:T(8,128)(2,1)}, bf16[320,128]{1,0:T(8,128)(2,1)S(1)}, u32[]{:S(2)}, u32[]{:S(2)}) collective-permute-start(bf16[320,128]{1,0:T(8,128)(2,1)} %get-tuple-element.79), channel_id=1, source_target_pairs={{0,24},{1,25},{2,26},{3,27},{4,28},{5,29},{6,30},{7,31},{8,0},{9,1... | collective-permute-start | bytes 245768 | tf_op jit(solution)/shard_map/ppermute | solution.py:559
  158.9 18.8 %collective-permute-start.14 = (bf16[320,128]{1,0:T(8,128)(2,1)}, bf16[320,128]{1,0:T(8,128)(2,1)S(1)}, u32[]{:S(2)}, u32[]{:S(2)}) collective-permute-start(bf16[320,128]{1,0:T(8,128)(2,1)} %get-tuple-element.80), channel_id=1, source_target_pairs={{0,6},{1,7},{2,8},{3,9},{4,10},{5,11},{6,12},{7,13},{8,14},{9,15},... | collective-permute-start | bytes 245768 | tf_op jit(solution)/shard_map/ppermute | solution.py:559
  160.9 29.0 %collective-permute-start.15 = (bf16[320,128]{1,0:T(8,128)(2,1)}, bf16[320,128]{1,0:T(8,128)(2,1)S(1)}, u32[]{:S(2)}, u32[]{:S(2)}) collective-permute-start(bf16[320,128]{1,0:T(8,128)(2,1)} %get-tuple-element.81), channel_id=1, source_target_pairs={{0,26},{1,27},{2,28},{3,29},{4,30},{5,31},{6,0},{7,1},{8,2},{9,3},... | collective-permute-start | bytes 245768 | tf_op jit(solution)/shard_map/ppermute | solution.py:559
  167.8 22.0 %collective-permute-start.16 = (bf16[320,128]{1,0:T(8,128)(2,1)}, bf16[320,128]{1,0:T(8,128)(2,1)S(1)}, u32[]{:S(2)}, u32[]{:S(2)}) collective-permute-start(bf16[320,128]{1,0:T(8,128)(2,1)} %get-tuple-element.82), channel_id=1, source_target_pairs={{0,4},{1,5},{2,6},{3,7},{4,8},{5,9},{6,10},{7,11},{8,12},{9,13},{1... | collective-permute-start | bytes 245768 | tf_op jit(solution)/shard_map/ppermute | solution.py:559
  169.8 20.1 %collective-permute-start.17 = (bf16[320,128]{1,0:T(8,128)(2,1)}, bf16[320,128]{1,0:T(8,128)(2,1)S(1)}, u32[]{:S(2)}, u32[]{:S(2)}) collective-permute-start(bf16[320,128]{1,0:T(8,128)(2,1)} %get-tuple-element.83), channel_id=1, source_target_pairs={{0,28},{1,29},{2,30},{3,31},{4,0},{5,1},{6,2},{7,3},{8,4},{9,5},{1... | collective-permute-start | bytes 245768 | tf_op jit(solution)/shard_map/ppermute | solution.py:559
  175.8 14.1 %collective-permute-start.18 = (bf16[320,128]{1,0:T(8,128)(2,1)}, bf16[320,128]{1,0:T(8,128)(2,1)S(1)}, u32[]{:S(2)}, u32[]{:S(2)}) collective-permute-start(bf16[320,128]{1,0:T(8,128)(2,1)} %get-tuple-element.84), channel_id=1, source_target_pairs={{0,2},{1,3},{2,4},{3,5},{4,6},{5,7},{6,8},{7,9},{8,10},{9,11},{10,... | collective-permute-start | bytes 245768 | tf_op jit(solution)/shard_map/ppermute | solution.py:559
  177.7 12.1 %collective-permute-start.19 = (bf16[320,128]{1,0:T(8,128)(2,1)}, bf16[320,128]{1,0:T(8,128)(2,1)S(1)}, u32[]{:S(2)}, u32[]{:S(2)}) collective-permute-start(bf16[320,128]{1,0:T(8,128)(2,1)} %get-tuple-element.85), channel_id=1, source_target_pairs={{0,30},{1,31},{2,0},{3,1},{4,2},{5,3},{6,4},{7,5},{8,6},{9,7},{10,... | collective-permute-start | bytes 245768 | tf_op jit(solution)/shard_map/ppermute | solution.py:559
  182.9 1.1 copy-start.11
  184.0 6.0 %copy-start.4 = (f32[320,128]{1,0:T(8,128)S(1)}, f32[320,128]{1,0:T(8,128)}, u32[]{:S(2)}) copy-start(f32[320,128]{1,0:T(8,128)} %get-tuple-element.86.refs_17_.first_ref) | copy-start | bytes 491524
  184.0 6.0 %copy-start.8 = (f32[2048]{0:T(1024)S(1)}, f32[2048]{0:T(1024)}, u32[]{:S(2)}) copy-start(f32[2048]{0:T(1024)} %param.18) | copy-start | bytes 24580
  184.0 6.0 %copy-start.9 = (bf16[320,128]{1,0:T(8,128)(2,1)S(1)}, bf16[320,128]{1,0:T(8,128)(2,1)}, u32[]{:S(2)}) copy-start(bf16[320,128]{1,0:T(8,128)(2,1)} %get-tuple-element.70.refs_0_) | copy-start | bytes 245764
  189.9 2.8 copy-start.5
  192.7 1.3 copy-start.6
  194.1 1.2 copy-start.7
  206.0 28.4 %collective-permute-start.22 = (bf16[320,128]{1,0:T(8,128)(2,1)S(1)}, bf16[320,128]{1,0:T(8,128)(2,1)S(1)}, u32[]{:S(2)}, u32[]{:S(2)}) collective-permute-start(bf16[320,128]{1,0:T(8,128)(2,1)S(1)} %get-tuple-element.92), channel_id=1, source_target_pairs={{0,16},{1,17},{2,18},{3,19},{4,20},{5,21},{6,22},{7,23},{8,24},{9,... | collective-permute-start | bytes 245768 | tf_op jit(solution)/shard_map/ppermute | solution.py:559
  207.9 33.4 %collective-permute-start.23 = (bf16[320,128]{1,0:T(8,128)(2,1)S(1)}, bf16[320,128]{1,0:T(8,128)(2,1)S(1)}, u32[]{:S(2)}, u32[]{:S(2)}) collective-permute-start(bf16[320,128]{1,0:T(8,128)(2,1)S(1)} %get-tuple-element.93), channel_id=1, source_target_pairs={{0,14},{1,15},{2,16},{3,17},{4,18},{5,19},{6,20},{7,21},{8,22},{9,... | collective-permute-start | bytes 245768 | tf_op jit(solution)/shard_map/ppermute | solution.py:559
  217.9 28.4 %collective-permute-start.24 = (bf16[320,128]{1,0:T(8,128)(2,1)S(1)}, bf16[320,128]{1,0:T(8,128)(2,1)S(1)}, u32[]{:S(2)}, u32[]{:S(2)}) collective-permute-start(bf16[320,128]{1,0:T(8,128)(2,1)S(1)} %get-tuple-element.94), channel_id=1, source_target_pairs={{0,18},{1,19},{2,20},{3,21},{4,22},{5,23},{6,24},{7,25},{8,26},{9,... | collective-permute-start | bytes 245768 | tf_op jit(solution)/shard_map/ppermute | solution.py:559
  221.6 32.0 %collective-permute-start.25 = (bf16[320,128]{1,0:T(8,128)(2,1)S(1)}, bf16[320,128]{1,0:T(8,128)(2,1)S(1)}, u32[]{:S(2)}, u32[]{:S(2)}) collective-permute-start(bf16[320,128]{1,0:T(8,128)(2,1)S(1)} %get-tuple-element.95), channel_id=1, source_target_pairs={{0,12},{1,13},{2,14},{3,15},{4,16},{5,17},{6,18},{7,19},{8,20},{9,... | collective-permute-start | bytes 245768 | tf_op jit(solution)/shard_map/ppermute | solution.py:559
  229.4 26.6 %collective-permute-start.26 = (bf16[320,128]{1,0:T(8,128)(2,1)S(1)}, bf16[320,128]{1,0:T(8,128)(2,1)S(1)}, u32[]{:S(2)}, u32[]{:S(2)}) collective-permute-start(bf16[320,128]{1,0:T(8,128)(2,1)S(1)} %get-tuple-element.96), channel_id=1, source_target_pairs={{0,20},{1,21},{2,22},{3,23},{4,24},{5,25},{6,26},{7,27},{8,28},{9,... | collective-permute-start | bytes 245768 | tf_op jit(solution)/shard_map/ppermute | solution.py:559
  234.4 26.9 %collective-permute-start.27 = (bf16[320,128]{1,0:T(8,128)(2,1)S(1)}, bf16[320,128]{1,0:T(8,128)(2,1)S(1)}, u32[]{:S(2)}, u32[]{:S(2)}) collective-permute-start(bf16[320,128]{1,0:T(8,128)(2,1)S(1)} %get-tuple-element.97), channel_id=1, source_target_pairs={{0,10},{1,11},{2,12},{3,13},{4,14},{5,15},{6,16},{7,17},{8,18},{9,... | collective-permute-start | bytes 245768 | tf_op jit(solution)/shard_map/ppermute | solution.py:559
  241.4 23.6 %collective-permute-start.28 = (bf16[320,128]{1,0:T(8,128)(2,1)S(1)}, bf16[320,128]{1,0:T(8,128)(2,1)S(1)}, u32[]{:S(2)}, u32[]{:S(2)}) collective-permute-start(bf16[320,128]{1,0:T(8,128)(2,1)S(1)} %get-tuple-element.98), channel_id=1, source_target_pairs={{0,22},{1,23},{2,24},{3,25},{4,26},{5,27},{6,28},{7,29},{8,30},{9,... | collective-permute-start | bytes 245768 | tf_op jit(solution)/shard_map/ppermute | solution.py:559
  246.3 22.5 %collective-permute-start.29 = (bf16[320,128]{1,0:T(8,128)(2,1)S(1)}, bf16[320,128]{1,0:T(8,128)(2,1)S(1)}, u32[]{:S(2)}, u32[]{:S(2)}) collective-permute-start(bf16[320,128]{1,0:T(8,128)(2,1)S(1)} %get-tuple-element.99), channel_id=1, source_target_pairs={{0,8},{1,9},{2,10},{3,11},{4,12},{5,13},{6,14},{7,15},{8,16},{9,17... | collective-permute-start | bytes 245768 | tf_op jit(solution)/shard_map/ppermute | solution.py:559
  253.6 19.4 %collective-permute-start.30 = (bf16[320,128]{1,0:T(8,128)(2,1)S(1)}, bf16[320,128]{1,0:T(8,128)(2,1)S(1)}, u32[]{:S(2)}, u32[]{:S(2)}) collective-permute-start(bf16[320,128]{1,0:T(8,128)(2,1)S(1)} %get-tuple-element.100), channel_id=1, source_target_pairs={{0,24},{1,25},{2,26},{3,27},{4,28},{5,29},{6,30},{7,31},{8,0},{9,1... | collective-permute-start | bytes 245768 | tf_op jit(solution)/shard_map/ppermute | solution.py:559
  256.0 29.0 %collective-permute-start.31 = (bf16[320,128]{1,0:T(8,128)(2,1)S(1)}, bf16[320,128]{1,0:T(8,128)(2,1)S(1)}, u32[]{:S(2)}, u32[]{:S(2)}) collective-permute-start(bf16[320,128]{1,0:T(8,128)(2,1)S(1)} %get-tuple-element.101), channel_id=1, source_target_pairs={{0,6},{1,7},{2,8},{3,9},{4,10},{5,11},{6,12},{7,13},{8,14},{9,15},... | collective-permute-start | bytes 245768 | tf_op jit(solution)/shard_map/ppermute | solution.py:559
  261.2 23.9 %collective-permute-start.32 = (bf16[320,128]{1,0:T(8,128)(2,1)S(1)}, bf16[320,128]{1,0:T(8,128)(2,1)S(1)}, u32[]{:S(2)}, u32[]{:S(2)}) collective-permute-start(bf16[320,128]{1,0:T(8,128)(2,1)S(1)} %get-tuple-element.102), channel_id=1, source_target_pairs={{0,26},{1,27},{2,28},{3,29},{4,30},{5,31},{6,0},{7,1},{8,2},{9,3},... | collective-permute-start | bytes 245768 | tf_op jit(solution)/shard_map/ppermute | solution.py:559
  264.9 20.2 %collective-permute-start.33 = (bf16[320,128]{1,0:T(8,128)(2,1)S(1)}, bf16[320,128]{1,0:T(8,128)(2,1)S(1)}, u32[]{:S(2)}, u32[]{:S(2)}) collective-permute-start(bf16[320,128]{1,0:T(8,128)(2,1)S(1)} %get-tuple-element.103), channel_id=1, source_target_pairs={{0,4},{1,5},{2,6},{3,7},{4,8},{5,9},{6,10},{7,11},{8,12},{9,13},{1... | collective-permute-start | bytes 245768 | tf_op jit(solution)/shard_map/ppermute | solution.py:559
  268.8 16.3 %collective-permute-start.34 = (bf16[320,128]{1,0:T(8,128)(2,1)S(1)}, bf16[320,128]{1,0:T(8,128)(2,1)S(1)}, u32[]{:S(2)}, u32[]{:S(2)}) collective-permute-start(bf16[320,128]{1,0:T(8,128)(2,1)S(1)} %get-tuple-element.104), channel_id=1, source_target_pairs={{0,28},{1,29},{2,30},{3,31},{4,0},{5,1},{6,2},{7,3},{8,4},{9,5},{1... | collective-permute-start | bytes 245768 | tf_op jit(solution)/shard_map/ppermute | solution.py:559
  272.9 12.2 %collective-permute-start.35 = (bf16[320,128]{1,0:T(8,128)(2,1)S(1)}, bf16[320,128]{1,0:T(8,128)(2,1)S(1)}, u32[]{:S(2)}, u32[]{:S(2)}) collective-permute-start(bf16[320,128]{1,0:T(8,128)(2,1)S(1)} %get-tuple-element.105), channel_id=1, source_target_pairs={{0,2},{1,3},{2,4},{3,5},{4,6},{5,7},{6,8},{7,9},{8,10},{9,11},{10,... | collective-permute-start | bytes 245768 | tf_op jit(solution)/shard_map/ppermute | solution.py:559
  285.1 72.8 %copy-start.3 = (f32[512,128]{1,0:T(8,128)S(1)}, f32[512,128]{1,0:T(8,128)}, u32[]{:S(2)}) copy-start(f32[512,128]{1,0:T(8,128)} %get-tuple-element.123.refs_16_) | copy-start | bytes 786436
  285.1 109.8 %all-to-all-start.2 = ((bf16[32,160,128]{2,1,0:T(8,128)(2,1)}), bf16[32,160,128]{2,1,0:T(8,128)(2,1)S(1)}, u32[]{:S(2)}, u32[]{:S(2)}) async-start(bf16[32,160,128]{2,1,0:T(8,128)(2,1)} %bitcast.23), calls=%async_computation.2 | async-start | bytes 2621440 | tf_op jit(solution)/shard_map/all_to_all | solution.py:542
  297.3 60.6 %collective-permute-start.36 = (bf16[320,128]{1,0:T(8,128)(2,1)S(1)}, bf16[320,128]{1,0:T(8,128)(2,1)S(1)}, u32[]{:S(2)}, u32[]{:S(2)}) collective-permute-start(bf16[320,128]{1,0:T(8,128)(2,1)S(1)} %get-tuple-element.122), channel_id=1, source_target_pairs={{0,30},{1,31},{2,0},{3,1},{4,2},{5,3},{6,4},{7,5},{8,6},{9,7},{10,... | collective-permute-start | bytes 245768 | tf_op jit(solution)/shard_map/ppermute | solution.py:559
  362.2 3.8 collective-permute-start.37
  370.9 8.7 %collective-permute-start.41 = (f32[72,128]{1,0:T(8,128)}, f32[72,128]{1,0:T(8,128)S(1)}, u32[]{:S(2)}, u32[]{:S(2)}) collective-permute-start(f32[72,128]{1,0:T(8,128)} %get-tuple-element.127), channel_id=1, source_target_pairs={{128,0},{160,32},{192,64},{224,96},{256,128},{288,160},{320,192},{... | collective-permute-start | bytes 110600 | tf_op jit(solution)/shard_map/ppermute | solution.py:537
  372.2 7.7 %collective-permute-start.40 = (f32[72,128]{1,0:T(8,128)}, f32[72,128]{1,0:T(8,128)S(1)}, u32[]{:S(2)}, u32[]{:S(2)}) collective-permute-start(f32[72,128]{1,0:T(8,128)} %get-tuple-element.127), channel_id=1, source_target_pairs={{96,0},{128,32},{160,64},{192,96},{224,128},{256,160},{288,192},{3... | collective-permute-start | bytes 110600 | tf_op jit(solution)/shard_map/ppermute | solution.py:537
  375.5 8.5 %collective-permute-start.39 = (f32[72,128]{1,0:T(8,128)}, f32[72,128]{1,0:T(8,128)S(1)}, u32[]{:S(2)}, u32[]{:S(2)}) collective-permute-start(f32[72,128]{1,0:T(8,128)} %get-tuple-element.127), channel_id=1, source_target_pairs={{64,0},{96,32},{128,64},{160,96},{192,128},{224,160},{256,192},{28... | collective-permute-start | bytes 110600 | tf_op jit(solution)/shard_map/ppermute | solution.py:537
  377.5 8.2 %collective-permute-start.38 = (f32[72,128]{1,0:T(8,128)}, f32[72,128]{1,0:T(8,128)S(1)}, u32[]{:S(2)}, u32[]{:S(2)}) collective-permute-start(f32[72,128]{1,0:T(8,128)} %get-tuple-element.127), channel_id=1, source_target_pairs={{32,0},{64,32},{96,64},{128,96},{160,128},{192,160},{224,192},{256... | collective-permute-start | bytes 110600 | tf_op jit(solution)/shard_map/ppermute | solution.py:537
  379.6 6.0 %copy-start.18 = (f32[72,128]{1,0:T(8,128)}, f32[72,128]{1,0:T(8,128)S(1)}, u32[]{:S(2)}) copy-start(f32[72,128]{1,0:T(8,128)S(1)} %collective-permute-done.41.m4_ref) | copy-start | bytes 110596
  379.9 5.7 %copy-start.19 = (f32[72,128]{1,0:T(8,128)}, f32[72,128]{1,0:T(8,128)S(1)}, u32[]{:S(2)}) copy-start(f32[72,128]{1,0:T(8,128)S(1)} %collective-permute-done.40.m3_ref) | copy-start | bytes 110596
  384.0 1.6 copy-start.20
  394.9 1.1 copy-start.10
  (9 other events, 7.0 us)
Sparse Core Ops, SparseCore 0:
  11.0 68.0 all-gather.2
  82.1 76.6 all-gather.4

commit v5 on v3

--- a/solution.py
+++ b/solution.py
@@ -26,6 +26,7 @@
 FBLOCKS = WIDTH // LANES
 REACH = 4
 VMEM = 60 * 1024 * 1024
+VMEM_PART = 50 * 1024 * 1024
 
 LAST = (((1,), (1,)), ((), ()))
 FIRST = (((0,), (0,)), ((), ()))
@@ -88,15 +89,15 @@
     lax.fori_loop(0, ROWS // BLOCK, step, 0, unroll=4)
 
 
-def call(kernel, outs, args, in_specs, scratch=(), flops=0, moved=0, name=None):
+def call(kernel, outs, args, in_specs, scratch=(), flops=0, moved=0, name=None, vmem=VMEM, out_specs=None):
     vm = pl.BlockSpec(memory_space=pltpu.VMEM)
     return pl.pallas_call(
         kernel,
         out_shape=tuple(jax.ShapeDtypeStruct(shape, kind) for shape, kind in outs),
         in_specs=in_specs,
-        out_specs=tuple(vm for _ in outs),
+        out_specs=out_specs or tuple(vm for _ in outs),
         scratch_shapes=list(scratch),
-        compiler_params=pltpu.CompilerParams(vmem_limit_bytes=VMEM),
+        compiler_params=pltpu.CompilerParams(vmem_limit_bytes=vmem),
         cost_estimate=pl.CostEstimate(flops=flops, bytes_accessed=moved, transcendentals=0),
         name=name,
     )(*args)
@@ -104,7 +105,7 @@
 
 VM = pl.BlockSpec(memory_space=pltpu.VMEM)
 SM = pl.BlockSpec(memory_space=pltpu.SMEM)
-HBM = pl.BlockSpec(memory_space=pl.ANY)
+HBM = pl.BlockSpec(memory_space=pltpu.HBM)
 
 
 def grad_rows_kernel(core_ref, own_ids_ref, their_ids_ref, own_ref, their_ref, out_ref, wide_ref):
@@ -339,21 +340,42 @@
 def expert_kernel(
     rows_ref,
     gain_ref,
-    first_ref,
-    grad_ref,
-    dhid_ref,
+    first_hbm,
+    grad_hbm,
+    dhid_hbm,
     in_hbm,
-    msg_ref,
-    normed_ref,
-    hidden_ref,
+    msg_hbm,
+    normed_hbm,
+    hidden_hbm,
     y_ref,
     scaled_ref,
     dcat_ref,
     in_ref,
-    sem,
+    first_ref,
+    grad_ref,
+    dhid_ref,
+    normed_ref,
+    hidden_ref,
+    msg_ref,
+    fetch_sems,
+    store_sems,
+    msg_sems,
 ):
-    fetch = pltpu.make_async_copy(in_hbm, in_ref, sem)
-    fetch.start()
+    fetches = [
+        pltpu.make_async_copy(src, dst, fetch_sems.at[i])
+        for i, (src, dst) in enumerate(
+            (
+                (in_hbm, in_ref),
+                (dhid_hbm, dhid_ref),
+                (grad_hbm, grad_ref),
+                (first_hbm, first_ref),
+            )
+        )
+    ]
+    for fetch in fetches:
+        fetch.start()
+    keep_normed = pltpu.make_async_copy(normed_ref, normed_hbm, store_sems.at[0])
+    keep_hidden = pltpu.make_async_copy(hidden_ref, hidden_hbm, store_sems.at[1])
 
     def unpack(k, squares):
         lanes = pl.ds(pl.multiple_of(k * LANES, LANES), LANES)
@@ -372,7 +394,9 @@
         return carry
 
     lax.fori_loop(0, FBLOCKS, scale, 0, unroll=4)
-    fetch.wait()
+    keep_normed.start()
+    fetches[0].wait()
+    fetches[1].wait()
 
     def project(i, carry):
         lanes = pl.ds(pl.multiple_of(i * 256, 256), 256)
@@ -387,7 +411,10 @@
         dcat_ref[:, lanes_up] = (dhid * swish).astype(bf16)
         return carry
 
-    lax.fori_loop(0, FF // 256, project, 0)
+    lax.fori_loop(0, FF // 256, project, 0, unroll=True)
+    keep_hidden.start()
+    fetches[2].wait()
+    fetches[3].wait()
     first = first_ref[...]
     first2 = jnp.concatenate([first, first], axis=1)
 
@@ -400,24 +427,43 @@
         product = scaled * y_ref[:, lanes]
         return acc + product[:, :LANES] + product[:, LANES:]
 
-    acc = lax.fori_loop(0, WIDTH // 256, back, jnp.zeros((SLOTS, LANES), f32))
+    acc = lax.fori_loop(0, WIDTH // 256, back, jnp.zeros((SLOTS, LANES), f32), unroll=2)
     mean_grad = jnp.sum(acc, axis=1, keepdims=True) * (1.0 / WIDTH)
     pull = jnp.broadcast_to(rscale * rscale * rscale * mean_grad, (SLOTS, LANES))
 
-    def pack(k, carry):
-        lanes = pl.ds(pl.multiple_of(k * LANES, LANES), LANES)
-        part = rscale_b * scaled_ref[:, lanes] - pull * y_ref[:, lanes]
-        msg_ref[pl.ds(pl.multiple_of(k * SLOTS, SLOTS), SLOTS), :] = part.astype(bf16)
-        return carry
-
-    lax.fori_loop(0, FBLOCKS, pack, 0, unroll=4)
+    parts = 4
+    sends = []
+    for part in range(parts):
+        for k in range(part * FBLOCKS // parts, (part + 1) * FBLOCKS // parts):
+            lanes = slice(k * LANES, (k + 1) * LANES)
+            msg_ref[k * SLOTS : (k + 1) * SLOTS, :] = (
+                rscale_b * scaled_ref[:, lanes] - pull * y_ref[:, lanes]
+            ).astype(bf16)
+        rows = pl.ds(part * (ROWS // parts), ROWS // parts)
+        sends.append(
+            pltpu.make_async_copy(msg_ref.at[rows, :], msg_hbm.at[rows, :], msg_sems.at[part])
+        )
+        sends[-1].start()
+    for copy in (keep_normed, keep_hidden, *sends):
+        copy.wait()
 
 
 def expert_out_kernel(
-    hidden_ref, normed_ref, weight_ref, first_ref, out_hbm, msg_ref, wide_ref, out_ref, sem
+    expert_ref,
+    hidden_ref,
+    normed_ref,
+    weight_ref,
+    first_ref,
+    out_hbm,
+    own_ref,
+    their_ref,
+    wide_ref,
+    out_ref,
+    sem,
 ):
     fetch = pltpu.make_async_copy(out_hbm, out_ref, sem)
     fetch.start()
+    core = lax.rem(expert_ref[0], 2)
     weight = weight_ref[...]
     weight2 = jnp.concatenate([weight, weight], axis=1)
     first = first_ref[...]
@@ -435,22 +481,43 @@
                 for c in range(CAP):
                     at = (par * CAP + c) * PAIRS
                     wide_ref[
-                        pl.ds(par * BLOCK + c * FBLOCKS + fb, PAIRS, stride=2 * BLOCK), :
+                        pl.ds(par * (ROWS // 2) + c * FBLOCKS + fb, PAIRS, stride=BLOCK), :
                     ] = part[at : at + PAIRS]
         return carry
 
     lax.fori_loop(0, WIDTH // 256, matmul, 0)
-    round_rows(msg_ref, wide_ref)
-
-
-def combine_kernel(ids_ref, rows_ref, out_ref, wide_ref):
+    half_rows = ROWS // 2
+
+    def split(i, carry):
+        at = pl.multiple_of(i * BLOCK, BLOCK)
+        own_at = pl.multiple_of(core * half_rows + at, BLOCK)
+        their_at = pl.multiple_of((1 - core) * half_rows + at, BLOCK)
+        own_ref[pl.ds(at, BLOCK), :] = wide_ref[pl.ds(own_at, BLOCK), :].astype(bf16)
+        their_ref[pl.ds(at, BLOCK), :] = wide_ref[pl.ds(their_at, BLOCK), :].astype(bf16)
+        return carry
+
+    lax.fori_loop(0, CHIPS, split, 0, unroll=2)
+
+
+def combine_kernel(expert_ref, ids_ref, rows_ref, out_ref, wide_ref):
     round_rows(wide_ref, rows_ref)
-    select = slot_onehot(rank_table(ids_ref[0:1, :], ids_ref[1:2, :], earlier_mask()))
+    core = lax.rem(expert_ref[0], 2)
+    earlier = earlier_mask()
+    select = jnp.concatenate(
+        [
+            slot_onehot(rank_table(ids_ref[0:1, :], ids_ref[1:2, :], earlier, CHIPS, side))
+            for side in (core, 1 - core)
+        ],
+        axis=0,
+    )
 
     def step(fb, carry):
         rows = jnp.concatenate(
             [
-                wide_ref[pl.ds(c * FBLOCKS + fb, EXPERTS, stride=BLOCK), :].astype(bf16)
+                wide_ref[
+                    pl.ds(side * BLOCK + c * FBLOCKS + fb, CHIPS, stride=2 * BLOCK), :
+                ].astype(bf16)
+                for side in range(2)
                 for c in range(CAP)
             ],
             axis=0,
@@ -535,13 +602,6 @@
     return lax.ppermute(value, "ctx", pairs)
 
 
-def exchanged(rows):
-    blocks = rows.reshape(EXPERTS, BLOCK, LANES)
-    return lax.all_to_all(blocks, "exp", split_axis=0, concat_axis=0, tiled=True).reshape(
-        ROWS, LANES
-    )
-
-
 def exchanged_by_core(rows):
     blocks = rows.reshape(CHIPS, SLOTS, LANES)
     groups = [list(range(core, EXPERTS, 2)) for core in range(2)]
@@ -572,12 +632,15 @@
     wide = pltpu.VMEM((ROWS, LANES), f32)
     ids_own = expert_ids.T.astype(f32)
     tokens_own = jnp.concatenate([ids_own, route_weights.T], axis=0)
-    tokens = lax.all_to_all(
-        jnp.broadcast_to(tokens_own[None], (EXPERTS, 4, LANES)), "exp", 0, 0, tiled=True
-    )
+    tokens_sent = jnp.broadcast_to(tokens_own[None], (EXPERTS, 4, LANES))
+    tokens_sent, expert_in, expert_out, out_grad, ids_own = lax.optimization_barrier(
+        (tokens_sent, expert_in, expert_out, out_grad, ids_own)
+    )
+    tokens = lax.all_to_all(tokens_sent, "exp", 0, 0, tiled=True)
     tokens = tokens.reshape(PAIRS, 2, 4, LANES).transpose(2, 1, 0, 3).reshape(4, CHUNKS, LANES)
 
     me_core = lax.rem(me_exp, 2).astype(i32).reshape(1)
+    me = me_exp.astype(i32).reshape(1)
 
     their_ids = from_other_core(ids_own)
     their_grad = from_other_core(out_grad)
@@ -629,7 +692,7 @@
             ((SLOTS, LANES), f32),
             ((SLOTS, LANES), f32),
         ],
-        (me_exp.astype(i32).reshape(1), y_own, y_their, tokens),
+        (me, y_own, y_their, tokens),
         [SM] + [VM] * 3,
         [wide],
         flops=4 * HP * SLOTS * SEQ,
@@ -647,6 +710,7 @@
         flops=2 * SLOTS * FF * WIDTH,
         moved=8 << 20,
         name="hidden_grad",
+        vmem=VMEM_PART,
     )
     back_out_rows, normed, hidden = call(
         expert_kernel,
@@ -656,31 +720,47 @@
             ((SLOTS, FF), bf16),
         ],
         (y_in_rows, norm_gain.reshape(1, WIDTH), slot_first, grad_slots, d_hidden, weight_in),
-        [VM, VM, VM, VM, VM, HBM],
+        [VM, VM, HBM, HBM, HBM, HBM],
         [
             pltpu.VMEM((SLOTS, WIDTH), f32),
             pltpu.VMEM((SLOTS, WIDTH), f32),
             pltpu.VMEM((SLOTS, 2 * FF), bf16),
             pltpu.VMEM((WIDTH, 2 * FF), bf16),
-            pltpu.SemaphoreType.DMA,
+            pltpu.VMEM((SLOTS, LANES), f32),
+            pltpu.VMEM((SLOTS, WIDTH), bf16),
+            pltpu.VMEM((SLOTS, FF), f32),
+            pltpu.VMEM((SLOTS, WIDTH), bf16),
+            pltpu.VMEM((SLOTS, FF), bf16),
+            pltpu.VMEM((ROWS, LANES), bf16),
+            pltpu.SemaphoreType.DMA((4,)),
+            pltpu.SemaphoreType.DMA((2,)),
+            pltpu.SemaphoreType.DMA((4,)),
         ],
         flops=8 * SLOTS * FF * WIDTH,
         moved=14 << 20,
         name="expert",
+        out_specs=(HBM, HBM, HBM),
     )
     back_in_rows = exchanged_by_core(back_out_rows)
 
-    (result_rows,) = call(
+    own_rows, their_rows = call(
         expert_out_kernel,
-        [((ROWS, LANES), bf16)],
-        (hidden, normed, slot_weight, slot_first, weight_out),
-        [VM, VM, VM, VM, HBM],
+        [((ROWS // 2, LANES), bf16)] * 2,
+        (me, hidden, normed, slot_weight, slot_first, weight_out),
+        [SM, VM, VM, VM, VM, HBM],
         [wide, pltpu.VMEM((WIDTH, FF), bf16), pltpu.SemaphoreType.DMA],
         flops=2 * SLOTS * FF * WIDTH,
         moved=8 << 20,
         name="expert_out",
     )
-    returned_rows = exchanged(result_rows)
+    result_rows = jnp.concatenate(
+        [
+            rows.reshape(CHIPS, BLOCK, LANES)
+            for rows in (own_rows, from_other_core(their_rows))
+        ],
+        axis=1,
+    ).reshape(ROWS, LANES)
+    returned_rows = exchanged_by_core(result_rows)
 
     own_sums, their_sums = call(
         slot_sums_kernel,
@@ -691,6 +771,7 @@
         flops=4 * HP * SLOTS * SEQ,
         moved=4 << 20,
         name="slot_sums",
+        vmem=VMEM_PART,
     )
     y_grad, back_message = call(
         grad_kernel,
@@ -715,12 +796,13 @@
     (block_out,) = call(
         combine_kernel,
         [((WIDTH, LANES), bf16)],
-        (ids_own, returned_rows),
-        [VM, VM],
+        (me, ids_own, returned_rows),
+        [SM, VM, VM],
         [wide],
         flops=2 * SLOTS * LANES * WIDTH,
         moved=4 << 20,
         name="combine",
+        vmem=VMEM_PART,
     )
     return (block_out, input_grad)
 

time: 357 us -> 345 us (0.966)
  Pallas kernels: 81.3 us -> 72.8 us
  waiting for transfers between devices: 172 us -> 165 us
    all_to_all x2 -> x1, waiting for transfers between devices: 34.3 us -> 5.24 us  [per_device(): tokens = lax.all_to_all(tokens_sent, 'exp', 0, 0, tiled=True)]
    all_to_all x3 -> x4, waiting for transfers between devices: 123 us -> 143 us  [exchanged_by_core(): lax.all_to_all(blocks, 'exp', split_axis=0, concat_axis=0, tiled=True, ax...]
    pallas_call x11, Pallas kernels: 81.3 us -> 72.8 us  [call(): pl.pallas_call(kernel, out_shape=tuple((jax.ShapeDtypeStruct(shape, kind)...]
    all_to_all x2 -> x1, starting transfers between devices: 22 us -> 15.6 us  [per_device(): tokens = lax.all_to_all(tokens_sent, 'exp', 0, 0, tiled=True)]
    all_to_all x3 -> x4, starting transfers between devices: 23.8 us -> 29.9 us  [exchanged_by_core(): lax.all_to_all(blocks, 'exp', split_axis=0, concat_axis=0, tiled=True, ax...]
    ppermute x4 -> x5, starting transfers between devices: 8.18 us -> 9.84 us  [from_other_core(): return lax.ppermute(value, 'exp', [(i, i ^ 1) for i in range(EXPERTS)])]
    unnamed x36 -> x42, local copies, waits for them, and re-layouts: 7.95 us -> 7.71 us
  transfers between devices with their start and end apart: 19 -> 20, of which waited for: 13 -> 14; matrix products, arithmetic and copies ran while one was open for 1% -> 1% of each run, Pallas kernels for 18% -> 17%
where the time goes in v5:
time: 345 us; the launch traced here: 343 us
  waiting for transfers between devices  165 us (48%)
  starting transfers between devices  78.2 us (23%)
  Pallas kernels  72.8 us (21%)
  between operations  14.4 us (4%)
  local copies, waits for them, and re-layouts  9.63 us (3%)
  other arithmetic  3.69 us (1%)
    all_to_all x4, waiting for transfers between devices, exchanged_by_core(): lax.all_to_all(blocks, 'exp', split_axis=0, concat_axis=0, tiled=True, ax...  143 us
    pallas_call x11, Pallas kernels, call(): pl.pallas_call(kernel, out_shape=tuple((jax.ShapeDtypeStruct(shape, kind)...  72.8 us
    all_to_all x4, starting transfers between devices, exchanged_by_core(): lax.all_to_all(blocks, 'exp', split_axis=0, concat_axis=0, tiled=True, ax...  29.9 us
    ppermute x8, starting transfers between devices, sent_along(): return lax.ppermute(value, 'ctx', pairs)  22.8 us
    all_to_all x1, starting transfers between devices, per_device(): tokens = lax.all_to_all(tokens_sent, 'exp', 0, 0, tiled=True)  15.6 us
    ppermute x5, starting transfers between devices, from_other_core(): return lax.ppermute(value, 'exp', [(i, i ^ 1) for i in range(EXPERTS)])  9.84 us
    ppermute x8, waiting for transfers between devices, sent_along(): return lax.ppermute(value, 'ctx', pairs)  8.99 us
    unnamed x42, local copies, waits for them, and re-layouts  7.71 us
  transfers between devices with their start and end apart: 20, of which 14 were waited for; matrix products, arithmetic and copies ran while one was open for 1% of the time, Pallas kernels for 17%

profile of v5, /device:TPU:6, one launch (start us, length us, event | category | flops | bytes accessed | tf_op | source)
XLA Modules:
  0.0 343.4 jit_solution(11981173777231018037)
XLA Ops:
  7.2 0.0 all-gather.3.cloned.1.call-start
  7.2 0.7 convert_bitcast_fusion.own_ids_ref.ids_ref
  7.9 0.7 pad_maximum_fusion.1
  8.6 0.6 broadcast_in_dim.2
  9.2 0.0 all-gather.3.cloned.1.call-update
  9.2 0.0 all-gather.5.cloned.1.call-start
  9.3 0.7 all-gather.5.cloned.1.call-update
  10.0 1.9 collective-permute-start.6
  11.9 15.6 %all-to-all-start = ((f32[32,4,128]{2,1,0:T(4,128)}), f32[32,4,128]{2,1,0:T(4,128)S(1)}, u32[]{:S(2)}, u32[]{:S(2)}) async-start(f32[32,4,128]{2,1,0:T(4,128)} %broadcast_in_dim.2), calls=%async_computation | async-start | bytes 131072 | tf_op jit(solution)/shard_map/all_to_all | solution.py:639
  27.5 2.2 collective-permute-start.5
  29.7 0.8 collective-permute-done.5.their_ids_ref
  30.6 0.6 copy-done.19
  31.1 0.2 copy-done.8
  31.4 5.3 %grad_rows.1 = bf16[5120,128]{1,0:T(8,128)(2,1)} custom-call(s32[1]{0:T(128)} %bitcast.10.core_ref, f32[2,128]{1,0:T(2,128)} %copy-done.3, f32[2,128]{1,0:T(2,128)} %copy-done.19, bf16[2048,128]{1,0:T(8,128)(2,1)} %own_ref, bf16[2048,128]{1,0:T(8,128)(2,1)} %copy-done.8), custom_call_target="tpu_custom_call" | custom-call | flops 167772160 | bytes 4194304 | tf_op jit(solution)/shard_map/grad_rows/pallas_call | solution.py:94
  36.7 5.2 %all-to-all-done = f32[32,4,128]{2,1,0:T(4,128)S(1)} async-done(((f32[32,4,128]{2,1,0:T(4,128)}), f32[32,4,128]{2,1,0:T(4,128)S(1)}, u32[]{:S(2)}, u32[]{:S(2)}) %all-to-all-start) | async-done | bytes 65568 | tf_op jit(solution)/shard_map/all_to_all | solution.py:639
  42.0 6.8 %all-to-all-start.2 = ((bf16[16,320,128]{2,1,0:T(8,128)(2,1)}), bf16[16,320,128]{2,1,0:T(8,128)(2,1)S(1)}, u32[]{:S(2)}, u32[]{:S(2)}) async-start(bf16[16,320,128]{2,1,0:T(8,128)(2,1)} %bitcast.27), calls=%async_computation.2 | async-start | bytes 2621440 | tf_op jit(solution)/shard_map/all_to_all | solution.py:608
  48.7 0.6 reshape.55.decay_ref
  49.4 4.1 %shard_state.1 = (f32[256,128]{1,0:T(8,128)}, f32[256,128]{1,0:T(8,128)}, f32[72,128]{1,0:T(8,128)}) custom-call(s32[8]{0:T(128)} %docs_ref.1, s32[1]{0:T(128)} %bitcast.3.base_ref, f32[64,128]{1,0:T(8,128)} %reshape.55.decay_ref, bf16[64,4096]{1,0:T(8,128)(2,1)} %x_ref.3, bf16[128,4096]{1,0:T(8,128)(2,1)} %write_ref.5), custom_call_target="tpu_custom_call" | custom-call | flops 67108864 | bytes 3145728 | tf_op jit(solution)/shard_map/shard_state/pallas_call | solution.py:94
  53.5 3.5 %collective-permute-start.3 = (f32[72,128]{1,0:T(8,128)}, f32[72,128]{1,0:T(8,128)S(1)}, u32[]{:S(2)}, u32[]{:S(2)}) collective-permute-start(f32[72,128]{1,0:T(8,128)} %get-tuple-element.30), channel_id=1, source_target_pairs={{0,128},{32,160},{64,192},{96,224},{128,256},{160,288},{192,320},{... | collective-permute-start | bytes 110600 | tf_op jit(solution)/shard_map/ppermute | solution.py:602
  56.9 3.8 %collective-permute-start.2 = (f32[72,128]{1,0:T(8,128)}, f32[72,128]{1,0:T(8,128)S(1)}, u32[]{:S(2)}, u32[]{:S(2)}) collective-permute-start(f32[72,128]{1,0:T(8,128)} %get-tuple-element.30), channel_id=1, source_target_pairs={{0,96},{32,128},{64,160},{96,192},{128,224},{160,256},{192,288},{2... | collective-permute-start | bytes 110600 | tf_op jit(solution)/shard_map/ppermute | solution.py:602
  60.7 3.7 %collective-permute-start.1 = (f32[72,128]{1,0:T(8,128)}, f32[72,128]{1,0:T(8,128)S(1)}, u32[]{:S(2)}, u32[]{:S(2)}) collective-permute-start(f32[72,128]{1,0:T(8,128)} %get-tuple-element.30), channel_id=1, source_target_pairs={{0,64},{32,96},{64,128},{96,160},{128,192},{160,224},{192,256},{22... | collective-permute-start | bytes 110600 | tf_op jit(solution)/shard_map/ppermute | solution.py:602
  64.5 4.0 %collective-permute-start = (f32[72,128]{1,0:T(8,128)}, f32[72,128]{1,0:T(8,128)S(1)}, u32[]{:S(2)}, u32[]{:S(2)}) collective-permute-start(f32[72,128]{1,0:T(8,128)} %get-tuple-element.30), channel_id=1, source_target_pairs={{0,32},{32,64},{64,96},{96,128},{128,160},{160,192},{192,224},{224... | collective-permute-start | bytes 110600 | tf_op jit(solution)/shard_map/ppermute | solution.py:602
  68.5 0.4 collective-permute-done.1.m2_ref
  68.9 2.4 collective-permute-done.m1_ref
  71.3 0.6 copy-done.13
  71.9 11.0 %mixer_forward.1 = (bf16[64,4096]{1,0:T(8,128)(2,1)}, bf16[8192,128]{1,0:T(8,128)(2,1)}) custom-call(f32[72,128]{1,0:T(8,128)} %copy-done.13, f32[72,128]{1,0:T(8,128)} %copy-done.12, f32[72,128]{1,0:T(8,128)} %copy-done.11, f32[72,128]{1,0:T(8,128)} %copy-done.10, f32[256,128]{1,0:T(8,128)} %get-tuple-element.31.rt_ref, bf16[64,4096]{1,0:T(8,128)(2,1)} %x_ref.3, ...), custom_call_target="tpu_custom_call" | custom-call | flops 268435456 | bytes 9437184 | tf_op jit(solution)/shard_map/mixer_forward/pallas_call | solution.py:94
  82.9 1.9 collective-permute-start.4
  84.8 0.6 copy.15
  85.4 1.4 collective-permute-done.4.their_ref
  86.9 0.8 copy-done.20
  87.7 8.3 %dispatch.1 = (bf16[5120,128]{1,0:T(8,128)(2,1)}, f32[512,128]{1,0:T(8,128)}, f32[320,128]{1,0:T(8,128)}, f32[320,128]{1,0:T(8,128)}) custom-call(s32[1]{0:T(128)} %bitcast.expert_ref, bf16[64,4096]{1,0:T(8,128)(2,1)} %get-tuple-element.32.own_ref, bf16[64,4096]{1,0:T(8,128)(2,1)} %copy-done.20, f32[4,32,128]{2,1,0:T(8,128)} %bitcast.34), custom_call_target="tpu_custom_call" | custom-call | flops 335544320 | bytes 4194304 | tf_op jit(solution)/shard_map/dispatch/pallas_call | solution.py:94
  95.9 13.8 %all-to-all-done.2 = bf16[16,320,128]{2,1,0:T(8,128)(2,1)S(1)} async-done(((bf16[16,320,128]{2,1,0:T(8,128)(2,1)}), bf16[16,320,128]{2,1,0:T(8,128)(2,1)S(1)}, u32[]{:S(2)}, u32[]{:S(2)}) %all-to-all-start.2) | async-done | bytes 1310752 | tf_op jit(solution)/shard_map/all_to_all | solution.py:608
  109.7 8.6 %all-to-all-start.1 = ((bf16[16,320,128]{2,1,0:T(8,128)(2,1)}), bf16[16,320,128]{2,1,0:T(8,128)(2,1)S(1)}, u32[]{:S(2)}, u32[]{:S(2)}) async-start(bf16[16,320,128]{2,1,0:T(8,128)(2,1)} %bitcast.30), calls=%async_computation.1 | async-start | bytes 2621440 | tf_op jit(solution)/shard_map/all_to_all | solution.py:608
  118.3 0.0 all-gather.3.cloned.1.call-done
  118.4 3.5 %hidden_grad.1 = (bf16[320,2048]{1,0:T(8,128)(2,1)S(1)}, f32[320,768]{1,0:T(8,128)S(1)}) custom-call(bf16[5120,128]{1,0:T(8,128)(2,1)S(1)} %bitcast.24, f32[320,128]{1,0:T(8,128)S(1)} %copy-done.1, bf16[2048,768]{1,0:T(8,128)(2,1)} %bitcast.25), custom_call_target="tpu_custom_call" | custom-call | flops 1006632960 | bytes 8388608 | tf_op jit(solution)/shard_map/hidden_grad/pallas_call | solution.py:94
  121.9 1.1 copy-done.5
  123.0 1.0 copy-done.6
  124.0 55.2 %all-to-all-done.1 = bf16[16,320,128]{2,1,0:T(8,128)(2,1)S(1)} async-done(((bf16[16,320,128]{2,1,0:T(8,128)(2,1)}), bf16[16,320,128]{2,1,0:T(8,128)(2,1)S(1)}, u32[]{:S(2)}, u32[]{:S(2)}) %all-to-all-start.1) | async-done | bytes 1310752 | tf_op jit(solution)/shard_map/all_to_all | solution.py:608
  179.2 1.1 copy-done.7
  180.3 11.9 %expert.1 = (bf16[5120,128]{1,0:T(8,128)(2,1)}, bf16[320,2048]{1,0:T(8,128)(2,1)}, bf16[320,768]{1,0:T(8,128)(2,1)}) custom-call(bf16[5120,128]{1,0:T(8,128)(2,1)} %bitcast.29, f32[1,2048]{1,0:T(1,128)} %bitcast.37, f32[320,128]{1,0:T(8,128)} %get-tuple-element.35.first_hbm.first_ref, bf16[320,2048]{1,0:T(8,128)(2,1)} %copy-done.5, f32[320,768]{1,0:T(8,128)} %copy-done.6, ...), custom_call_target="tpu_custom_call" | custom-call | flops 4026531840 | bytes 14680064 | tf_op jit(solution)/shard_map/expert/pallas_call | solution.py:94
  192.2 8.5 %all-to-all-start.4 = ((bf16[16,320,128]{2,1,0:T(8,128)(2,1)}), bf16[16,320,128]{2,1,0:T(8,128)(2,1)S(1)}, u32[]{:S(2)}, u32[]{:S(2)}) async-start(bf16[16,320,128]{2,1,0:T(8,128)(2,1)} %bitcast.28), calls=%async_computation.4 | async-start | bytes 2621440 | tf_op jit(solution)/shard_map/all_to_all | solution.py:608
  200.8 9.3 %expert_out.1 = (bf16[2560,128]{1,0:T(8,128)(2,1)}, bf16[2560,128]{1,0:T(8,128)(2,1)}) custom-call(s32[1]{0:T(128)} %bitcast.expert_ref, bf16[320,768]{1,0:T(8,128)(2,1)} %get-tuple-element.42.hidden_ref, bf16[320,2048]{1,0:T(8,128)(2,1)} %get-tuple-element.43.normed_ref, f32[320,128]{1,0:T(8,128)} %get-tuple-element.37.weight_ref, ...), custom_call_target="tpu_custom_call" | custom-call | flops 1006632960 | bytes 8388608 | tf_op jit(solution)/shard_map/expert_out/pallas_call | solution.py:94
  210.1 1.9 collective-permute-start.7
  212.0 2.3 collective-permute-done.7
  214.3 2.3 pad_maximum_fusion
  216.6 47.3 %all-to-all-done.4 = bf16[16,320,128]{2,1,0:T(8,128)(2,1)S(1)} async-done(((bf16[16,320,128]{2,1,0:T(8,128)(2,1)}), bf16[16,320,128]{2,1,0:T(8,128)(2,1)S(1)}, u32[]{:S(2)}, u32[]{:S(2)}) %all-to-all-start.4) | async-done | bytes 1310752 | tf_op jit(solution)/shard_map/all_to_all | solution.py:608
  264.0 6.0 %all-to-all-start.3 = ((bf16[16,320,128]{2,1,0:T(8,128)(2,1)}), bf16[16,320,128]{2,1,0:T(8,128)(2,1)S(1)}, u32[]{:S(2)}, u32[]{:S(2)}) async-start(bf16[16,320,128]{2,1,0:T(8,128)(2,1)} %pad_maximum_fusion), calls=%async_computation.3 | async-start | bytes 2621440 | tf_op jit(solution)/shard_map/all_to_all | solution.py:608
  270.0 3.2 slot_sums.1
  273.3 1.0 copy-done
  274.3 1.9 collective-permute-start.8
  276.2 1.9 collective-permute-done.8.their_ref
  278.1 0.8 copy-done.9
  278.9 4.2 %mixer_grad.1 = (bf16[64,4096]{1,0:T(8,128)(2,1)}, f32[72,128]{1,0:T(8,128)}) custom-call(f32[64,4096]{1,0:T(8,128)} %copy-done, bf16[64,4096]{1,0:T(8,128)(2,1)} %copy-done.9, bf16[128,4096]{1,0:T(8,128)(2,1)} %read_ref.5, f32[256,128]{1,0:T(8,128)} %get-tuple-element.50.dt_ref), custom_call_target="tpu_custom_call" | custom-call | flops 268435456 | bytes 6291456 | tf_op jit(solution)/shard_map/mixer_grad/pallas_call | solution.py:94
  283.0 1.3 collective-permute-start.12
  284.3 2.4 collective-permute-start.11
  286.7 2.2 collective-permute-start.10
  288.9 1.9 collective-permute-start.9
  290.9 0.4 collective-permute-done.11.m3_ref
  291.3 3.9 %collective-permute-done.10.m2_ref = f32[72,128]{1,0:T(8,128)S(1)} collective-permute-done((f32[72,128]{1,0:T(8,128)}, f32[72,128]{1,0:T(8,128)S(1)}, u32[]{:S(2)}, u32[]{:S(2)}) %collective-permute-start.10) | collective-permute-done | bytes 36896 | tf_op jit(solution)/shard_map/ppermute | solution.py:602
  295.2 1.9 collective-permute-done.9.m1_ref
  297.1 0.6 copy-done.17
  297.7 8.7 %mixer_backward.1 = bf16[64,4096]{1,0:T(8,128)(2,1)} custom-call(f32[72,128]{1,0:T(8,128)} %copy-done.17, f32[72,128]{1,0:T(8,128)} %copy-done.16, f32[72,128]{1,0:T(8,128)} %copy-done.15, f32[72,128]{1,0:T(8,128)} %copy-done.14, f32[256,128]{1,0:T(8,128)} %get-tuple-element.31.rt_ref, bf16[64,4096]{1,0:T(8,128)(2,1)} %get-tuple-element.52.grad_ref, ...), custom_call_target="tpu_custom_call" | custom-call | flops 268435456 | bytes 6291456 | tf_op jit(solution)/shard_map/mixer_backward/pallas_call | solution.py:94
  306.4 26.9 %all-to-all-done.3 = bf16[16,320,128]{2,1,0:T(8,128)(2,1)S(1)} async-done(((bf16[16,320,128]{2,1,0:T(8,128)(2,1)}), bf16[16,320,128]{2,1,0:T(8,128)(2,1)S(1)}, u32[]{:S(2)}, u32[]{:S(2)}) %all-to-all-start.3) | async-done | bytes 1310752 | tf_op jit(solution)/shard_map/all_to_all | solution.py:608
  333.3 3.3 combine.1
  (38 shorter events, 0.1 us)
Async XLA Ops:
  7.2 111.2 %all-gather.3.cloned.1.call-start = ((), (), s32[]{:S(2)}) async-start(), calls=%async_computation.5 | async-start | bytes 3342336 | tf_op jit(solution)/shard_map/all_gather | solution.py:660
  7.9 22.7 %copy-start.3 = (f32[2,128]{1,0:T(2,128)}, f32[2,128]{1,0:T(2,128)S(1)}, u32[]{:S(2)}) copy-start(f32[2,128]{1,0:T(2,128)S(1)} %convert_bitcast_fusion.own_ids_ref.ids_ref) | copy-start | bytes 3076
  9.2 170.0 %all-gather.5.cloned.1.call-start = ((), (), s32[]{:S(2)}) async-start(), calls=%async_computation.6 | async-start | bytes 6684672 | tf_op jit(solution)/shard_map/all_gather | solution.py:659
  10.0 20.6 %collective-permute-start.6 = (bf16[2048,128]{1,0:T(8,128)(2,1)}, bf16[2048,128]{1,0:T(8,128)(2,1)S(1)}, u32[]{:S(2)}, u32[]{:S(2)}) collective-permute-start(bf16[2048,128]{1,0:T(8,128)(2,1)} %own_ref), channel_id=1, source_target_pairs={{0,1},{1,0},{2,3},{3,2},{4,5},{5,4},{6,7},{7,6},{8,9},{9,8},{10,11... | collective-permute-start | bytes 1572872 | tf_op jit(solution)/shard_map/ppermute | solution.py:614
  11.9 30.0 %all-to-all-start = ((f32[32,4,128]{2,1,0:T(4,128)}), f32[32,4,128]{2,1,0:T(4,128)S(1)}, u32[]{:S(2)}, u32[]{:S(2)}) async-start(f32[32,4,128]{2,1,0:T(4,128)} %broadcast_in_dim.2), calls=%async_computation | async-start | bytes 131072 | tf_op jit(solution)/shard_map/all_to_all | solution.py:639
  27.5 3.0 collective-permute-start.5
  30.6 0.6 copy-start.19
  30.6 0.8 copy-start.8
  41.9 6.8 %copy-start.18 = (f32[2,4096]{1,0:T(2,128)S(1)}, f32[2,4096]{1,0:T(2,128)}, u32[]{:S(2)}) copy-start(f32[2,4096]{1,0:T(2,128)} %param.14) | copy-start | bytes 98308
  42.0 67.8 %all-to-all-start.2 = ((bf16[16,320,128]{2,1,0:T(8,128)(2,1)}), bf16[16,320,128]{2,1,0:T(8,128)(2,1)S(1)}, u32[]{:S(2)}, u32[]{:S(2)}) async-start(bf16[16,320,128]{2,1,0:T(8,128)(2,1)} %bitcast.27), calls=%async_computation.2 | async-start | bytes 2621440 | tf_op jit(solution)/shard_map/all_to_all | solution.py:608
  53.5 15.0 %collective-permute-start.3 = (f32[72,128]{1,0:T(8,128)}, f32[72,128]{1,0:T(8,128)S(1)}, u32[]{:S(2)}, u32[]{:S(2)}) collective-permute-start(f32[72,128]{1,0:T(8,128)} %get-tuple-element.30), channel_id=1, source_target_pairs={{0,128},{32,160},{64,192},{96,224},{128,256},{160,288},{192,320},{... | collective-permute-start | bytes 110600 | tf_op jit(solution)/shard_map/ppermute | solution.py:602
  56.9 11.5 %collective-permute-start.2 = (f32[72,128]{1,0:T(8,128)}, f32[72,128]{1,0:T(8,128)S(1)}, u32[]{:S(2)}, u32[]{:S(2)}) collective-permute-start(f32[72,128]{1,0:T(8,128)} %get-tuple-element.30), channel_id=1, source_target_pairs={{0,96},{32,128},{64,160},{96,192},{128,224},{160,256},{192,288},{2... | collective-permute-start | bytes 110600 | tf_op jit(solution)/shard_map/ppermute | solution.py:602
  60.7 8.2 %collective-permute-start.1 = (f32[72,128]{1,0:T(8,128)}, f32[72,128]{1,0:T(8,128)S(1)}, u32[]{:S(2)}, u32[]{:S(2)}) collective-permute-start(f32[72,128]{1,0:T(8,128)} %get-tuple-element.30), channel_id=1, source_target_pairs={{0,64},{32,96},{64,128},{96,160},{128,192},{160,224},{192,256},{22... | collective-permute-start | bytes 110600 | tf_op jit(solution)/shard_map/ppermute | solution.py:602
  64.5 6.8 %collective-permute-start = (f32[72,128]{1,0:T(8,128)}, f32[72,128]{1,0:T(8,128)S(1)}, u32[]{:S(2)}, u32[]{:S(2)}) collective-permute-start(f32[72,128]{1,0:T(8,128)} %get-tuple-element.30), channel_id=1, source_target_pairs={{0,32},{32,64},{64,96},{96,128},{128,160},{160,192},{192,224},{224... | collective-permute-start | bytes 110600 | tf_op jit(solution)/shard_map/ppermute | solution.py:602
  68.5 2.8 copy-start.10
  68.5 2.8 copy-start.11
  68.9 2.4 copy-start.12
  71.3 0.6 copy-start.13
  82.9 4.0 %collective-permute-start.4 = (bf16[64,4096]{1,0:T(8,128)(2,1)}, bf16[64,4096]{1,0:T(8,128)(2,1)S(1)}, u32[]{:S(2)}, u32[]{:S(2)}) collective-permute-start(bf16[64,4096]{1,0:T(8,128)(2,1)} %get-tuple-element.32.own_ref), channel_id=1, source_target_pairs={{0,1},{1,0},{2,3},{3,2},{4,5},{5,4},{6,7},{7,6},{8,9},{9,8},{10,11... | collective-permute-start | bytes 1572872 | tf_op jit(solution)/shard_map/ppermute | solution.py:614
  86.9 0.8 copy-start.20
  109.7 8.6 %copy-start.1 = (f32[320,128]{1,0:T(8,128)S(1)}, f32[320,128]{1,0:T(8,128)}, u32[]{:S(2)}) copy-start(f32[320,128]{1,0:T(8,128)} %get-tuple-element.37.weight_ref) | copy-start | bytes 491524
  109.7 69.5 %all-to-all-start.1 = ((bf16[16,320,128]{2,1,0:T(8,128)(2,1)}), bf16[16,320,128]{2,1,0:T(8,128)(2,1)S(1)}, u32[]{:S(2)}, u32[]{:S(2)}) async-start(bf16[16,320,128]{2,1,0:T(8,128)(2,1)} %bitcast.30), calls=%async_computation.1 | async-start | bytes 2621440 | tf_op jit(solution)/shard_map/all_to_all | solution.py:608
  121.9 1.1 copy-start.5
  123.0 1.0 copy-start.6
  179.2 1.1 copy-start.7
  192.2 71.7 %all-to-all-start.4 = ((bf16[16,320,128]{2,1,0:T(8,128)(2,1)}), bf16[16,320,128]{2,1,0:T(8,128)(2,1)S(1)}, u32[]{:S(2)}, u32[]{:S(2)}) async-start(bf16[16,320,128]{2,1,0:T(8,128)(2,1)} %bitcast.28), calls=%async_computation.4 | async-start | bytes 2621440 | tf_op jit(solution)/shard_map/all_to_all | solution.py:608
  210.1 4.2 %collective-permute-start.7 = (bf16[2560,128]{1,0:T(8,128)(2,1)}, bf16[2560,128]{1,0:T(8,128)(2,1)S(1)}, u32[]{:S(2)}, u32[]{:S(2)}) collective-permute-start(bf16[2560,128]{1,0:T(8,128)(2,1)} %get-tuple-element.45), channel_id=1, source_target_pairs={{0,1},{1,0},{2,3},{3,2},{4,5},{5,4},{6,7},{7,6},{8,9},{9,8},{10,11... | collective-permute-start | bytes 1966088 | tf_op jit(solution)/shard_map/ppermute | solution.py:614
  216.6 53.4 %copy-start.2 = (f32[512,128]{1,0:T(8,128)S(1)}, f32[512,128]{1,0:T(8,128)}, u32[]{:S(2)}) copy-start(f32[512,128]{1,0:T(8,128)} %get-tuple-element.47.rank_ref) | copy-start | bytes 786436
  264.0 69.3 %all-to-all-start.3 = ((bf16[16,320,128]{2,1,0:T(8,128)(2,1)}), bf16[16,320,128]{2,1,0:T(8,128)(2,1)S(1)}, u32[]{:S(2)}, u32[]{:S(2)}) async-start(bf16[16,320,128]{2,1,0:T(8,128)(2,1)} %pad_maximum_fusion), calls=%async_computation.3 | async-start | bytes 2621440 | tf_op jit(solution)/shard_map/all_to_all | solution.py:608
  273.3 1.0 copy-start
  274.3 3.8 %collective-permute-start.8 = (bf16[64,4096]{1,0:T(8,128)(2,1)S(1)}, bf16[64,4096]{1,0:T(8,128)(2,1)S(1)}, u32[]{:S(2)}, u32[]{:S(2)}) collective-permute-start(bf16[64,4096]{1,0:T(8,128)(2,1)S(1)} %get-tuple-element.49), channel_id=1, source_target_pairs={{0,1},{1,0},{2,3},{3,2},{4,5},{5,4},{6,7},{7,6},{8,9},{9,8},{10,11... | collective-permute-start | bytes 1572872 | tf_op jit(solution)/shard_map/ppermute | solution.py:614
  278.1 0.8 copy-start.9
  283.0 7.8 %collective-permute-start.12 = (f32[72,128]{1,0:T(8,128)}, f32[72,128]{1,0:T(8,128)S(1)}, u32[]{:S(2)}, u32[]{:S(2)}) collective-permute-start(f32[72,128]{1,0:T(8,128)} %get-tuple-element.51), channel_id=1, source_target_pairs={{128,0},{160,32},{192,64},{224,96},{256,128},{288,160},{320,192},{... | collective-permute-start | bytes 110600 | tf_op jit(solution)/shard_map/ppermute | solution.py:602
  284.3 7.0 %collective-permute-start.11 = (f32[72,128]{1,0:T(8,128)}, f32[72,128]{1,0:T(8,128)S(1)}, u32[]{:S(2)}, u32[]{:S(2)}) collective-permute-start(f32[72,128]{1,0:T(8,128)} %get-tuple-element.51), channel_id=1, source_target_pairs={{96,0},{128,32},{160,64},{192,96},{224,128},{256,160},{288,192},{3... | collective-permute-start | bytes 110600 | tf_op jit(solution)/shard_map/ppermute | solution.py:602
  286.7 8.5 %collective-permute-start.10 = (f32[72,128]{1,0:T(8,128)}, f32[72,128]{1,0:T(8,128)S(1)}, u32[]{:S(2)}, u32[]{:S(2)}) collective-permute-start(f32[72,128]{1,0:T(8,128)} %get-tuple-element.51), channel_id=1, source_target_pairs={{64,0},{96,32},{128,64},{160,96},{192,128},{224,160},{256,192},{28... | collective-permute-start | bytes 110600 | tf_op jit(solution)/shard_map/ppermute | solution.py:602
  288.9 8.2 %collective-permute-start.9 = (f32[72,128]{1,0:T(8,128)}, f32[72,128]{1,0:T(8,128)S(1)}, u32[]{:S(2)}, u32[]{:S(2)}) collective-permute-start(f32[72,128]{1,0:T(8,128)} %get-tuple-element.51), channel_id=1, source_target_pairs={{32,0},{64,32},{96,64},{128,96},{160,128},{192,160},{224,192},{256... | collective-permute-start | bytes 110600 | tf_op jit(solution)/shard_map/ppermute | solution.py:602
  290.9 6.2 %copy-start.14 = (f32[72,128]{1,0:T(8,128)}, f32[72,128]{1,0:T(8,128)S(1)}, u32[]{:S(2)}) copy-start(f32[72,128]{1,0:T(8,128)S(1)} %collective-permute-done.12.m4_ref) | copy-start | bytes 110596
  291.3 5.8 %copy-start.15 = (f32[72,128]{1,0:T(8,128)}, f32[72,128]{1,0:T(8,128)S(1)}, u32[]{:S(2)}) copy-start(f32[72,128]{1,0:T(8,128)S(1)} %collective-permute-done.11.m3_ref) | copy-start | bytes 110596
  295.1 1.9 copy-start.16
  297.1 0.6 copy-start.17
  297.7 35.6 %copy-start.4 = (f32[2,128]{1,0:T(2,128)S(1)}, f32[2,128]{1,0:T(2,128)}, u32[]{:S(2)}) copy-start(f32[2,128]{1,0:T(2,128)} %copy-done.3) | copy-start | bytes 3076
Sparse Core Ops, SparseCore 0:
  11.0 67.7 all-gather.2
  81.8 77.1 all-gather.4

commit v6 on v5

--- a/solution.py
+++ b/solution.py
@@ -337,6 +337,24 @@
     lax.fori_loop(0, FF // 256, matmul, 0)
 
 
+EXPERT_SPECS = [VM, VM, HBM, HBM, HBM, HBM]
+EXPERT_SCRATCH = [
+    pltpu.VMEM((SLOTS, WIDTH), f32),
+    pltpu.VMEM((SLOTS, WIDTH), f32),
+    pltpu.VMEM((SLOTS, 2 * FF), bf16),
+    pltpu.VMEM((WIDTH, 2 * FF), bf16),
+    pltpu.VMEM((SLOTS, LANES), f32),
+    pltpu.VMEM((SLOTS, WIDTH), bf16),
+    pltpu.VMEM((SLOTS, FF), f32),
+    pltpu.VMEM((SLOTS, WIDTH), bf16),
+    pltpu.VMEM((SLOTS, FF), bf16),
+    pltpu.VMEM((ROWS, LANES), bf16),
+    pltpu.SemaphoreType.DMA((4,)),
+    pltpu.SemaphoreType.DMA,
+    pltpu.SemaphoreType.DMA((4,)),
+]
+
+
 def expert_kernel(
     rows_ref,
     gain_ref,
@@ -345,8 +363,8 @@
     dhid_hbm,
     in_hbm,
     msg_hbm,
-    normed_hbm,
     hidden_hbm,
+    rscale_out_ref,
     y_ref,
     scaled_ref,
     dcat_ref,
@@ -354,11 +372,11 @@
     first_ref,
     grad_ref,
     dhid_ref,
-    normed_ref,
+    gained_ref,
     hidden_ref,
     msg_ref,
     fetch_sems,
-    store_sems,
+    store_sem,
     msg_sems,
 ):
     fetches = [
@@ -374,13 +392,13 @@
     ]
     for fetch in fetches:
         fetch.start()
-    keep_normed = pltpu.make_async_copy(normed_ref, normed_hbm, store_sems.at[0])
-    keep_hidden = pltpu.make_async_copy(hidden_ref, hidden_hbm, store_sems.at[1])
+    keep_hidden = pltpu.make_async_copy(hidden_ref, hidden_hbm, store_sem)
 
     def unpack(k, squares):
         lanes = pl.ds(pl.multiple_of(k * LANES, LANES), LANES)
         y = rows_ref[pl.ds(pl.multiple_of(k * SLOTS, SLOTS), SLOTS), :].astype(f32)
         y_ref[:, lanes] = y
+        gained_ref[:, lanes] = (y * gain_ref[:, lanes]).astype(bf16)
         return squares + y * y
 
     squares = lax.fori_loop(0, FBLOCKS, unpack, jnp.zeros((SLOTS, LANES), f32), unroll=2)
@@ -388,21 +406,16 @@
     rscale = lax.rsqrt(mean + 1e-06)
     rscale_b = jnp.broadcast_to(rscale, (SLOTS, LANES))
 
-    def scale(k, carry):
-        lanes = pl.ds(pl.multiple_of(k * LANES, LANES), LANES)
-        normed_ref[:, lanes] = (y_ref[:, lanes] * rscale_b * gain_ref[:, lanes]).astype(bf16)
-        return carry
-
-    lax.fori_loop(0, FBLOCKS, scale, 0, unroll=4)
-    keep_normed.start()
+    rscale_out_ref[...] = rscale_b
+    rscale2 = jnp.concatenate([rscale_b, rscale_b], axis=1)
     fetches[0].wait()
     fetches[1].wait()
 
     def project(i, carry):
         lanes = pl.ds(pl.multiple_of(i * 256, 256), 256)
         lanes_up = pl.ds(pl.multiple_of(FF + i * 256, 256), 256)
-        gate = dot(normed_ref[...], in_ref[:, lanes])
-        up = dot(normed_ref[...], in_ref[:, lanes_up])
+        gate = rscale2 * dot(gained_ref[...], in_ref[:, lanes])
+        up = rscale2 * dot(gained_ref[...], in_ref[:, lanes_up])
         sigmoid = 1.0 / (1.0 + jnp.exp(-gate))
         swish = gate * sigmoid
         hidden_ref[:, lanes] = (swish * up).astype(bf16)
@@ -427,7 +440,7 @@
         product = scaled * y_ref[:, lanes]
         return acc + product[:, :LANES] + product[:, LANES:]
 
-    acc = lax.fori_loop(0, WIDTH // 256, back, jnp.zeros((SLOTS, LANES), f32), unroll=2)
+    acc = lax.fori_loop(0, WIDTH // 256, back, jnp.zeros((SLOTS, LANES), f32), unroll=8)
     mean_grad = jnp.sum(acc, axis=1, keepdims=True) * (1.0 / WIDTH)
     pull = jnp.broadcast_to(rscale * rscale * rscale * mean_grad, (SLOTS, LANES))
 
@@ -444,14 +457,16 @@
             pltpu.make_async_copy(msg_ref.at[rows, :], msg_hbm.at[rows, :], msg_sems.at[part])
         )
         sends[-1].start()
-    for copy in (keep_normed, keep_hidden, *sends):
+    for copy in (keep_hidden, *sends):
         copy.wait()
 
 
 def expert_out_kernel(
     expert_ref,
     hidden_ref,
-    normed_ref,
+    rows_ref,
+    rscale_ref,
+    gain_ref,
     weight_ref,
     first_ref,
     out_hbm,
@@ -466,17 +481,18 @@
     core = lax.rem(expert_ref[0], 2)
     weight = weight_ref[...]
     weight2 = jnp.concatenate([weight, weight], axis=1)
-    first = first_ref[...]
-    first2 = jnp.concatenate([first, first], axis=1)
+    first = first_ref[...] * rscale_ref[...]
     fetch.wait()
 
     def matmul(i, carry):
         lanes = pl.ds(pl.multiple_of(i * 256, 256), 256)
         result = dot_last(hidden_ref[...], out_ref[lanes, :])
-        result = weight2 * result + first2 * normed_ref[:, lanes].astype(f32)
+        result = weight2 * result
         for half in range(2):
-            part = result[:, half * LANES : (half + 1) * LANES]
             fb = 2 * i + half
+            y = rows_ref[pl.ds(pl.multiple_of(fb * SLOTS, SLOTS), SLOTS), :].astype(f32)
+            gain = gain_ref[:, pl.ds(pl.multiple_of(fb * LANES, LANES), LANES)]
+            part = result[:, half * LANES : (half + 1) * LANES] + first * (y * gain)
             for par in range(2):
                 for c in range(CAP):
                     at = (par * CAP + c) * PAIRS
@@ -526,7 +542,7 @@
         out_ref[pl.ds(at, LANES), :] = dot_first(rows, select).astype(bf16)
         return carry
 
-    lax.fori_loop(0, FBLOCKS, step, 0, unroll=4)
+    lax.fori_loop(0, FBLOCKS, step, 0, unroll=8)
 
 
 def slot_sums_kernel(core_ref, rows_ref, rank_ref, own_ref, their_ref, wide_ref):
@@ -629,10 +645,15 @@
 ):
     me_ctx = lax.axis_index("ctx")
     me_exp = lax.axis_index("exp")
-    wide = pltpu.VMEM((ROWS, LANES), f32)
+    wide = pltpu.VMEM((ROWS + SLOTS, LANES), f32)
     ids_own = expert_ids.T.astype(f32)
-    tokens_own = jnp.concatenate([ids_own, route_weights.T], axis=0)
-    tokens_sent = jnp.broadcast_to(tokens_own[None], (EXPERTS, 4, LANES))
+    tokens_sent = jnp.concatenate(
+        [
+            jnp.broadcast_to(ids_own[None], (EXPERTS, 2, LANES)),
+            jnp.broadcast_to(route_weights.T[None], (EXPERTS, 2, LANES)),
+        ],
+        axis=1,
+    )
     tokens_sent, expert_in, expert_out, out_grad, ids_own = lax.optimization_barrier(
         (tokens_sent, expert_in, expert_out, out_grad, ids_own)
     )
@@ -660,7 +681,7 @@
     weight_out = lax.all_gather(expert_out, "ctx", axis=1, tiled=True)[0]
     rt, dt, message = call(
         tables_kernel,
-        [((CHUNKS * 8, LANES), f32), ((CHUNKS * 8, LANES), f32), ((HP + 8, LANES), f32)],
+        [((CHUNKS * 8 + 8, LANES), f32), ((CHUNKS * 8 + 8, LANES), f32), ((HP + 8, LANES), f32)],
         (
             doc_lengths,
             (me_ctx * SEQ).astype(i32).reshape(1),
@@ -712,42 +733,37 @@
         name="hidden_grad",
         vmem=VMEM_PART,
     )
-    back_out_rows, normed, hidden = call(
+    back_out_rows, hidden, rscale = call(
         expert_kernel,
         [
             ((ROWS, LANES), bf16),
-            ((SLOTS, WIDTH), bf16),
             ((SLOTS, FF), bf16),
+            ((SLOTS, LANES), f32),
         ],
         (y_in_rows, norm_gain.reshape(1, WIDTH), slot_first, grad_slots, d_hidden, weight_in),
-        [VM, VM, HBM, HBM, HBM, HBM],
-        [
-            pltpu.VMEM((SLOTS, WIDTH), f32),
-            pltpu.VMEM((SLOTS, WIDTH), f32),
-            pltpu.VMEM((SLOTS, 2 * FF), bf16),
-            pltpu.VMEM((WIDTH, 2 * FF), bf16),
-            pltpu.VMEM((SLOTS, LANES), f32),
-            pltpu.VMEM((SLOTS, WIDTH), bf16),
-            pltpu.VMEM((SLOTS, FF), f32),
-            pltpu.VMEM((SLOTS, WIDTH), bf16),
-            pltpu.VMEM((SLOTS, FF), bf16),
-            pltpu.VMEM((ROWS, LANES), bf16),
-            pltpu.SemaphoreType.DMA((4,)),
-            pltpu.SemaphoreType.DMA((2,)),
-            pltpu.SemaphoreType.DMA((4,)),
-        ],
+        EXPERT_SPECS,
+        EXPERT_SCRATCH,
         flops=8 * SLOTS * FF * WIDTH,
         moved=14 << 20,
         name="expert",
-        out_specs=(HBM, HBM, HBM),
+        out_specs=(HBM, HBM, VM),
     )
     back_in_rows = exchanged_by_core(back_out_rows)
 
     own_rows, their_rows = call(
         expert_out_kernel,
         [((ROWS // 2, LANES), bf16)] * 2,
-        (me, hidden, normed, slot_weight, slot_first, weight_out),
-        [SM, VM, VM, VM, VM, HBM],
+        (
+            me,
+            hidden,
+            y_in_rows,
+            rscale,
+            norm_gain.reshape(1, WIDTH),
+            slot_weight,
+            slot_first,
+            weight_out,
+        ),
+        [SM] + [VM] * 6 + [HBM],
         [wide, pltpu.VMEM((WIDTH, FF), bf16), pltpu.SemaphoreType.DMA],
         flops=2 * SLOTS * FF * WIDTH,
         moved=8 << 20,

time: 345 us -> 344 us (level)
  no operation moved by 1% of the time
where the time goes in v6:
time: 344 us; the launch traced here: 343 us
  waiting for transfers between devices  165 us (48%)
  starting transfers between devices  78.2 us (23%)
  Pallas kernels  71.9 us (21%)
  between operations  14.4 us (4%)
  local copies, waits for them, and re-layouts  9.67 us (3%)
  other arithmetic  3.67 us (1%)
    all_to_all x4, waiting for transfers between devices, exchanged_by_core(): lax.all_to_all(blocks, 'exp', split_axis=0, concat_axis=0, tiled=True, ax...  143 us
    pallas_call x11, Pallas kernels, call(): pl.pallas_call(kernel, out_shape=tuple((jax.ShapeDtypeStruct(shape, kind)...  71.9 us
    all_to_all x4, starting transfers between devices, exchanged_by_core(): lax.all_to_all(blocks, 'exp', split_axis=0, concat_axis=0, tiled=True, ax...  29.9 us
    ppermute x8, starting transfers between devices, sent_along(): return lax.ppermute(value, 'ctx', pairs)  22.8 us
    all_to_all x1, starting transfers between devices, per_device(): tokens = lax.all_to_all(tokens_sent, 'exp', 0, 0, tiled=True)  15.6 us
    ppermute x5, starting transfers between devices, from_other_core(): return lax.ppermute(value, 'exp', [(i, i ^ 1) for i in range(EXPERTS)])  9.84 us
    ppermute x8, waiting for transfers between devices, sent_along(): return lax.ppermute(value, 'ctx', pairs)  8.99 us
    unnamed x42, local copies, waits for them, and re-layouts  7.69 us
  transfers between devices with their start and end apart: 20, of which 14 were waited for; matrix products, arithmetic and copies ran while one was open for 1% of the time, Pallas kernels for 17%

profile of v6, /device:TPU:6, one launch (start us, length us, event | category | flops | bytes accessed | tf_op | source)
XLA Modules:
  0.0 342.5 jit_solution(9767168645365958154)
XLA Ops:
  7.2 0.0 all-gather.3.cloned.1.call-start
  7.2 0.7 convert_bitcast_fusion.own_ids_ref.ids_ref
  7.9 0.7 broadcast_in_dim.5
  8.6 0.7 pad_maximum_fusion.1
  9.3 0.0 all-gather.3.cloned.1.call-update
  9.3 0.0 all-gather.5.cloned.1.call-start
  9.3 0.7 all-gather.5.cloned.1.call-update
  10.0 1.9 collective-permute-start.6
  12.0 15.6 %all-to-all-start = ((f32[32,4,128]{2,1,0:T(4,128)}), f32[32,4,128]{2,1,0:T(4,128)S(1)}, u32[]{:S(2)}, u32[]{:S(2)}) async-start(f32[32,4,128]{2,1,0:T(4,128)} %pad_maximum_fusion.1), calls=%async_computation | async-start | bytes 131072 | tf_op jit(solution)/shard_map/all_to_all | solution.py:660
  27.6 2.2 collective-permute-start.5
  29.8 0.8 collective-permute-done.5.their_ids_ref
  30.6 0.6 copy-done.19
  31.2 0.2 copy-done.8
  31.4 5.3 %grad_rows.1 = bf16[5120,128]{1,0:T(8,128)(2,1)} custom-call(s32[1]{0:T(128)} %bitcast.10.core_ref, f32[2,128]{1,0:T(2,128)} %copy-done.3, f32[2,128]{1,0:T(2,128)} %copy-done.19, bf16[2048,128]{1,0:T(8,128)(2,1)} %own_ref, bf16[2048,128]{1,0:T(8,128)(2,1)} %copy-done.8), custom_call_target="tpu_custom_call" | custom-call | flops 167772160 | bytes 4194304 | tf_op jit(solution)/shard_map/grad_rows/pallas_call | solution.py:94
  36.8 5.2 %all-to-all-done = f32[32,4,128]{2,1,0:T(4,128)S(1)} async-done(((f32[32,4,128]{2,1,0:T(4,128)}), f32[32,4,128]{2,1,0:T(4,128)S(1)}, u32[]{:S(2)}, u32[]{:S(2)}) %all-to-all-start) | async-done | bytes 65568 | tf_op jit(solution)/shard_map/all_to_all | solution.py:660
  42.0 6.8 %all-to-all-start.2 = ((bf16[16,320,128]{2,1,0:T(8,128)(2,1)}), bf16[16,320,128]{2,1,0:T(8,128)(2,1)S(1)}, u32[]{:S(2)}, u32[]{:S(2)}) async-start(bf16[16,320,128]{2,1,0:T(8,128)(2,1)} %bitcast.27), calls=%async_computation.2 | async-start | bytes 2621440 | tf_op jit(solution)/shard_map/all_to_all | solution.py:624
  48.8 0.6 reshape.57.decay_ref
  49.4 4.1 %shard_state.1 = (f32[264,128]{1,0:T(8,128)}, f32[264,128]{1,0:T(8,128)}, f32[72,128]{1,0:T(8,128)}) custom-call(s32[8]{0:T(128)} %docs_ref.1, s32[1]{0:T(128)} %bitcast.3.base_ref, f32[64,128]{1,0:T(8,128)} %reshape.57.decay_ref, bf16[64,4096]{1,0:T(8,128)(2,1)} %x_ref.3, bf16[128,4096]{1,0:T(8,128)(2,1)} %write_ref.5), custom_call_target="tpu_custom_call" | custom-call | flops 67108864 | bytes 3145728 | tf_op jit(solution)/shard_map/shard_state/pallas_call | solution.py:94
  53.5 3.5 %collective-permute-start.3 = (f32[72,128]{1,0:T(8,128)}, f32[72,128]{1,0:T(8,128)S(1)}, u32[]{:S(2)}, u32[]{:S(2)}) collective-permute-start(f32[72,128]{1,0:T(8,128)} %get-tuple-element.30), channel_id=1, source_target_pairs={{0,128},{32,160},{64,192},{96,224},{128,256},{160,288},{192,320},{... | collective-permute-start | bytes 110600 | tf_op jit(solution)/shard_map/ppermute | solution.py:618
  57.0 3.8 %collective-permute-start.2 = (f32[72,128]{1,0:T(8,128)}, f32[72,128]{1,0:T(8,128)S(1)}, u32[]{:S(2)}, u32[]{:S(2)}) collective-permute-start(f32[72,128]{1,0:T(8,128)} %get-tuple-element.30), channel_id=1, source_target_pairs={{0,96},{32,128},{64,160},{96,192},{128,224},{160,256},{192,288},{2... | collective-permute-start | bytes 110600 | tf_op jit(solution)/shard_map/ppermute | solution.py:618
  60.8 3.7 %collective-permute-start.1 = (f32[72,128]{1,0:T(8,128)}, f32[72,128]{1,0:T(8,128)S(1)}, u32[]{:S(2)}, u32[]{:S(2)}) collective-permute-start(f32[72,128]{1,0:T(8,128)} %get-tuple-element.30), channel_id=1, source_target_pairs={{0,64},{32,96},{64,128},{96,160},{128,192},{160,224},{192,256},{22... | collective-permute-start | bytes 110600 | tf_op jit(solution)/shard_map/ppermute | solution.py:618
  64.5 4.0 %collective-permute-start = (f32[72,128]{1,0:T(8,128)}, f32[72,128]{1,0:T(8,128)S(1)}, u32[]{:S(2)}, u32[]{:S(2)}) collective-permute-start(f32[72,128]{1,0:T(8,128)} %get-tuple-element.30), channel_id=1, source_target_pairs={{0,32},{32,64},{64,96},{96,128},{128,160},{160,192},{192,224},{224... | collective-permute-start | bytes 110600 | tf_op jit(solution)/shard_map/ppermute | solution.py:618
  68.6 0.3 collective-permute-done.1.m2_ref
  68.9 2.4 collective-permute-done.m1_ref
  71.3 0.6 copy-done.17
  71.9 11.0 %mixer_forward.1 = (bf16[64,4096]{1,0:T(8,128)(2,1)}, bf16[8192,128]{1,0:T(8,128)(2,1)}) custom-call(f32[72,128]{1,0:T(8,128)} %copy-done.17, f32[72,128]{1,0:T(8,128)} %copy-done.16, f32[72,128]{1,0:T(8,128)} %copy-done.15, f32[72,128]{1,0:T(8,128)} %copy-done.14, f32[264,128]{1,0:T(8,128)} %get-tuple-element.31.rt_ref, bf16[64,4096]{1,0:T(8,128)(2,1)} %x_ref.3, ...), custom_call_target="tpu_custom_call" | custom-call | flops 268435456 | bytes 9437184 | tf_op jit(solution)/shard_map/mixer_forward/pallas_call | solution.py:94
  82.9 1.9 collective-permute-start.4
  84.8 0.6 copy.15
  85.5 1.4 collective-permute-done.4.their_ref
  86.9 0.8 copy-done.20
  87.7 8.2 %dispatch.1 = (bf16[5120,128]{1,0:T(8,128)(2,1)}, f32[512,128]{1,0:T(8,128)}, f32[320,128]{1,0:T(8,128)}, f32[320,128]{1,0:T(8,128)}) custom-call(s32[1]{0:T(128)} %bitcast.expert_ref, bf16[64,4096]{1,0:T(8,128)(2,1)} %get-tuple-element.32.own_ref, bf16[64,4096]{1,0:T(8,128)(2,1)} %copy-done.20, f32[4,32,128]{2,1,0:T(8,128)} %bitcast.35), custom_call_target="tpu_custom_call" | custom-call | flops 335544320 | bytes 4194304 | tf_op jit(solution)/shard_map/dispatch/pallas_call | solution.py:94
  95.9 13.9 %all-to-all-done.2 = bf16[16,320,128]{2,1,0:T(8,128)(2,1)S(1)} async-done(((bf16[16,320,128]{2,1,0:T(8,128)(2,1)}), bf16[16,320,128]{2,1,0:T(8,128)(2,1)S(1)}, u32[]{:S(2)}, u32[]{:S(2)}) %all-to-all-start.2) | async-done | bytes 1310752 | tf_op jit(solution)/shard_map/all_to_all | solution.py:624
  109.8 8.6 %all-to-all-start.1 = ((bf16[16,320,128]{2,1,0:T(8,128)(2,1)}), bf16[16,320,128]{2,1,0:T(8,128)(2,1)S(1)}, u32[]{:S(2)}, u32[]{:S(2)}) async-start(bf16[16,320,128]{2,1,0:T(8,128)(2,1)} %bitcast.31), calls=%async_computation.1 | async-start | bytes 2621440 | tf_op jit(solution)/shard_map/all_to_all | solution.py:624
  118.4 0.0 all-gather.3.cloned.1.call-done
  118.4 3.5 %hidden_grad.1 = (bf16[320,2048]{1,0:T(8,128)(2,1)S(1)}, f32[320,768]{1,0:T(8,128)S(1)}) custom-call(bf16[5120,128]{1,0:T(8,128)(2,1)S(1)} %bitcast.24, f32[320,128]{1,0:T(8,128)S(1)} %copy-done.1, bf16[2048,768]{1,0:T(8,128)(2,1)} %bitcast.25), custom_call_target="tpu_custom_call" | custom-call | flops 1006632960 | bytes 8388608 | tf_op jit(solution)/shard_map/hidden_grad/pallas_call | solution.py:94
  122.0 1.1 copy-done.5
  123.0 1.0 copy-done.6
  124.0 55.3 %all-to-all-done.1 = bf16[16,320,128]{2,1,0:T(8,128)(2,1)S(1)} async-done(((bf16[16,320,128]{2,1,0:T(8,128)(2,1)}), bf16[16,320,128]{2,1,0:T(8,128)(2,1)S(1)}, u32[]{:S(2)}, u32[]{:S(2)}) %all-to-all-start.1) | async-done | bytes 1310752 | tf_op jit(solution)/shard_map/all_to_all | solution.py:624
  179.3 1.1 copy-done.7
  180.3 11.4 %expert.1 = (bf16[5120,128]{1,0:T(8,128)(2,1)}, bf16[320,768]{1,0:T(8,128)(2,1)}, f32[320,128]{1,0:T(8,128)}) custom-call(bf16[5120,128]{1,0:T(8,128)(2,1)} %bitcast.28, f32[1,2048]{1,0:T(1,128)} %bitcast.36, f32[320,128]{1,0:T(8,128)} %get-tuple-element.35.first_hbm.first_ref, bf16[320,2048]{1,0:T(8,128)(2,1)} %copy-done.5, f32[320,768]{1,0:T(8,128)} %copy-done.6, ...), custom_call_target="tpu_custom_call" | custom-call | flops 4026531840 | bytes 14680064 | tf_op jit(solution)/shard_map/expert/pallas_call | solution.py:94
  191.7 8.5 %all-to-all-start.4 = ((bf16[16,320,128]{2,1,0:T(8,128)(2,1)}), bf16[16,320,128]{2,1,0:T(8,128)(2,1)S(1)}, u32[]{:S(2)}, u32[]{:S(2)}) async-start(bf16[16,320,128]{2,1,0:T(8,128)(2,1)} %bitcast.30), calls=%async_computation.4 | async-start | bytes 2621440 | tf_op jit(solution)/shard_map/all_to_all | solution.py:624
  200.2 9.4 %expert_out.1 = (bf16[2560,128]{1,0:T(8,128)(2,1)}, bf16[2560,128]{1,0:T(8,128)(2,1)}) custom-call(s32[1]{0:T(128)} %bitcast.expert_ref, bf16[320,768]{1,0:T(8,128)(2,1)} %get-tuple-element.42.hidden_ref, bf16[5120,128]{1,0:T(8,128)(2,1)} %bitcast.29, f32[320,128]{1,0:T(8,128)} %get-tuple-element.43.rscale_ref, f32[1,2048]{1,0:T(1,128)} %bitcast.37, ...), custom_call_target="tpu_custom_call" | custom-call | flops 1006632960 | bytes 8388608 | tf_op jit(solution)/shard_map/expert_out/pallas_call | solution.py:94
  209.6 1.9 collective-permute-start.7
  211.5 2.3 collective-permute-done.7
  213.8 2.3 pad_maximum_fusion
  216.1 47.3 %all-to-all-done.4 = bf16[16,320,128]{2,1,0:T(8,128)(2,1)S(1)} async-done(((bf16[16,320,128]{2,1,0:T(8,128)(2,1)}), bf16[16,320,128]{2,1,0:T(8,128)(2,1)S(1)}, u32[]{:S(2)}, u32[]{:S(2)}) %all-to-all-start.4) | async-done | bytes 1310752 | tf_op jit(solution)/shard_map/all_to_all | solution.py:624
  263.4 6.0 %all-to-all-start.3 = ((bf16[16,320,128]{2,1,0:T(8,128)(2,1)}), bf16[16,320,128]{2,1,0:T(8,128)(2,1)S(1)}, u32[]{:S(2)}, u32[]{:S(2)}) async-start(bf16[16,320,128]{2,1,0:T(8,128)(2,1)} %pad_maximum_fusion), calls=%async_computation.3 | async-start | bytes 2621440 | tf_op jit(solution)/shard_map/all_to_all | solution.py:624
  269.5 3.2 slot_sums.1
  272.7 1.0 copy-done
  273.7 1.9 collective-permute-start.8
  275.6 1.9 collective-permute-done.8.their_ref
  277.5 0.8 copy-done.9
  278.3 4.2 %mixer_grad.1 = (bf16[64,4096]{1,0:T(8,128)(2,1)}, f32[72,128]{1,0:T(8,128)}) custom-call(f32[64,4096]{1,0:T(8,128)} %copy-done, bf16[64,4096]{1,0:T(8,128)(2,1)} %copy-done.9, bf16[128,4096]{1,0:T(8,128)(2,1)} %read_ref.5, f32[264,128]{1,0:T(8,128)} %get-tuple-element.50.dt_ref), custom_call_target="tpu_custom_call" | custom-call | flops 268435456 | bytes 6291456 | tf_op jit(solution)/shard_map/mixer_grad/pallas_call | solution.py:94
  282.5 1.3 collective-permute-start.12
  283.7 2.4 collective-permute-start.11
  286.1 2.2 collective-permute-start.10
  288.4 1.9 collective-permute-start.9
  290.3 0.4 collective-permute-done.11.m3_ref
  290.7 3.9 %collective-permute-done.10.m2_ref = f32[72,128]{1,0:T(8,128)S(1)} collective-permute-done((f32[72,128]{1,0:T(8,128)}, f32[72,128]{1,0:T(8,128)S(1)}, u32[]{:S(2)}, u32[]{:S(2)}) %collective-permute-start.10) | collective-permute-done | bytes 36896 | tf_op jit(solution)/shard_map/ppermute | solution.py:618
  294.6 1.9 collective-permute-done.9.m1_ref
  296.6 0.6 copy-done.13
  297.2 8.7 %mixer_backward.1 = bf16[64,4096]{1,0:T(8,128)(2,1)} custom-call(f32[72,128]{1,0:T(8,128)} %copy-done.13, f32[72,128]{1,0:T(8,128)} %copy-done.12, f32[72,128]{1,0:T(8,128)} %copy-done.11, f32[72,128]{1,0:T(8,128)} %copy-done.10, f32[264,128]{1,0:T(8,128)} %get-tuple-element.31.rt_ref, bf16[64,4096]{1,0:T(8,128)(2,1)} %get-tuple-element.52.grad_ref, ...), custom_call_target="tpu_custom_call" | custom-call | flops 268435456 | bytes 6291456 | tf_op jit(solution)/shard_map/mixer_backward/pallas_call | solution.py:94
  305.8 26.9 %all-to-all-done.3 = bf16[16,320,128]{2,1,0:T(8,128)(2,1)S(1)} async-done(((bf16[16,320,128]{2,1,0:T(8,128)(2,1)}), bf16[16,320,128]{2,1,0:T(8,128)(2,1)S(1)}, u32[]{:S(2)}, u32[]{:S(2)}) %all-to-all-start.3) | async-done | bytes 1310752 | tf_op jit(solution)/shard_map/all_to_all | solution.py:624
  332.7 2.9 combine.1
  (39 shorter events, 0.1 us)
Async XLA Ops:
  7.2 111.2 %all-gather.3.cloned.1.call-start = ((), (), s32[]{:S(2)}) async-start(), calls=%async_computation.5 | async-start | bytes 3342336 | tf_op jit(solution)/shard_map/all_gather | solution.py:681
  7.9 22.7 %copy-start.3 = (f32[2,128]{1,0:T(2,128)}, f32[2,128]{1,0:T(2,128)S(1)}, u32[]{:S(2)}) copy-start(f32[2,128]{1,0:T(2,128)S(1)} %convert_bitcast_fusion.own_ids_ref.ids_ref) | copy-start | bytes 3076
  9.3 170.0 %all-gather.5.cloned.1.call-start = ((), (), s32[]{:S(2)}) async-start(), calls=%async_computation.6 | async-start | bytes 6684672 | tf_op jit(solution)/shard_map/all_gather | solution.py:680
  10.0 20.6 %collective-permute-start.6 = (bf16[2048,128]{1,0:T(8,128)(2,1)}, bf16[2048,128]{1,0:T(8,128)(2,1)S(1)}, u32[]{:S(2)}, u32[]{:S(2)}) collective-permute-start(bf16[2048,128]{1,0:T(8,128)(2,1)} %own_ref), channel_id=1, source_target_pairs={{0,1},{1,0},{2,3},{3,2},{4,5},{5,4},{6,7},{7,6},{8,9},{9,8},{10,11... | collective-permute-start | bytes 1572872 | tf_op jit(solution)/shard_map/ppermute | solution.py:630
  12.0 30.0 %all-to-all-start = ((f32[32,4,128]{2,1,0:T(4,128)}), f32[32,4,128]{2,1,0:T(4,128)S(1)}, u32[]{:S(2)}, u32[]{:S(2)}) async-start(f32[32,4,128]{2,1,0:T(4,128)} %pad_maximum_fusion.1), calls=%async_computation | async-start | bytes 131072 | tf_op jit(solution)/shard_map/all_to_all | solution.py:660
  27.6 3.0 collective-permute-start.5
  30.6 0.6 copy-start.19
  30.6 0.8 copy-start.8
  42.0 6.8 %copy-start.18 = (f32[2,4096]{1,0:T(2,128)S(1)}, f32[2,4096]{1,0:T(2,128)}, u32[]{:S(2)}) copy-start(f32[2,4096]{1,0:T(2,128)} %param.14) | copy-start | bytes 98308
  42.0 67.8 %all-to-all-start.2 = ((bf16[16,320,128]{2,1,0:T(8,128)(2,1)}), bf16[16,320,128]{2,1,0:T(8,128)(2,1)S(1)}, u32[]{:S(2)}, u32[]{:S(2)}) async-start(bf16[16,320,128]{2,1,0:T(8,128)(2,1)} %bitcast.27), calls=%async_computation.2 | async-start | bytes 2621440 | tf_op jit(solution)/shard_map/all_to_all | solution.py:624
  53.5 15.0 %collective-permute-start.3 = (f32[72,128]{1,0:T(8,128)}, f32[72,128]{1,0:T(8,128)S(1)}, u32[]{:S(2)}, u32[]{:S(2)}) collective-permute-start(f32[72,128]{1,0:T(8,128)} %get-tuple-element.30), channel_id=1, source_target_pairs={{0,128},{32,160},{64,192},{96,224},{128,256},{160,288},{192,320},{... | collective-permute-start | bytes 110600 | tf_op jit(solution)/shard_map/ppermute | solution.py:618
  57.0 11.6 %collective-permute-start.2 = (f32[72,128]{1,0:T(8,128)}, f32[72,128]{1,0:T(8,128)S(1)}, u32[]{:S(2)}, u32[]{:S(2)}) collective-permute-start(f32[72,128]{1,0:T(8,128)} %get-tuple-element.30), channel_id=1, source_target_pairs={{0,96},{32,128},{64,160},{96,192},{128,224},{160,256},{192,288},{2... | collective-permute-start | bytes 110600 | tf_op jit(solution)/shard_map/ppermute | solution.py:618
  60.8 8.2 %collective-permute-start.1 = (f32[72,128]{1,0:T(8,128)}, f32[72,128]{1,0:T(8,128)S(1)}, u32[]{:S(2)}, u32[]{:S(2)}) collective-permute-start(f32[72,128]{1,0:T(8,128)} %get-tuple-element.30), channel_id=1, source_target_pairs={{0,64},{32,96},{64,128},{96,160},{128,192},{160,224},{192,256},{22... | collective-permute-start | bytes 110600 | tf_op jit(solution)/shard_map/ppermute | solution.py:618
  64.5 6.8 %collective-permute-start = (f32[72,128]{1,0:T(8,128)}, f32[72,128]{1,0:T(8,128)S(1)}, u32[]{:S(2)}, u32[]{:S(2)}) collective-permute-start(f32[72,128]{1,0:T(8,128)} %get-tuple-element.30), channel_id=1, source_target_pairs={{0,32},{32,64},{64,96},{96,128},{128,160},{160,192},{192,224},{224... | collective-permute-start | bytes 110600 | tf_op jit(solution)/shard_map/ppermute | solution.py:618
  68.5 2.8 copy-start.14
  68.6 2.8 copy-start.15
  68.9 2.4 copy-start.16
  71.3 0.6 copy-start.17
  82.9 4.0 %collective-permute-start.4 = (bf16[64,4096]{1,0:T(8,128)(2,1)}, bf16[64,4096]{1,0:T(8,128)(2,1)S(1)}, u32[]{:S(2)}, u32[]{:S(2)}) collective-permute-start(bf16[64,4096]{1,0:T(8,128)(2,1)} %get-tuple-element.32.own_ref), channel_id=1, source_target_pairs={{0,1},{1,0},{2,3},{3,2},{4,5},{5,4},{6,7},{7,6},{8,9},{9,8},{10,11... | collective-permute-start | bytes 1572872 | tf_op jit(solution)/shard_map/ppermute | solution.py:630
  86.9 0.8 copy-start.20
  109.8 8.6 %copy-start.1 = (f32[320,128]{1,0:T(8,128)S(1)}, f32[320,128]{1,0:T(8,128)}, u32[]{:S(2)}) copy-start(f32[320,128]{1,0:T(8,128)} %get-tuple-element.37.weight_ref) | copy-start | bytes 491524
  109.8 69.5 %all-to-all-start.1 = ((bf16[16,320,128]{2,1,0:T(8,128)(2,1)}), bf16[16,320,128]{2,1,0:T(8,128)(2,1)S(1)}, u32[]{:S(2)}, u32[]{:S(2)}) async-start(bf16[16,320,128]{2,1,0:T(8,128)(2,1)} %bitcast.31), calls=%async_computation.1 | async-start | bytes 2621440 | tf_op jit(solution)/shard_map/all_to_all | solution.py:624
  122.0 1.1 copy-start.5
  123.0 1.0 copy-start.6
  179.3 1.1 copy-start.7
  191.7 71.7 %all-to-all-start.4 = ((bf16[16,320,128]{2,1,0:T(8,128)(2,1)}), bf16[16,320,128]{2,1,0:T(8,128)(2,1)S(1)}, u32[]{:S(2)}, u32[]{:S(2)}) async-start(bf16[16,320,128]{2,1,0:T(8,128)(2,1)} %bitcast.30), calls=%async_computation.4 | async-start | bytes 2621440 | tf_op jit(solution)/shard_map/all_to_all | solution.py:624
  209.6 4.2 %collective-permute-start.7 = (bf16[2560,128]{1,0:T(8,128)(2,1)}, bf16[2560,128]{1,0:T(8,128)(2,1)S(1)}, u32[]{:S(2)}, u32[]{:S(2)}) collective-permute-start(bf16[2560,128]{1,0:T(8,128)(2,1)} %get-tuple-element.45), channel_id=1, source_target_pairs={{0,1},{1,0},{2,3},{3,2},{4,5},{5,4},{6,7},{7,6},{8,9},{9,8},{10,11... | collective-permute-start | bytes 1966088 | tf_op jit(solution)/shard_map/ppermute | solution.py:630
  216.1 53.4 %copy-start.2 = (f32[512,128]{1,0:T(8,128)S(1)}, f32[512,128]{1,0:T(8,128)}, u32[]{:S(2)}) copy-start(f32[512,128]{1,0:T(8,128)} %get-tuple-element.47.rank_ref) | copy-start | bytes 786436
  263.4 69.3 %all-to-all-start.3 = ((bf16[16,320,128]{2,1,0:T(8,128)(2,1)}), bf16[16,320,128]{2,1,0:T(8,128)(2,1)S(1)}, u32[]{:S(2)}, u32[]{:S(2)}) async-start(bf16[16,320,128]{2,1,0:T(8,128)(2,1)} %pad_maximum_fusion), calls=%async_computation.3 | async-start | bytes 2621440 | tf_op jit(solution)/shard_map/all_to_all | solution.py:624
  272.7 1.0 copy-start
  273.7 3.8 %collective-permute-start.8 = (bf16[64,4096]{1,0:T(8,128)(2,1)S(1)}, bf16[64,4096]{1,0:T(8,128)(2,1)S(1)}, u32[]{:S(2)}, u32[]{:S(2)}) collective-permute-start(bf16[64,4096]{1,0:T(8,128)(2,1)S(1)} %get-tuple-element.49), channel_id=1, source_target_pairs={{0,1},{1,0},{2,3},{3,2},{4,5},{5,4},{6,7},{7,6},{8,9},{9,8},{10,11... | collective-permute-start | bytes 1572872 | tf_op jit(solution)/shard_map/ppermute | solution.py:630
  277.5 0.8 copy-start.9
  282.5 7.8 %collective-permute-start.12 = (f32[72,128]{1,0:T(8,128)}, f32[72,128]{1,0:T(8,128)S(1)}, u32[]{:S(2)}, u32[]{:S(2)}) collective-permute-start(f32[72,128]{1,0:T(8,128)} %get-tuple-element.51), channel_id=1, source_target_pairs={{128,0},{160,32},{192,64},{224,96},{256,128},{288,160},{320,192},{... | collective-permute-start | bytes 110600 | tf_op jit(solution)/shard_map/ppermute | solution.py:618
  283.7 7.0 %collective-permute-start.11 = (f32[72,128]{1,0:T(8,128)}, f32[72,128]{1,0:T(8,128)S(1)}, u32[]{:S(2)}, u32[]{:S(2)}) collective-permute-start(f32[72,128]{1,0:T(8,128)} %get-tuple-element.51), channel_id=1, source_target_pairs={{96,0},{128,32},{160,64},{192,96},{224,128},{256,160},{288,192},{3... | collective-permute-start | bytes 110600 | tf_op jit(solution)/shard_map/ppermute | solution.py:618
  286.1 8.5 %collective-permute-start.10 = (f32[72,128]{1,0:T(8,128)}, f32[72,128]{1,0:T(8,128)S(1)}, u32[]{:S(2)}, u32[]{:S(2)}) collective-permute-start(f32[72,128]{1,0:T(8,128)} %get-tuple-element.51), channel_id=1, source_target_pairs={{64,0},{96,32},{128,64},{160,96},{192,128},{224,160},{256,192},{28... | collective-permute-start | bytes 110600 | tf_op jit(solution)/shard_map/ppermute | solution.py:618
  288.4 8.2 %collective-permute-start.9 = (f32[72,128]{1,0:T(8,128)}, f32[72,128]{1,0:T(8,128)S(1)}, u32[]{:S(2)}, u32[]{:S(2)}) collective-permute-start(f32[72,128]{1,0:T(8,128)} %get-tuple-element.51), channel_id=1, source_target_pairs={{32,0},{64,32},{96,64},{128,96},{160,128},{192,160},{224,192},{256... | collective-permute-start | bytes 110600 | tf_op jit(solution)/shard_map/ppermute | solution.py:618
  290.3 6.2 %copy-start.10 = (f32[72,128]{1,0:T(8,128)}, f32[72,128]{1,0:T(8,128)S(1)}, u32[]{:S(2)}) copy-start(f32[72,128]{1,0:T(8,128)S(1)} %collective-permute-done.12.m4_ref) | copy-start | bytes 110596
  290.7 5.8 %copy-start.11 = (f32[72,128]{1,0:T(8,128)}, f32[72,128]{1,0:T(8,128)S(1)}, u32[]{:S(2)}) copy-start(f32[72,128]{1,0:T(8,128)S(1)} %collective-permute-done.11.m3_ref) | copy-start | bytes 110596
  294.6 1.9 copy-start.12
  296.5 0.6 copy-start.13
  297.2 35.5 %copy-start.4 = (f32[2,128]{1,0:T(2,128)S(1)}, f32[2,128]{1,0:T(2,128)}, u32[]{:S(2)}) copy-start(f32[2,128]{1,0:T(2,128)} %copy-done.3) | copy-start | bytes 3076
Sparse Core Ops, SparseCore 0:
  11.0 67.7 all-gather.2
  81.8 77.1 all-gather.4

commit v7 on v6

--- a/solution.py
+++ b/solution.py
@@ -308,7 +308,7 @@
 def arrived_grad_kernel(
     rows_ref, weight_ref, out_hbm, grad_ref, dhid_ref, wide_ref, scaled_ref, out_ref, sem
 ):
-    fetch = pltpu.make_async_copy(out_hbm, out_ref, sem)
+    fetch = pltpu.make_async_copy(out_hbm.at[:, pl.ds(2 * FF, FF)], out_ref, sem)
     fetch.start()
     round_rows(wide_ref, rows_ref)
 
@@ -383,7 +383,7 @@
         pltpu.make_async_copy(src, dst, fetch_sems.at[i])
         for i, (src, dst) in enumerate(
             (
-                (in_hbm, in_ref),
+                (in_hbm.at[:, pl.ds(0, 2 * FF)], in_ref),
                 (dhid_hbm, dhid_ref),
                 (grad_hbm, grad_ref),
                 (first_hbm, first_ref),
@@ -476,7 +476,7 @@
     out_ref,
     sem,
 ):
-    fetch = pltpu.make_async_copy(out_hbm, out_ref, sem)
+    fetch = pltpu.make_async_copy(out_hbm.at[:, pl.ds(2 * FF, FF)], out_ref, sem)
     fetch.start()
     core = lax.rem(expert_ref[0], 2)
     weight = weight_ref[...]
@@ -675,10 +675,12 @@
         moved=4 << 20,
         name="grad_rows",
     )
+
     grad_in_rows = exchanged_by_core(grad_out_rows)
-
-    weight_in = lax.all_gather(expert_in, "ctx", axis=1, tiled=True)[0]
-    weight_out = lax.all_gather(expert_out, "ctx", axis=1, tiled=True)[0]
+    weights = lax.all_gather(
+        jnp.concatenate([expert_in, expert_out], axis=2), "ctx", axis=1, tiled=True
+    )[0]
+
     rt, dt, message = call(
         tables_kernel,
         [((CHUNKS * 8 + 8, LANES), f32), ((CHUNKS * 8 + 8, LANES), f32), ((HP + 8, LANES), f32)],
@@ -725,7 +727,7 @@
     grad_slots, d_hidden = call(
         arrived_grad_kernel,
         [((SLOTS, WIDTH), bf16), ((SLOTS, FF), f32)],
-        (grad_in_rows, slot_weight, weight_out),
+        (grad_in_rows, slot_weight, weights),
         [VM, VM, HBM],
         [wide, pltpu.VMEM((SLOTS, WIDTH), bf16), pltpu.VMEM((WIDTH, FF), bf16), pltpu.SemaphoreType.DMA],
         flops=2 * SLOTS * FF * WIDTH,
@@ -740,7 +742,7 @@
             ((SLOTS, FF), bf16),
             ((SLOTS, LANES), f32),
         ],
-        (y_in_rows, norm_gain.reshape(1, WIDTH), slot_first, grad_slots, d_hidden, weight_in),
+        (y_in_rows, norm_gain.reshape(1, WIDTH), slot_first, grad_slots, d_hidden, weights),
         EXPERT_SPECS,
         EXPERT_SCRATCH,
         flops=8 * SLOTS * FF * WIDTH,
@@ -761,7 +763,7 @@
             norm_gain.reshape(1, WIDTH),
             slot_weight,
             slot_first,
-            weight_out,
+            weights,
         ),
         [SM] + [VM] * 6 + [HBM],
         [wide, pltpu.VMEM((WIDTH, FF), bf16), pltpu.SemaphoreType.DMA],

time: 344 us -> 344 us (level)
  transfers between devices with their start and end apart: 20 -> 19, of which waited for: 14 -> 14; matrix products, arithmetic and copies ran while one was open for 1% -> 1% of each run, Pallas kernels for 17% -> 17%
where the time goes in v7:
time: 344 us; the launch traced here: 343 us
  waiting for transfers between devices  166 us (48%)
  starting transfers between devices  75.9 us (22%)
  Pallas kernels  72.1 us (21%)
  between operations  14.4 us (4%)
  local copies, waits for them, and re-layouts  8.63 us (3%)
  other arithmetic  5.69 us (2%)
    all_to_all x4, waiting for transfers between devices, exchanged_by_core(): lax.all_to_all(blocks, 'exp', split_axis=0, concat_axis=0, tiled=True, ax...  146 us
    pallas_call x11, Pallas kernels, call(): pl.pallas_call(kernel, out_shape=tuple((jax.ShapeDtypeStruct(shape, kind)...  72.1 us
    all_to_all x4, starting transfers between devices, exchanged_by_core(): lax.all_to_all(blocks, 'exp', split_axis=0, concat_axis=0, tiled=True, ax...  27.7 us
    ppermute x8, starting transfers between devices, sent_along(): return lax.ppermute(value, 'ctx', pairs)  22.8 us
    all_to_all x1, starting transfers between devices, per_device(): tokens = lax.all_to_all(tokens_sent, 'exp', 0, 0, tiled=True)  15.6 us
    ppermute x5, starting transfers between devices, from_other_core(): return lax.ppermute(value, 'exp', [(i, i ^ 1) for i in range(EXPERTS)])  9.84 us
    ppermute x8, waiting for transfers between devices, sent_along(): return lax.ppermute(value, 'ctx', pairs)  8.98 us
  transfers between devices with their start and end apart: 19, of which 14 were waited for; matrix products, arithmetic and copies ran while one was open for 1% of the time, Pallas kernels for 17%

profile of v7, /device:TPU:6, one launch (start us, length us, event | category | flops | bytes accessed | tf_op | source)
XLA Modules:
  0.0 342.9 jit_solution(10807096783455578255)
XLA Ops:
  7.2 0.0 copy-start.7
  7.2 0.0 all-gather.2.cloned.1.call-start
  7.2 0.7 convert_bitcast_fusion.own_ids_ref.ids_ref
  8.0 0.7 broadcast_in_dim.5
  8.7 0.7 pad_maximum_fusion.2
  9.3 2.0 pad_maximum_fusion.1
  11.3 0.0 all-gather.2.cloned.1.call-update
  11.3 1.9 collective-permute-start.6
  13.2 15.6 %all-to-all-start = ((f32[32,4,128]{2,1,0:T(4,128)}), f32[32,4,128]{2,1,0:T(4,128)S(1)}, u32[]{:S(2)}, u32[]{:S(2)}) async-start(f32[32,4,128]{2,1,0:T(4,128)} %pad_maximum_fusion.2), calls=%async_computation | async-start | bytes 131072 | tf_op jit(solution)/shard_map/all_to_all | solution.py:660
  28.8 2.2 collective-permute-start.5
  31.0 0.8 collective-permute-done.5.their_ids_ref
  31.9 0.0 collective-permute-done.6.their_ref
  31.9 0.6 copy-done.19
  32.5 0.2 copy-done.8
  32.7 5.4 %grad_rows.1 = bf16[5120,128]{1,0:T(8,128)(2,1)} custom-call(s32[1]{0:T(128)} %bitcast.10.core_ref, f32[2,128]{1,0:T(2,128)} %copy-done.3, f32[2,128]{1,0:T(2,128)} %copy-done.19, bf16[2048,128]{1,0:T(8,128)(2,1)} %own_ref, bf16[2048,128]{1,0:T(8,128)(2,1)} %copy-done.8), custom_call_target="tpu_custom_call" | custom-call | flops 167772160 | bytes 4194304 | tf_op jit(solution)/shard_map/grad_rows/pallas_call | solution.py:94
  38.1 5.2 %all-to-all-done = f32[32,4,128]{2,1,0:T(4,128)S(1)} async-done(((f32[32,4,128]{2,1,0:T(4,128)}), f32[32,4,128]{2,1,0:T(4,128)S(1)}, u32[]{:S(2)}, u32[]{:S(2)}) %all-to-all-start) | async-done | bytes 65568 | tf_op jit(solution)/shard_map/all_to_all | solution.py:660
  43.3 6.9 %all-to-all-start.2 = ((bf16[16,320,128]{2,1,0:T(8,128)(2,1)}), bf16[16,320,128]{2,1,0:T(8,128)(2,1)S(1)}, u32[]{:S(2)}, u32[]{:S(2)}) async-start(bf16[16,320,128]{2,1,0:T(8,128)(2,1)} %bitcast.27), calls=%async_computation.2 | async-start | bytes 2621440 | tf_op jit(solution)/shard_map/all_to_all | solution.py:624
  50.1 0.6 reshape.57.decay_ref
  50.8 4.1 %shard_state.1 = (f32[264,128]{1,0:T(8,128)}, f32[264,128]{1,0:T(8,128)}, f32[72,128]{1,0:T(8,128)}) custom-call(s32[8]{0:T(128)} %docs_ref.1, s32[1]{0:T(128)} %bitcast.3.base_ref, f32[64,128]{1,0:T(8,128)} %reshape.57.decay_ref, bf16[64,4096]{1,0:T(8,128)(2,1)} %x_ref.3, bf16[128,4096]{1,0:T(8,128)(2,1)} %write_ref.5), custom_call_target="tpu_custom_call" | custom-call | flops 67108864 | bytes 3145728 | tf_op jit(solution)/shard_map/shard_state/pallas_call | solution.py:94
  54.9 3.5 %collective-permute-start.3 = (f32[72,128]{1,0:T(8,128)}, f32[72,128]{1,0:T(8,128)S(1)}, u32[]{:S(2)}, u32[]{:S(2)}) collective-permute-start(f32[72,128]{1,0:T(8,128)} %get-tuple-element.30), channel_id=1, source_target_pairs={{0,128},{32,160},{64,192},{96,224},{128,256},{160,288},{192,320},{... | collective-permute-start | bytes 110600 | tf_op jit(solution)/shard_map/ppermute | solution.py:618
  58.3 3.7 %collective-permute-start.2 = (f32[72,128]{1,0:T(8,128)}, f32[72,128]{1,0:T(8,128)S(1)}, u32[]{:S(2)}, u32[]{:S(2)}) collective-permute-start(f32[72,128]{1,0:T(8,128)} %get-tuple-element.30), channel_id=1, source_target_pairs={{0,96},{32,128},{64,160},{96,192},{128,224},{160,256},{192,288},{2... | collective-permute-start | bytes 110600 | tf_op jit(solution)/shard_map/ppermute | solution.py:618
  62.1 3.7 %collective-permute-start.1 = (f32[72,128]{1,0:T(8,128)}, f32[72,128]{1,0:T(8,128)S(1)}, u32[]{:S(2)}, u32[]{:S(2)}) collective-permute-start(f32[72,128]{1,0:T(8,128)} %get-tuple-element.30), channel_id=1, source_target_pairs={{0,64},{32,96},{64,128},{96,160},{128,192},{160,224},{192,256},{22... | collective-permute-start | bytes 110600 | tf_op jit(solution)/shard_map/ppermute | solution.py:618
  65.8 4.0 %collective-permute-start = (f32[72,128]{1,0:T(8,128)}, f32[72,128]{1,0:T(8,128)S(1)}, u32[]{:S(2)}, u32[]{:S(2)}) collective-permute-start(f32[72,128]{1,0:T(8,128)} %get-tuple-element.30), channel_id=1, source_target_pairs={{0,32},{32,64},{64,96},{96,128},{128,160},{160,192},{192,224},{224... | collective-permute-start | bytes 110600 | tf_op jit(solution)/shard_map/ppermute | solution.py:618
  69.9 0.5 collective-permute-done.1.m2_ref
  70.4 2.2 collective-permute-done.m1_ref
  72.7 0.6 copy-done.17
  73.3 11.0 %mixer_forward.1 = (bf16[64,4096]{1,0:T(8,128)(2,1)}, bf16[8192,128]{1,0:T(8,128)(2,1)}) custom-call(f32[72,128]{1,0:T(8,128)} %copy-done.17, f32[72,128]{1,0:T(8,128)} %copy-done.16, f32[72,128]{1,0:T(8,128)} %copy-done.15, f32[72,128]{1,0:T(8,128)} %copy-done.14, f32[264,128]{1,0:T(8,128)} %get-tuple-element.31.rt_ref, bf16[64,4096]{1,0:T(8,128)(2,1)} %x_ref.3, ...), custom_call_target="tpu_custom_call" | custom-call | flops 268435456 | bytes 9437184 | tf_op jit(solution)/shard_map/mixer_forward/pallas_call | solution.py:94
  84.2 1.9 collective-permute-start.4
  86.2 0.6 copy.15
  86.8 1.4 collective-permute-done.4.their_ref
  88.2 0.8 copy-done.20
  89.0 8.3 %dispatch.1 = (bf16[5120,128]{1,0:T(8,128)(2,1)}, f32[512,128]{1,0:T(8,128)}, f32[320,128]{1,0:T(8,128)}, f32[320,128]{1,0:T(8,128)}) custom-call(s32[1]{0:T(128)} %bitcast.expert_ref, bf16[64,4096]{1,0:T(8,128)(2,1)} %get-tuple-element.32.own_ref, bf16[64,4096]{1,0:T(8,128)(2,1)} %copy-done.20, f32[4,32,128]{2,1,0:T(8,128)} %bitcast.33), custom_call_target="tpu_custom_call" | custom-call | flops 335544320 | bytes 4194304 | tf_op jit(solution)/shard_map/dispatch/pallas_call | solution.py:94
  97.3 13.8 %all-to-all-done.2 = bf16[16,320,128]{2,1,0:T(8,128)(2,1)S(1)} async-done(((bf16[16,320,128]{2,1,0:T(8,128)(2,1)}), bf16[16,320,128]{2,1,0:T(8,128)(2,1)S(1)}, u32[]{:S(2)}, u32[]{:S(2)}) %all-to-all-start.2) | async-done | bytes 1310752 | tf_op jit(solution)/shard_map/all_to_all | solution.py:624
  111.1 8.6 %all-to-all-start.1 = ((bf16[16,320,128]{2,1,0:T(8,128)(2,1)}), bf16[16,320,128]{2,1,0:T(8,128)(2,1)}, u32[]{:S(2)}, u32[]{:S(2)}) async-start(bf16[16,320,128]{2,1,0:T(8,128)(2,1)} %bitcast.29), calls=%async_computation.1 | async-start | bytes 2621440 | tf_op jit(solution)/shard_map/all_to_all | solution.py:624
  119.8 0.0 all-gather.2.cloned.1.call-done
  119.8 3.5 %hidden_grad.1 = (bf16[320,2048]{1,0:T(8,128)(2,1)S(1)}, f32[320,768]{1,0:T(8,128)S(1)}) custom-call(bf16[5120,128]{1,0:T(8,128)(2,1)S(1)} %bitcast.23, f32[320,128]{1,0:T(8,128)S(1)} %copy-done.1, bf16[2048,2304]{1,0:T(8,128)(2,1)} %bitcast.24), custom_call_target="tpu_custom_call" | custom-call | flops 1006632960 | bytes 8388608 | tf_op jit(solution)/shard_map/hidden_grad/pallas_call | solution.py:94
  123.4 1.1 copy-done.5
  124.4 0.9 copy-done.6
  125.4 57.6 %all-to-all-done.1 = bf16[16,320,128]{2,1,0:T(8,128)(2,1)} async-done(((bf16[16,320,128]{2,1,0:T(8,128)(2,1)}), bf16[16,320,128]{2,1,0:T(8,128)(2,1)}, u32[]{:S(2)}, u32[]{:S(2)}) %all-to-all-start.1) | async-done | bytes 1310752 | tf_op jit(solution)/shard_map/all_to_all | solution.py:624
  183.0 11.5 %expert.1 = (bf16[5120,128]{1,0:T(8,128)(2,1)}, bf16[320,768]{1,0:T(8,128)(2,1)}, f32[320,128]{1,0:T(8,128)}) custom-call(bf16[5120,128]{1,0:T(8,128)(2,1)} %bitcast.8.rows_ref, f32[1,2048]{1,0:T(1,128)} %bitcast.34, f32[320,128]{1,0:T(8,128)} %get-tuple-element.35.first_hbm.first_ref, bf16[320,2048]{1,0:T(8,128)(2,1)} %copy-done.5, f32[320,768]{1,0:T(8,128)} %copy-done.6, ...), custom_call_target="tpu_custom_call" | custom-call | flops 4026531840 | bytes 14680064 | tf_op jit(solution)/shard_map/expert/pallas_call | solution.py:94
  194.5 6.1 %all-to-all-start.4 = ((bf16[16,320,128]{2,1,0:T(8,128)(2,1)}), bf16[16,320,128]{2,1,0:T(8,128)(2,1)S(1)}, u32[]{:S(2)}, u32[]{:S(2)}) async-start(bf16[16,320,128]{2,1,0:T(8,128)(2,1)} %bitcast.28), calls=%async_computation.4 | async-start | bytes 2621440 | tf_op jit(solution)/shard_map/all_to_all | solution.py:624
  200.6 9.3 %expert_out.1 = (bf16[2560,128]{1,0:T(8,128)(2,1)}, bf16[2560,128]{1,0:T(8,128)(2,1)}) custom-call(s32[1]{0:T(128)} %bitcast.expert_ref, bf16[320,768]{1,0:T(8,128)(2,1)} %get-tuple-element.42.hidden_ref, bf16[5120,128]{1,0:T(8,128)(2,1)} %bitcast.8.rows_ref, f32[320,128]{1,0:T(8,128)} %get-tuple-element.43.rscale_ref, f32[1,2048]{1,0:T(1,128)} %bitcast.35, ...), custom_call_target="tpu_custom_call" | custom-call | flops 1006632960 | bytes 8388608 | tf_op jit(solution)/shard_map/expert_out/pallas_call | solution.py:94
  210.0 1.9 collective-permute-start.7
  211.9 2.3 collective-permute-done.7
  214.2 2.3 pad_maximum_fusion
  216.5 47.3 %all-to-all-done.4 = bf16[16,320,128]{2,1,0:T(8,128)(2,1)S(1)} async-done(((bf16[16,320,128]{2,1,0:T(8,128)(2,1)}), bf16[16,320,128]{2,1,0:T(8,128)(2,1)S(1)}, u32[]{:S(2)}, u32[]{:S(2)}) %all-to-all-start.4) | async-done | bytes 1310752 | tf_op jit(solution)/shard_map/all_to_all | solution.py:624
  263.8 6.1 %all-to-all-start.3 = ((bf16[16,320,128]{2,1,0:T(8,128)(2,1)}), bf16[16,320,128]{2,1,0:T(8,128)(2,1)S(1)}, u32[]{:S(2)}, u32[]{:S(2)}) async-start(bf16[16,320,128]{2,1,0:T(8,128)(2,1)} %pad_maximum_fusion), calls=%async_computation.3 | async-start | bytes 2621440 | tf_op jit(solution)/shard_map/all_to_all | solution.py:624
  269.9 3.2 slot_sums.1
  273.2 1.0 copy-done
  274.2 1.9 collective-permute-start.8
  276.1 1.9 collective-permute-done.8.their_ref
  278.0 0.8 copy-done.9
  278.8 4.2 %mixer_grad.1 = (bf16[64,4096]{1,0:T(8,128)(2,1)}, f32[72,128]{1,0:T(8,128)}) custom-call(f32[64,4096]{1,0:T(8,128)} %copy-done, bf16[64,4096]{1,0:T(8,128)(2,1)} %copy-done.9, bf16[128,4096]{1,0:T(8,128)(2,1)} %read_ref.5, f32[264,128]{1,0:T(8,128)} %get-tuple-element.50.dt_ref), custom_call_target="tpu_custom_call" | custom-call | flops 268435456 | bytes 6291456 | tf_op jit(solution)/shard_map/mixer_grad/pallas_call | solution.py:94
  282.9 1.3 collective-permute-start.12
  284.2 2.5 collective-permute-start.11
  286.7 2.1 collective-permute-start.10
  288.8 1.9 collective-permute-start.9
  290.8 0.4 collective-permute-done.11.m3_ref
  291.2 4.0 %collective-permute-done.10.m2_ref = f32[72,128]{1,0:T(8,128)S(1)} collective-permute-done((f32[72,128]{1,0:T(8,128)}, f32[72,128]{1,0:T(8,128)S(1)}, u32[]{:S(2)}, u32[]{:S(2)}) %collective-permute-start.10) | collective-permute-done | bytes 36896 | tf_op jit(solution)/shard_map/ppermute | solution.py:618
  295.2 1.8 collective-permute-done.9.m1_ref
  297.0 0.6 copy-done.13
  297.6 8.7 %mixer_backward.1 = bf16[64,4096]{1,0:T(8,128)(2,1)} custom-call(f32[72,128]{1,0:T(8,128)} %copy-done.13, f32[72,128]{1,0:T(8,128)} %copy-done.12, f32[72,128]{1,0:T(8,128)} %copy-done.11, f32[72,128]{1,0:T(8,128)} %copy-done.10, f32[264,128]{1,0:T(8,128)} %get-tuple-element.31.rt_ref, bf16[64,4096]{1,0:T(8,128)(2,1)} %get-tuple-element.52.grad_ref, ...), custom_call_target="tpu_custom_call" | custom-call | flops 268435456 | bytes 6291456 | tf_op jit(solution)/shard_map/mixer_backward/pallas_call | solution.py:94
  306.3 26.8 %all-to-all-done.3 = bf16[16,320,128]{2,1,0:T(8,128)(2,1)S(1)} async-done(((bf16[16,320,128]{2,1,0:T(8,128)(2,1)}), bf16[16,320,128]{2,1,0:T(8,128)(2,1)S(1)}, u32[]{:S(2)}, u32[]{:S(2)}) %all-to-all-start.3) | async-done | bytes 1310752 | tf_op jit(solution)/shard_map/all_to_all | solution.py:624
  333.1 2.9 combine.1
  (37 shorter events, 0.1 us)
Async XLA Ops:
  7.2 4.1 %copy-start.7 = (bf16[2048,128]{1,0:T(8,128)(2,1)S(1)}, bf16[2048,128]{1,0:T(8,128)(2,1)}, u32[]{:S(2)}) copy-start(bf16[2048,128]{1,0:T(8,128)(2,1)} %own_ref) | copy-start | bytes 1572868
  7.2 112.6 %all-gather.2.cloned.1.call-start = ((), (), s32[]{:S(2)}) async-start(), calls=%async_computation.5 | async-start | bytes 10027008 | tf_op jit(solution)/shard_map/all_gather | solution.py:680
  8.0 23.9 %copy-start.3 = (f32[2,128]{1,0:T(2,128)}, f32[2,128]{1,0:T(2,128)S(1)}, u32[]{:S(2)}) copy-start(f32[2,128]{1,0:T(2,128)S(1)} %convert_bitcast_fusion.own_ids_ref.ids_ref) | copy-start | bytes 3076
  11.3 20.6 %collective-permute-start.6 = (bf16[2048,128]{1,0:T(8,128)(2,1)S(1)}, bf16[2048,128]{1,0:T(8,128)(2,1)S(1)}, u32[]{:S(2)}, u32[]{:S(2)}) collective-permute-start(bf16[2048,128]{1,0:T(8,128)(2,1)S(1)} %copy-done.7), channel_id=1, source_target_pairs={{0,1},{1,0},{2,3},{3,2},{4,5},{5,4},{6,7},{7,6},{8,9},{9,8},{10,11... | collective-permute-start | bytes 1572872 | tf_op jit(solution)/shard_map/ppermute | solution.py:630
  13.2 30.0 %all-to-all-start = ((f32[32,4,128]{2,1,0:T(4,128)}), f32[32,4,128]{2,1,0:T(4,128)S(1)}, u32[]{:S(2)}, u32[]{:S(2)}) async-start(f32[32,4,128]{2,1,0:T(4,128)} %pad_maximum_fusion.2), calls=%async_computation | async-start | bytes 131072 | tf_op jit(solution)/shard_map/all_to_all | solution.py:660
  28.8 3.0 collective-permute-start.5
  31.9 0.6 copy-start.19
  31.9 0.8 copy-start.8
  43.3 6.9 %copy-start.18 = (f32[2,4096]{1,0:T(2,128)S(1)}, f32[2,4096]{1,0:T(2,128)}, u32[]{:S(2)}) copy-start(f32[2,4096]{1,0:T(2,128)} %param.14) | copy-start | bytes 98308
  43.3 67.9 %all-to-all-start.2 = ((bf16[16,320,128]{2,1,0:T(8,128)(2,1)}), bf16[16,320,128]{2,1,0:T(8,128)(2,1)S(1)}, u32[]{:S(2)}, u32[]{:S(2)}) async-start(bf16[16,320,128]{2,1,0:T(8,128)(2,1)} %bitcast.27), calls=%async_computation.2 | async-start | bytes 2621440 | tf_op jit(solution)/shard_map/all_to_all | solution.py:624
  54.9 15.0 %collective-permute-start.3 = (f32[72,128]{1,0:T(8,128)}, f32[72,128]{1,0:T(8,128)S(1)}, u32[]{:S(2)}, u32[]{:S(2)}) collective-permute-start(f32[72,128]{1,0:T(8,128)} %get-tuple-element.30), channel_id=1, source_target_pairs={{0,128},{32,160},{64,192},{96,224},{128,256},{160,288},{192,320},{... | collective-permute-start | bytes 110600 | tf_op jit(solution)/shard_map/ppermute | solution.py:618
  58.3 11.5 %collective-permute-start.2 = (f32[72,128]{1,0:T(8,128)}, f32[72,128]{1,0:T(8,128)S(1)}, u32[]{:S(2)}, u32[]{:S(2)}) collective-permute-start(f32[72,128]{1,0:T(8,128)} %get-tuple-element.30), channel_id=1, source_target_pairs={{0,96},{32,128},{64,160},{96,192},{128,224},{160,256},{192,288},{2... | collective-permute-start | bytes 110600 | tf_op jit(solution)/shard_map/ppermute | solution.py:618
  62.1 8.3 %collective-permute-start.1 = (f32[72,128]{1,0:T(8,128)}, f32[72,128]{1,0:T(8,128)S(1)}, u32[]{:S(2)}, u32[]{:S(2)}) collective-permute-start(f32[72,128]{1,0:T(8,128)} %get-tuple-element.30), channel_id=1, source_target_pairs={{0,64},{32,96},{64,128},{96,160},{128,192},{160,224},{192,256},{22... | collective-permute-start | bytes 110600 | tf_op jit(solution)/shard_map/ppermute | solution.py:618
  65.8 6.8 %collective-permute-start = (f32[72,128]{1,0:T(8,128)}, f32[72,128]{1,0:T(8,128)S(1)}, u32[]{:S(2)}, u32[]{:S(2)}) collective-permute-start(f32[72,128]{1,0:T(8,128)} %get-tuple-element.30), channel_id=1, source_target_pairs={{0,32},{32,64},{64,96},{96,128},{128,160},{160,192},{192,224},{224... | collective-permute-start | bytes 110600 | tf_op jit(solution)/shard_map/ppermute | solution.py:618
  69.9 2.8 copy-start.14
  69.9 2.8 copy-start.15
  70.4 2.3 copy-start.16
  72.7 0.6 copy-start.17
  84.2 4.0 %collective-permute-start.4 = (bf16[64,4096]{1,0:T(8,128)(2,1)}, bf16[64,4096]{1,0:T(8,128)(2,1)S(1)}, u32[]{:S(2)}, u32[]{:S(2)}) collective-permute-start(bf16[64,4096]{1,0:T(8,128)(2,1)} %get-tuple-element.32.own_ref), channel_id=1, source_target_pairs={{0,1},{1,0},{2,3},{3,2},{4,5},{5,4},{6,7},{7,6},{8,9},{9,8},{10,11... | collective-permute-start | bytes 1572872 | tf_op jit(solution)/shard_map/ppermute | solution.py:630
  88.2 0.8 copy-start.20
  111.1 8.7 %copy-start.1 = (f32[320,128]{1,0:T(8,128)S(1)}, f32[320,128]{1,0:T(8,128)}, u32[]{:S(2)}) copy-start(f32[320,128]{1,0:T(8,128)} %get-tuple-element.37.weight_ref) | copy-start | bytes 491524
  111.1 71.9 %all-to-all-start.1 = ((bf16[16,320,128]{2,1,0:T(8,128)(2,1)}), bf16[16,320,128]{2,1,0:T(8,128)(2,1)}, u32[]{:S(2)}, u32[]{:S(2)}) async-start(bf16[16,320,128]{2,1,0:T(8,128)(2,1)} %bitcast.29), calls=%async_computation.1 | async-start | bytes 2621440 | tf_op jit(solution)/shard_map/all_to_all | solution.py:624
  123.4 1.1 copy-start.5
  124.4 1.0 copy-start.6
  194.5 69.3 %all-to-all-start.4 = ((bf16[16,320,128]{2,1,0:T(8,128)(2,1)}), bf16[16,320,128]{2,1,0:T(8,128)(2,1)S(1)}, u32[]{:S(2)}, u32[]{:S(2)}) async-start(bf16[16,320,128]{2,1,0:T(8,128)(2,1)} %bitcast.28), calls=%async_computation.4 | async-start | bytes 2621440 | tf_op jit(solution)/shard_map/all_to_all | solution.py:624
  210.0 4.2 %collective-permute-start.7 = (bf16[2560,128]{1,0:T(8,128)(2,1)}, bf16[2560,128]{1,0:T(8,128)(2,1)S(1)}, u32[]{:S(2)}, u32[]{:S(2)}) collective-permute-start(bf16[2560,128]{1,0:T(8,128)(2,1)} %get-tuple-element.45), channel_id=1, source_target_pairs={{0,1},{1,0},{2,3},{3,2},{4,5},{5,4},{6,7},{7,6},{8,9},{9,8},{10,11... | collective-permute-start | bytes 1966088 | tf_op jit(solution)/shard_map/ppermute | solution.py:630
  216.5 53.4 %copy-start.2 = (f32[512,128]{1,0:T(8,128)S(1)}, f32[512,128]{1,0:T(8,128)}, u32[]{:S(2)}) copy-start(f32[512,128]{1,0:T(8,128)} %get-tuple-element.47.rank_ref) | copy-start | bytes 786436
  263.8 69.2 %all-to-all-start.3 = ((bf16[16,320,128]{2,1,0:T(8,128)(2,1)}), bf16[16,320,128]{2,1,0:T(8,128)(2,1)S(1)}, u32[]{:S(2)}, u32[]{:S(2)}) async-start(bf16[16,320,128]{2,1,0:T(8,128)(2,1)} %pad_maximum_fusion), calls=%async_computation.3 | async-start | bytes 2621440 | tf_op jit(solution)/shard_map/all_to_all | solution.py:624
  273.2 1.0 copy-start
  274.2 3.8 %collective-permute-start.8 = (bf16[64,4096]{1,0:T(8,128)(2,1)S(1)}, bf16[64,4096]{1,0:T(8,128)(2,1)S(1)}, u32[]{:S(2)}, u32[]{:S(2)}) collective-permute-start(bf16[64,4096]{1,0:T(8,128)(2,1)S(1)} %get-tuple-element.49), channel_id=1, source_target_pairs={{0,1},{1,0},{2,3},{3,2},{4,5},{5,4},{6,7},{7,6},{8,9},{9,8},{10,11... | collective-permute-start | bytes 1572872 | tf_op jit(solution)/shard_map/ppermute | solution.py:630
  278.0 0.8 copy-start.9
  282.9 7.9 %collective-permute-start.12 = (f32[72,128]{1,0:T(8,128)}, f32[72,128]{1,0:T(8,128)S(1)}, u32[]{:S(2)}, u32[]{:S(2)}) collective-permute-start(f32[72,128]{1,0:T(8,128)} %get-tuple-element.51), channel_id=1, source_target_pairs={{128,0},{160,32},{192,64},{224,96},{256,128},{288,160},{320,192},{... | collective-permute-start | bytes 110600 | tf_op jit(solution)/shard_map/ppermute | solution.py:618
  284.2 7.0 %collective-permute-start.11 = (f32[72,128]{1,0:T(8,128)}, f32[72,128]{1,0:T(8,128)S(1)}, u32[]{:S(2)}, u32[]{:S(2)}) collective-permute-start(f32[72,128]{1,0:T(8,128)} %get-tuple-element.51), channel_id=1, source_target_pairs={{96,0},{128,32},{160,64},{192,96},{224,128},{256,160},{288,192},{3... | collective-permute-start | bytes 110600 | tf_op jit(solution)/shard_map/ppermute | solution.py:618
  286.7 8.5 %collective-permute-start.10 = (f32[72,128]{1,0:T(8,128)}, f32[72,128]{1,0:T(8,128)S(1)}, u32[]{:S(2)}, u32[]{:S(2)}) collective-permute-start(f32[72,128]{1,0:T(8,128)} %get-tuple-element.51), channel_id=1, source_target_pairs={{64,0},{96,32},{128,64},{160,96},{192,128},{224,160},{256,192},{28... | collective-permute-start | bytes 110600 | tf_op jit(solution)/shard_map/ppermute | solution.py:618
  288.8 8.2 %collective-permute-start.9 = (f32[72,128]{1,0:T(8,128)}, f32[72,128]{1,0:T(8,128)S(1)}, u32[]{:S(2)}, u32[]{:S(2)}) collective-permute-start(f32[72,128]{1,0:T(8,128)} %get-tuple-element.51), channel_id=1, source_target_pairs={{32,0},{64,32},{96,64},{128,96},{160,128},{192,160},{224,192},{256... | collective-permute-start | bytes 110600 | tf_op jit(solution)/shard_map/ppermute | solution.py:618
  290.8 6.2 %copy-start.10 = (f32[72,128]{1,0:T(8,128)}, f32[72,128]{1,0:T(8,128)S(1)}, u32[]{:S(2)}) copy-start(f32[72,128]{1,0:T(8,128)S(1)} %collective-permute-done.12.m4_ref) | copy-start | bytes 110596
  291.2 5.8 %copy-start.11 = (f32[72,128]{1,0:T(8,128)}, f32[72,128]{1,0:T(8,128)S(1)}, u32[]{:S(2)}) copy-start(f32[72,128]{1,0:T(8,128)S(1)} %collective-permute-done.11.m3_ref) | copy-start | bytes 110596
  295.2 1.8 copy-start.12
  297.0 0.6 copy-start.13
  297.6 35.5 %copy-start.4 = (f32[2,128]{1,0:T(2,128)S(1)}, f32[2,128]{1,0:T(2,128)}, u32[]{:S(2)}) copy-start(f32[2,128]{1,0:T(2,128)} %copy-done.3) | copy-start | bytes 3076
Sparse Core Ops, SparseCore 0:
  11.4 95.2 all-gather.1
